TPU v7x, 512 devices: a whole 4x4x16 slice. The times are simulated.
512 devices in a mesh: seq: 64 (over z, x), head: 8 (over y, core).
Axes of the slice: x: 4, y: 4, z: 16, core: 2. Of those that a mesh axis runs over, the one named last changes fastest.
Arguments:
- delta_query: bfloat16 [16384, 32, 128], P('seq', 'head'), may hold values from -40 to 40
- delta_key: bfloat16 [16384, 32, 128], P('seq', 'head'), may hold values from -40 to 40
- delta_value: bfloat16 [16384, 32, 256], P('seq', 'head'), may hold values from -16 to 16
- delta_gate: float32 [16384, 32], P('seq', 'head'), may hold values from -1 to 0
- delta_beta: float32 [16384, 32], P('seq', 'head'), may hold values from 0 to 1
- delta_count: int32 [64], P('seq'), may hold values from 32 to 256, as said below
- delta_gain: float32 [32, 256], P('head'), may hold values from 0.1 to 1.9
- attn_query: bfloat16 [16384, 32, 128], P('seq', 'head'), may hold values from -6 to 6
- attn_key: bfloat16 [16384, 32, 128], P('seq', 'head'), may hold values from -6 to 6
- attn_value: bfloat16 [16384, 32, 256], P('seq', 'head'), may hold values from -6 to 6
- attn_position: int32 [16384], P('seq'), may hold values from 0 to 32767, as said below
- attn_count: int32 [64], P('seq'), may hold values from 32 to 256, as said below
Outputs:
- delta_out: bfloat16 [16384, 32, 256], P('seq', 'head')
- attn_out: bfloat16 [16384, 32, 256], P('seq', 'head')
Inputs may be any that keep to these rules, and one draw needn't show every extreme that they name: `delta_count`: kept rows of each block of 512 token positions; some block holds exactly 256. `attn_count`: kept rows of each block of 512 token positions; some block holds exactly 256. `attn_position`: slot s holds a position of block b = s // 256, from b * 512 to (b + 1) * 512 - 1; the first attn_count[b] slots of a block hold distinct positions in rising order, its other slots arbitrary positions of the block.
All inputs are finite; a program needn't handle non-finite values.
Results may differ from a plain program's by a relative error of at most 0.0044.
Values may be sent and summed in bfloat16 or wider, within the bound.
No kernel may reach another device: no remote copies, remote signals or barrier semaphores. Data moves between devices by JAX's collectives and lax.ppermute only.
A program may use at most 128 MiB of HBM per device.

v0:
```python
import jax
import jax.numpy as jnp
from jax import lax
from jax.sharding import PartitionSpec as P

H = 32
VD = 256
WINDOW = 2048
GROUP = 64
TOK_DEV = 512


HIGHEST = lax.Precision.HIGHEST


def prefix(part, axis, combine, identity):
    place = lax.axis_index(axis)
    gathered = jax.tree.map(lambda a: lax.all_gather(a, axis), part)
    state = jax.tree.map(lambda a, e: jnp.zeros_like(a) + jnp.asarray(e, a.dtype), part, identity)

    def one(lap, state):
        return combine(
            state, jax.tree.map(lambda a: lax.dynamic_index_in_dim(a, lap, 0, False), gathered)
        )

    return lax.fori_loop(0, place, one, state)


def from_behind(block, axis, distance):
    devices = range(lax.axis_size(axis))
    route = [(i - distance, i) for i in devices if i - distance in devices]
    return lax.ppermute(block, axis, route)


def inverse_norms(block_rows):
    wide_rows = block_rows.astype(jnp.float32)
    return lax.rsqrt(jnp.sum(wide_rows * wide_rows, axis=-1) + 1e-06)


def group_terms(query_raw, key_raw, value_rows, gate_rows, beta_rows):
    group_len = gate_rows.shape[0]
    row_index = jnp.arange(group_len)[:, None]
    col_index = jnp.arange(group_len)[None, :]
    query_scale = inverse_norms(query_raw)
    key_scale = inverse_norms(key_raw)
    query_rows = query_raw.astype(jnp.float32) * query_scale[:, None]
    key_rows = key_raw.astype(jnp.float32) * key_scale[:, None]
    log_decay = jnp.cumsum(gate_rows)
    decay_pair = jnp.where(
        col_index <= row_index,
        jnp.exp(jnp.minimum(log_decay[:, None] - log_decay[None, :], 0.0)),
        0.0,
    )
    key_gram = (
        key_scale[:, None]
        * jnp.dot(key_raw, key_raw.T, preferred_element_type=jnp.float32)
        * key_scale[None, :]
    )
    system = jnp.eye(group_len, dtype=jnp.float32) + jnp.where(
        col_index < row_index, beta_rows[:, None] * decay_pair * key_gram, 0.0
    )
    decay_to = jnp.exp(log_decay)
    right_side = jnp.concatenate(
        [beta_rows[:, None] * value_rows, (beta_rows * decay_to)[:, None] * key_rows], axis=1
    )
    solved = lax.linalg.triangular_solve(system, right_side, left_side=True, lower=True)
    value_width = value_rows.shape[1]
    new_value = solved[:, :value_width]
    new_key = solved[:, value_width:]
    query_key = (
        query_scale[:, None]
        * jnp.dot(query_raw, key_raw.T, preferred_element_type=jnp.float32)
        * key_scale[None, :]
    )
    mixing = decay_pair * query_key
    decay_tail = jnp.exp(log_decay[-1] - log_decay)[:, None]
    local_out = jnp.dot(mixing, new_value, precision=HIGHEST)
    carry_out = decay_to[:, None] * query_rows - jnp.dot(mixing, new_key, precision=HIGHEST)
    transition = decay_to[-1] * jnp.eye(key_rows.shape[1], dtype=jnp.float32) - jnp.dot(
        key_rows.T, decay_tail * new_key, precision=HIGHEST
    )
    offset = jnp.dot(key_rows.T, decay_tail * new_value, precision=HIGHEST)
    return (local_out, carry_out, transition, offset)


def batched(left_side, right_side):
    return jnp.einsum("hij,hjk->hik", left_side, right_side, precision=HIGHEST)


def compose(earlier, following):
    return (batched(following[0], earlier[0]), batched(following[0], earlier[1]) + following[1])


def chain_entry(product, offset_sum, identity, zero_state):
    composed = prefix((product, offset_sum), "seq", compose, (identity, zero_state))
    return composed[1]


def delta_mixer(query_rows, key_rows, value_rows, gate_rows, beta_rows, count_here, gain_rows):
    capacity, head_count = gate_rows.shape
    key_width = key_rows.shape[2]
    value_width = value_rows.shape[2]
    live_rows = jnp.arange(capacity) < count_here[0]
    gate_live = jnp.where(live_rows[:, None], gate_rows, 0.0)
    beta_live = jnp.where(live_rows[:, None], beta_rows, 0.0)
    live_blocks = (count_here[0] + GROUP - 1) // GROUP
    identity = jnp.broadcast_to(
        jnp.eye(key_width, dtype=jnp.float32), (head_count, key_width, key_width)
    )
    zero_state = jnp.zeros((head_count, key_width, value_width), jnp.float32)

    def terms_at(block_index):
        start_row = block_index * GROUP

        def take_rows(array):
            return lax.dynamic_slice_in_dim(array, start_row, GROUP, 0)

        return jax.vmap(group_terms, in_axes=(1, 1, 1, 1, 1))(
            take_rows(query_rows),
            take_rows(key_rows),
            take_rows(value_rows).astype(jnp.float32),
            take_rows(gate_live),
            take_rows(beta_live),
        )

    def summarize(block_index, carry):
        product, offset_sum = carry
        local_out, carry_out, transition, offset = terms_at(block_index)
        return (batched(transition, product), batched(transition, offset_sum) + offset)

    product, offset_sum = lax.fori_loop(0, live_blocks, summarize, (identity, zero_state))
    entering = chain_entry(product, offset_sum, identity, zero_state)

    def replay(block_index, carry):
        state_now, out_buf = carry
        local_out, carry_out, transition, offset = terms_at(block_index)
        result = local_out + batched(carry_out, state_now)
        out_buf = lax.dynamic_update_slice_in_dim(
            out_buf, jnp.swapaxes(result, 0, 1), block_index * GROUP, 0
        )
        return (batched(transition, state_now) + offset, out_buf)

    state_end, mixed_rows = lax.fori_loop(
        0,
        live_blocks,
        replay,
        (entering, jnp.zeros((capacity, head_count, value_width), jnp.float32)),
    )
    mixed_rows = jnp.where(live_rows[:, None, None], mixed_rows, 0.0)
    square_sum = lax.psum(jnp.sum(mixed_rows * mixed_rows, axis=(1, 2)), "head")
    norm_factor = lax.rsqrt(square_sum / (H * VD) + 1e-06)
    return (mixed_rows * norm_factor[:, None, None] * gain_rows).astype(jnp.bfloat16)


def window_mixer(query_rows, key_rows, value_rows, position_rows, count_here):
    capacity = position_rows.shape[0]
    key_marks = jnp.where(jnp.arange(capacity) < count_here[0], position_rows + 1, 0)
    reach_blocks = max(1, WINDOW // TOK_DEV)
    key_parts = [key_rows]
    value_parts = [value_rows]
    mark_parts = [key_marks]
    moving = (key_rows, value_rows, key_marks)
    for distance in range(reach_blocks):
        moving = from_behind((moving[0], moving[1], moving[2]), "seq", 1)
        key_parts.append(moving[0])
        value_parts.append(moving[1])
        mark_parts.append(moving[2])
    all_keys = jnp.concatenate(key_parts, axis=0)
    all_values = jnp.concatenate(value_parts, axis=0)
    all_marks = jnp.concatenate(mark_parts, axis=0)
    score_scale = query_rows.shape[2] ** (-0.5)
    scores = (
        jnp.einsum("qhd,khd->hqk", query_rows, all_keys, preferred_element_type=jnp.float32)
        * score_scale
    )
    permitted_pairs = (
        (all_marks[None, :] > 0)
        & (all_marks[None, :] <= key_marks[:, None])
        & (all_marks[None, :] > key_marks[:, None] - WINDOW)
    )
    scores = jnp.where(permitted_pairs[None], scores, -1e30)
    top_score = jnp.max(scores, axis=2, keepdims=True)
    weights = jnp.exp(scores - top_score)
    totals = jnp.sum(weights, axis=2)
    rounded = weights.astype(jnp.bfloat16)
    mixed_rows = jnp.einsum("hqk,khv->qhv", rounded, all_values, preferred_element_type=jnp.float32)
    mixed_rows = mixed_rows / jnp.transpose(totals)[:, :, None]
    return jnp.where((key_marks > 0)[:, None, None], mixed_rows, 0.0).astype(jnp.bfloat16)


def shards(
    delta_query,
    delta_key,
    delta_value,
    delta_gate,
    delta_beta,
    delta_count,
    delta_gain,
    attn_query,
    attn_key,
    attn_value,
    attn_position,
    attn_count,
):
    delta_out = delta_mixer(
        delta_query, delta_key, delta_value, delta_gate, delta_beta, delta_count, delta_gain
    )
    attn_out = window_mixer(attn_query, attn_key, attn_value, attn_position, attn_count)
    return (delta_out, attn_out)


def solution(mesh):
    return jax.shard_map(
        shards,
        mesh=mesh,
        in_specs=(
            P("seq", "head", None),
            P("seq", "head", None),
            P("seq", "head", None),
            P("seq", "head"),
            P("seq", "head"),
            P("seq"),
            P("head", None),
            P("seq", "head", None),
            P("seq", "head", None),
            P("seq", "head", None),
            P("seq"),
            P("seq"),
        ),
        out_specs=(P("seq", "head", None), P("seq", "head", None)),
        check_vma=False,
    )
```

profile of v0, /device:TPU:486, one launch (start us, length us, event | category | flops | bytes accessed | tf_op | source)
XLA Modules:
  0.0 827.6 jit_solution(5562641110810628931)
XLA Ops:
  11.9 71.5 %while.36 = (s32[]{:T(128)}, f32[4,128,128]{2,1,0:T(8,128)S(1)}, f32[4,128,256]{2,1,0:T(8,128)S(1)}, s32[]{:T(128)}, f32[256,4]{1,0:T(8,128)S(1)}, /*index=5*/bf...) while((s32[]{:T(128)}, f32[4,128,128]{2,1,0:T(8,128)S(1)}, ...), condition=%wide.region_3.5_spmd, body=%wide.region_0.4_spmd.sunk | while | flops 533827840 | bytes 6421283 | solution.py:131
  12.9 19.7 %custom-call.13 = f32[4,1,64,64]{2,3,1,0:T(8,128)S(1)} custom-call(f32[4,1,64,64]{3,2,1,0:T(8,128)S(1)} %fusion.176), custom_call_target="InvertDiagBlocksLowerTriangular" | custom-call | tf_op jit(solution)/shard_map/while/body/vmap()/triangular_solve/custom-call.1 | solution.py:66
  36.8 19.7 %custom-call.13 = f32[4,1,64,64]{2,3,1,0:T(8,128)S(1)} custom-call(f32[4,1,64,64]{3,2,1,0:T(8,128)S(1)} %fusion.176), custom_call_target="InvertDiagBlocksLowerTriangular" | custom-call | tf_op jit(solution)/shard_map/while/body/vmap()/triangular_solve/custom-call.1 | solution.py:66
  60.6 19.7 %custom-call.13 = f32[4,1,64,64]{2,3,1,0:T(8,128)S(1)} custom-call(f32[4,1,64,64]{3,2,1,0:T(8,128)S(1)} %fusion.176), custom_call_target="InvertDiagBlocksLowerTriangular" | custom-call | tf_op jit(solution)/shard_map/while/body/vmap()/triangular_solve/custom-call.1 | solution.py:66
  88.5 1.7 fusion.100
  92.4 9.6 %collective-permute-done.4 = s32[256]{0:T(256)S(1)} collective-permute-done((s32[256]{0:T(256)S(1)}, s32[256]{0:T(256)S(1)}, u32[]{:S(2)}, u32[]{:S(2)}) %collective-permute-start.4) | collective-permute-done | bytes 1056 | tf_op jit(solution)/shard_map/ppermute | solution.py:32
  103.3 4.1 collective-permute-done.5
  108.8 4.1 collective-permute-done.6
  115.6 2.9 collective-permute-done.7
  119.8 7.2 collective-permute-done.9
  130.9 11.4 %collective-permute-done.10 = bf16[256,4,128]{2,0,1:T(8,128)(2,1)S(1)} collective-permute-done((bf16[256,4,128]{2,0,1:T(8,128)(2,1)S(1)}, bf16[256,4,128]{2,0,1:T(8,128)(2,1)S(1)}, u32[]{:S(2)}, u32[]{:S(2)}) %collective-permute-start.10) | collective-permute-done | bytes 262176 | tf_op jit(solution)/shard_map/ppermute | solution.py:32
  147.3 7.9 collective-permute-done.11
  156.0 2.3 fusion.83
  158.3 4.9 collective-permute-done.2
  166.3 11.3 %collective-permute-done.3 = bf16[256,4,256]{0,2,1:T(8,128)(2,1)S(1)} collective-permute-done((bf16[256,4,256]{0,2,1:T(8,128)(2,1)S(1)}, bf16[256,4,256]{0,2,1:T(8,128)(2,1)S(1)}, u32[]{:S(2)}, u32[]{:S(2)}) %collective-permute-start.3) | collective-permute-done | bytes 524320 | tf_op jit(solution)/shard_map/ppermute | solution.py:32
  180.2 131.4 %all-gather.5.cloned.1.call-done = f32[256,128,128]{2,1,0:T(8,128)} async-done(((f32[4,128,128]{2,1,0:T(8,128)}), f32[256,128,128]{2,1,0:T(8,128)}) %all-gather.5.cloned.1.call-update) | async-done | bytes 16777232 | tf_op jit(solution)/shard_map/all_gather | solution.py:18
  311.6 296.9 %all-gather.7.cloned.1.call-done = f32[256,128,256]{2,1,0:T(8,128)} async-done(((f32[4,128,256]{2,1,0:T(8,128)}), f32[256,128,256]{2,1,0:T(8,128)}) %all-gather.7.cloned.1.call-update) | async-done | bytes 33554448 | tf_op jit(solution)/shard_map/all_gather | solution.py:18
  608.5 112.6 %while.37 = (s32[]{:T(128)}, f32[4,128,256]{2,1,0:T(8,128)S(1)}, s32[]{:T(128)}, f32[64,4,128,128]{3,2,1,0:T(8,128)}, f32[64,4,128,256]{3,2,1,0:T(8,128)}, /*index=5*/s32[]{:T(128)}, s32[]{:T(128)}, s32[]{:T(128)}) while((s32[]{:T(128)}, f32[4,128,256]{2,1,0:T(8,128)S(1)}, s32[]{:T(128)}, f32[64,4,128,128]{3,2,1,0:T(8,128)}, ...), condition=%wide.region_5.7_spmd, body=%wide.region_4.6_spmd.sunk | while | flops 201457664 | bytes 2884735 | solution.py:26
  608.6 1.7 convolution_add_fusion.8
  610.4 1.7 convolution_add_fusion.8
  612.2 1.7 convolution_add_fusion.8
  614.0 1.7 convolution_add_fusion.8
  626.5 1.7 convolution_add_fusion.8
  628.3 1.7 convolution_add_fusion.8
  635.4 1.7 convolution_add_fusion.8
  640.8 1.7 convolution_add_fusion.8
  642.6 1.7 convolution_add_fusion.8
  647.9 1.7 convolution_add_fusion.8
  649.7 1.7 convolution_add_fusion.8
  655.1 1.7 convolution_add_fusion.8
  662.2 1.7 convolution_add_fusion.8
  664.0 1.7 convolution_add_fusion.8
  676.5 1.7 convolution_add_fusion.8
  678.3 1.7 convolution_add_fusion.8
  685.5 1.7 convolution_add_fusion.8
  689.1 1.7 convolution_add_fusion.8
  690.8 1.7 convolution_add_fusion.8
  698.0 1.7 convolution_add_fusion.8
  703.4 1.7 convolution_add_fusion.8
  705.1 1.7 convolution_add_fusion.8
  710.5 1.7 convolution_add_fusion.8
  712.3 1.7 convolution_add_fusion.8
  717.7 1.7 convolution_add_fusion.8
  721.3 83.5 %while.38 = (s32[]{:T(128)}, f32[4,128,256]{2,1,0:T(8,128)S(1)}, f32[256,4,256]{2,0,1:T(8,128)S(1)}, s32[]{:T(128)}, f32[256,4]{1,0:T(8,128)}, /*index=5*/bf16[2...) while((s32[]{:T(128)}, f32[4,128,256]{2,1,0:T(8,128)S(1)}, ...), condition=%wide.region_10.12_spmd, body=%wide.region_6.11_spmd.sunk | while | flops 613912832 | bytes 7822135 | solution.py:143
  725.0 20.4 %custom-call.14 = f32[4,1,64,64]{2,3,1,0:T(8,128)S(1)} custom-call(f32[4,1,64,64]{3,2,1,0:T(8,128)} %fusion.205), custom_call_target="InvertDiagBlocksLowerTriangular" | custom-call | tf_op jit(solution)/shard_map/while/body/vmap()/triangular_solve/custom-call.1 | solution.py:66
  752.8 20.4 %custom-call.14 = f32[4,1,64,64]{2,3,1,0:T(8,128)S(1)} custom-call(f32[4,1,64,64]{3,2,1,0:T(8,128)} %fusion.205), custom_call_target="InvertDiagBlocksLowerTriangular" | custom-call | tf_op jit(solution)/shard_map/while/body/vmap()/triangular_solve/custom-call.1 | solution.py:66
  780.6 20.4 %custom-call.14 = f32[4,1,64,64]{2,3,1,0:T(8,128)S(1)} custom-call(f32[4,1,64,64]{3,2,1,0:T(8,128)} %fusion.205), custom_call_target="InvertDiagBlocksLowerTriangular" | custom-call | tf_op jit(solution)/shard_map/while/body/vmap()/triangular_solve/custom-call.1 | solution.py:66
  805.3 14.2 %psum.7 = f32[256]{0:T(256)S(1)} all-reduce(f32[256]{0:T(256)S(1)} %multiply_reduce_fusion), channel_id=1, replica_groups=mesh['seq'=64,'head'=8] {'head'}, use_global_device_ids=true, to_apply=%region_12.14 | all-reduce | flops 256 | bytes 2048 | tf_op jit(solution)/shard_map/psum | solution.py:150
  (326 shorter events, 135.3 us)
Async XLA Ops:
  7.2 148.8 %copy-start = (bf16[256,4,128]{2,1,0:T(4,128)(2,1)S(1)}, bf16[256,4,128]{2,1,0:T(4,128)(2,1)}, u32[]{:S(2)}) copy-start(bf16[256,4,128]{2,1,0:T(4,128)(2,1)} %param.27) | copy-start | bytes 786436
  7.2 304.4 %all-gather.5.cloned.1.call-start = ((), (), s32[]{:S(2)}) async-start(), calls=%async_computation | async-start | bytes 17039360 | tf_op jit(solution)/shard_map/all_gather | solution.py:18
  11.9 73.0 %copy-start.5 = (bf16[256,4,256]{2,1,0:T(4,128)(2,1)S(1)}, bf16[256,4,256]{2,1,0:T(4,128)(2,1)}, u32[]{:S(2)}) copy-start(bf16[256,4,256]{2,1,0:T(4,128)(2,1)} %param.29) | copy-start | bytes 1572868
  11.9 75.3 %copy-start.8 = (s32[256]{0:T(256)S(1)}, s32[256]{0:T(256)}, u32[]{:S(2)}) copy-start(s32[256]{0:T(256)} %param.30) | copy-start | bytes 3076
  83.4 0.7 copy-start.3
  83.4 0.9 copy-start.2
  83.5 47.5 %copy-start.4 = (f32[256,4]{1,0:T(8,128)}, f32[256,4]{1,0:T(8,128)S(1)}, u32[]{:S(2)}) copy-start(f32[256,4]{1,0:T(8,128)S(1)} %get-tuple-element.561) | copy-start | bytes 12292
  84.2 524.3 %all-gather.7.cloned.1.call-start = ((), (), s32[]{:S(2)}) async-start(), calls=%async_computation.1 | async-start | bytes 34078720 | tf_op jit(solution)/shard_map/all_gather | solution.py:18
  85.3 33.2 %collective-permute-start = (bf16[256,4,256]{0,2,1:T(8,128)(2,1)S(1)}, bf16[256,4,256]{0,2,1:T(8,128)(2,1)S(1)}, u32[]{:S(2)}, u32[]{:S(2)}) collective-permute-start(bf16[256,4,256]{0,2,1:T(8,128)(2,1)S(1)} %copy.102), channel_id=1, source_target_pairs={{0,8},{8,16},{16,24},{24,32},{32,40},{40,48},{48,56},{56,64},{64,7... | collective-permute-start | bytes 1572872 | tf_op jit(solution)/shard_map/ppermute | solution.py:32
  87.2 14.8 %collective-permute-start.4 = (s32[256]{0:T(256)S(1)}, s32[256]{0:T(256)S(1)}, u32[]{:S(2)}, u32[]{:S(2)}) collective-permute-start(s32[256]{0:T(256)S(1)} %get-tuple-element.245), channel_id=1, source_target_pairs={{0,8},{8,16},{16,24},{24,32},{32,40},{40,48},{48,56},{56,64},{64,7... | collective-permute-start | bytes 3080 | tf_op jit(solution)/shard_map/ppermute | solution.py:32
  90.3 24.0 %collective-permute-start.8 = (bf16[256,4,128]{2,0,1:T(8,128)(2,1)S(1)}, bf16[256,4,128]{2,0,1:T(8,128)(2,1)S(1)}, u32[]{:S(2)}, u32[]{:S(2)}) collective-permute-start(bf16[256,4,128]{2,0,1:T(8,128)(2,1)S(1)} %get-tuple-element.264), channel_id=1, source_target_pairs={{0,8},{8,16},{16,24},{24,32},{32,40},{40,48},{48,56},{56,64},{64,7... | collective-permute-start | bytes 786440 | tf_op jit(solution)/shard_map/ppermute | solution.py:32
  102.0 5.5 collective-permute-start.5
  107.5 5.5 collective-permute-start.6
  112.9 5.5 collective-permute-start.7
  114.3 12.7 %collective-permute-start.9 = (bf16[256,4,128]{2,0,1:T(8,128)(2,1)S(1)}, bf16[256,4,128]{2,0,1:T(8,128)(2,1)S(1)}, u32[]{:S(2)}, u32[]{:S(2)}) collective-permute-start(bf16[256,4,128]{2,0,1:T(8,128)(2,1)S(1)} %collective-permute-done.8), channel_id=1, source_target_pairs={{0,8},{8,16},{16,24},{24,32},{32,40},{40,48},{48,56},{56,64},{64,7... | collective-permute-start | bytes 786440 | tf_op jit(solution)/shard_map/ppermute | solution.py:32
  118.5 26.7 %collective-permute-start.1 = (bf16[256,4,256]{0,2,1:T(8,128)(2,1)S(1)}, bf16[256,4,256]{0,2,1:T(8,128)(2,1)S(1)}, u32[]{:S(2)}, u32[]{:S(2)}) collective-permute-start(bf16[256,4,256]{0,2,1:T(8,128)(2,1)S(1)} %collective-permute-done), channel_id=1, source_target_pairs={{0,8},{8,16},{16,24},{24,32},{32,40},{40,48},{48,56},{56,64},{64,7... | collective-permute-start | bytes 1572872 | tf_op jit(solution)/shard_map/ppermute | solution.py:32
  126.9 15.4 %collective-permute-start.10 = (bf16[256,4,128]{2,0,1:T(8,128)(2,1)S(1)}, bf16[256,4,128]{2,0,1:T(8,128)(2,1)S(1)}, u32[]{:S(2)}, u32[]{:S(2)}) collective-permute-start(bf16[256,4,128]{2,0,1:T(8,128)(2,1)S(1)} %collective-permute-done.9), channel_id=1, source_target_pairs={{0,8},{8,16},{16,24},{24,32},{32,40},{40,48},{48,56},{56,64},{64,7... | collective-permute-start | bytes 786440 | tf_op jit(solution)/shard_map/ppermute | solution.py:32
  142.4 12.8 %collective-permute-start.11 = (bf16[256,4,128]{2,0,1:T(8,128)(2,1)S(1)}, bf16[256,4,128]{2,0,1:T(8,128)(2,1)S(1)}, u32[]{:S(2)}, u32[]{:S(2)}) collective-permute-start(bf16[256,4,128]{2,0,1:T(8,128)(2,1)S(1)} %collective-permute-done.10), channel_id=1, source_target_pairs={{0,8},{8,16},{16,24},{24,32},{32,40},{40,48},{48,56},{56,64},{64,7... | collective-permute-start | bytes 786440 | tf_op jit(solution)/shard_map/ppermute | solution.py:32
  145.1 18.1 %collective-permute-start.2 = (bf16[256,4,256]{0,2,1:T(8,128)(2,1)S(1)}, bf16[256,4,256]{0,2,1:T(8,128)(2,1)S(1)}, u32[]{:S(2)}, u32[]{:S(2)}) collective-permute-start(bf16[256,4,256]{0,2,1:T(8,128)(2,1)S(1)} %collective-permute-done.1), channel_id=1, source_target_pairs={{0,8},{8,16},{16,24},{24,32},{32,40},{40,48},{48,56},{56,64},{64,7... | collective-permute-start | bytes 1572872 | tf_op jit(solution)/shard_map/ppermute | solution.py:32
  163.2 14.4 %collective-permute-start.3 = (bf16[256,4,256]{0,2,1:T(8,128)(2,1)S(1)}, bf16[256,4,256]{0,2,1:T(8,128)(2,1)S(1)}, u32[]{:S(2)}, u32[]{:S(2)}) collective-permute-start(bf16[256,4,256]{0,2,1:T(8,128)(2,1)S(1)} %collective-permute-done.2), channel_id=1, source_target_pairs={{0,8},{8,16},{16,24},{24,32},{32,40},{40,48},{48,56},{56,64},{64,7... | collective-permute-start | bytes 1572872 | tf_op jit(solution)/shard_map/ppermute | solution.py:32
  164.5 1.7 copy-start.6
  804.8 14.7 %copy-start.7 = (f32[4,256]{1,0:T(4,128)S(1)}, f32[4,256]{1,0:T(4,128)}, u32[]{:S(2)}) copy-start(f32[4,256]{1,0:T(4,128)} %param.26) | copy-start | bytes 12292
  804.8 16.0 %copy-start.1 = (bf16[256,4,128]{2,1,0:T(4,128)(2,1)S(1)}, bf16[256,4,128]{2,1,0:T(4,128)(2,1)}, u32[]{:S(2)}) copy-start(bf16[256,4,128]{2,1,0:T(4,128)(2,1)} %param.27) | copy-start | bytes 786436
Sparse Core Ops, SparseCore 0:
  84.3 227.2 all-gather.4
  315.1 293.3 all-gather.6
where the time goes:
time: 843 us; the launch traced here: 828 us
  waiting for transfers between devices  492 us (58%)
  matrix products  135 us (16%)
  other arithmetic  127 us (15%)
  local copies, waits for them, and re-layouts  24.3 us (3%)
  between operations  15.8 us (2%)
  starting transfers between devices  15.5 us (2%)
  blocking collectives  14.2 us (2%)
    all_gather x2, waiting for transfers between devices, prefix(): gathered = jax.tree.map(lambda a: lax.all_gather(a, axis), part)  428 us
    another operation x12, other arithmetic, group_terms(): lax.linalg.triangular_solve(system, right_side, left_side=True, lower=True)  120 us
    dot_general x75, matrix products, batched(): return jnp.einsum('hij,hjk->hik', left_side, right_side, precision=HIGHEST)  114 us
    ppermute x12, waiting for transfers between devices, from_behind(): return lax.ppermute(block, axis, route)  63.5 us
  transfers between devices with their start and end apart: 14, of which 11 were waited for; matrix products, arithmetic and copies ran while one was open for 2% of the time, Pallas kernels for 0%

commit v1 on v0

v1 whole, which is shorter than its diff:
```python
import jax
import jax.numpy as jnp
from jax import lax
from jax.experimental import pallas as pl
from jax.experimental.pallas import tpu as pltpu
from jax.sharding import Mesh, PartitionSpec as P

ROWS = 256
KD = 128
VD = 256
HEADS = 4
HIDDEN = 8192
WINDOW = 2048
REACH = 4
PART = VD // 4
MARK_ROWS = 16
VMEM_BYTES = 48 * 2**20

SEQ = ("zh", "zl", "x")
f32 = jnp.float32
bf16 = jnp.bfloat16


def halves(x):
    high = x.astype(bf16)
    return high, (x - high.astype(f32)).astype(bf16)


def dot(a, b, dims=((1,), (0,))):
    return lax.dot_general(a, b, (dims, ((), ())), preferred_element_type=f32)


def dot3(a, b):
    ah, al = halves(a)
    bh, bl = halves(b)
    return dot(ah, bh) + (dot(ah, bl) + dot(al, bh))


def dot2(a, b):
    ah, al = halves(a)
    return dot(ah, b) + dot(al, b)


def call(body, out_shape, scalars=0, inputs=1, scratch=()):
    whole = pl.BlockSpec(memory_space=pltpu.VMEM)
    small = pl.BlockSpec(memory_space=pltpu.SMEM)
    return pl.pallas_call(
        body,
        in_specs=[small] * scalars + [whole] * inputs,
        out_specs=jax.tree.map(lambda _: whole, out_shape),
        out_shape=out_shape,
        scratch_shapes=list(scratch),
        compiler_params=pltpu.CompilerParams(vmem_limit_bytes=VMEM_BYTES),
    )


def block_terms(
    count_ref, q_ref, k_ref, v_ref, gate_ref, beta_ref, map_ref, carry_ref, local_ref, x_ref, a_ref
):
    count = count_ref[0]
    row = lax.broadcasted_iota(jnp.int32, (ROWS, ROWS), 0)
    col = lax.broadcasted_iota(jnp.int32, (ROWS, ROWS), 1)
    lane = lax.broadcasted_iota(jnp.int32, (1, ROWS), 1)
    eye = row == col
    kept = []
    for h in range(HEADS):
        k = k_ref[h]
        gate = jnp.where(lane < count, gate_ref[h : h + 1, :], 0.0)
        beta = jnp.where(lane < count, beta_ref[h : h + 1, :], 0.0)
        log_col = jnp.sum(jnp.where(col <= row, gate, 0.0), axis=1, keepdims=True)
        log_row = jnp.sum(jnp.where(eye, log_col, 0.0), axis=0, keepdims=True)
        beta_col = jnp.sum(jnp.where(eye, beta, 0.0), axis=1, keepdims=True)
        gram = dot(k, k, ((1,), (1,)))
        squares = jnp.where(eye, gram, 0.0)
        k_col = lax.rsqrt(jnp.sum(squares, axis=1, keepdims=True) + 1e-6)
        k_row = lax.rsqrt(jnp.sum(squares, axis=0, keepdims=True) + 1e-6)
        decay = jnp.where(col <= row, jnp.exp(jnp.minimum(log_col - log_row, 0.0)), 0.0)
        a = jnp.where(col < row, (beta_col * k_col) * decay * (gram * k_row), 0.0)
        a_ref[h] = a
        x_ref[h] = jnp.where(eye, 1.0, jnp.where((row >> 1) == (col >> 1), -a, 0.0))
        q = q_ref[h]
        wide = q.astype(f32)
        q_col = lax.rsqrt(jnp.sum(wide * wide, axis=1, keepdims=True) + 1e-6)
        local_ref[h] = (q_col * decay) * (dot(q, k, ((1,), (1,))) * k_row)
        kept.append((log_col, log_row, beta, k_col, k_row, q_col))
    step = 1
    while (2 << step) <= ROWS:
        m = 1 << step
        for h in range(HEADS):
            x = x_ref[h]
            if m < 64:
                below = ((row >> (step + 1)) == (col >> (step + 1))) & ((row >> step) != (col >> step))
                x_ref[h] = x - dot3(dot3(x, jnp.where(below, a_ref[h], 0.0)), x)
            else:
                for s in range(0, ROWS, 2 * m):
                    first = x[s : s + m, s : s + m]
                    second = x[s + m : s + 2 * m, s + m : s + 2 * m]
                    between = a_ref[h, s + m : s + 2 * m, s : s + m]
                    x_ref[h, s + m : s + 2 * m, s : s + m] = -dot3(second, dot3(between, first))
        step += 1
    row_k = lax.broadcasted_iota(jnp.int32, (KD, KD), 0)
    col_k = lax.broadcasted_iota(jnp.int32, (KD, KD), 1)
    for h in range(HEADS):
        log_col, log_row, beta, k_col, k_row, q_col = kept[h]
        k = k_ref[h]
        x = x_ref[h]
        new_value = dot2(x * beta, v_ref[h])
        new_key = dot2(x * (beta * jnp.exp(log_row) * k_row), k)
        new = jnp.concatenate([new_key, new_value], axis=1)
        last = log_col[ROWS - 1 : ROWS, :]
        high, low = halves((jnp.exp(last - log_col) * k_col) * new)
        update = dot(k, high, ((0,), (0,))) + dot(k, low, ((0,), (0,)))
        map_ref[h, :, :KD] = jnp.where(row_k == col_k, jnp.exp(last), 0.0) - update[:, :KD]
        map_ref[h, :, KD:] = update[:, KD:]
        mixed = dot3(local_ref[h], new)
        carry_ref[h] = (jnp.exp(log_col) * q_col) * q_ref[h].astype(f32) - mixed[:, :KD]
        local_ref[h] = mixed[:, KD:]


def compose_maps(maps_ref, before_ref, total_ref):
    state = maps_ref[0]
    for i in range(1, 4):
        before_ref[i - 1] = state
        later = maps_ref[i]
        state = dot3(later[:, :KD], state)
        width = state.shape[1]
        state = jnp.concatenate([state[:, :KD], state[:, KD:] + later[:, KD:]], axis=1)
    total_ref[...] = state


def step_state(map_ref, earlier_ref, out_ref):
    out_ref[...] = dot3(map_ref[:, :KD], earlier_ref[:, KD:]) + map_ref[:, KD:]


def group_states(place_ref, earlier_ref, one_ref, two_ref, before_ref, out_ref):
    place = place_ref[0]
    last = dot3(earlier_ref[:, :KD], two_ref[...]) + earlier_ref[:, KD:]
    state = jnp.where(
        place == 0,
        0.0,
        jnp.where(place == 1, earlier_ref[:, KD:], jnp.where(place == 2, one_ref[...], last)),
    )
    out_ref[0] = state
    for i in range(3):
        out_ref[i + 1] = dot3(before_ref[i, :, :KD], state) + before_ref[i, :, KD:]


def plane_states(parts_ref, before_ref, out_ref):
    state = jnp.concatenate([parts_ref[i] for i in range(4)], axis=1)
    out_ref[0] = state
    for i in range(3):
        out_ref[i + 1] = dot3(before_ref[i, :, :KD], state) + before_ref[i, :, KD:]


def raw_rows(carry_ref, local_ref, state_ref, raw_ref, square_ref):
    total = jnp.zeros((ROWS, VD), f32)
    for h in range(HEADS):
        raw = local_ref[h] + dot3(carry_ref[h], state_ref[h])
        raw_ref[h] = raw
        total = total + raw * raw
    column = jnp.sum(total, axis=1, keepdims=True)
    row = lax.broadcasted_iota(jnp.int32, (ROWS, ROWS), 0)
    col = lax.broadcasted_iota(jnp.int32, (ROWS, ROWS), 1)
    square_ref[...] = jnp.broadcast_to(
        jnp.sum(jnp.where(row == col, column, 0.0), axis=0, keepdims=True), square_ref.shape
    )


def attend(q_ref, own_ref, one_ref, two_ref, three_ref, four_ref, out_ref):
    row = lax.broadcasted_iota(jnp.int32, (ROWS, ROWS), 0)
    col = lax.broadcasted_iota(jnp.int32, (ROWS, ROWS), 1)
    blocks = (own_ref, one_ref, two_ref, three_ref, four_ref)

    def marks_of(ref):
        coded = ref[0, ROWS : ROWS + MARK_ROWS, :ROWS].astype(f32)
        return coded[0:1, :] * 256.0 + coded[1:2, :]

    own_marks = marks_of(own_ref)
    query_marks = jnp.sum(jnp.where(row == col, own_marks, 0.0), axis=1, keepdims=True)
    limits = []
    for ref in blocks[:REACH]:
        marks = marks_of(ref)
        limits.append(jnp.where(marks > 0.0, marks, 1e9))
    oldest = marks_of(blocks[REACH])
    oldest = jnp.where(oldest > 0.0, oldest, -1e9)
    for h in range(HEADS):
        q = q_ref[h]
        scores = []
        for d, ref in enumerate(blocks):
            score = dot(q, ref[h, :ROWS, :KD], ((1,), (1,))) * KD**-0.5
            if d < REACH:
                allowed = limits[d] <= query_marks
            else:
                allowed = oldest > query_marks - float(WINDOW)
            scores.append(jnp.where(allowed, score, -1e30))
        top = scores[0]
        for score in scores[1:]:
            top = jnp.maximum(top, score)
        top = jnp.max(top, axis=1, keepdims=True)
        weight_sum = jnp.zeros((ROWS, ROWS), f32)
        mixed = jnp.zeros((ROWS, VD), f32)
        for score, ref in zip(scores, blocks):
            weights = jnp.exp(score - top)
            weight_sum = weight_sum + weights
            mixed = mixed + dot(weights.astype(bf16), ref[h, :ROWS, KD:])
        mixed = mixed / jnp.sum(weight_sum, axis=1, keepdims=True)
        out_ref[h] = jnp.where(query_marks > 0.0, mixed, 0.0).astype(bf16)


def heads_first(block):
    return jnp.swapaxes(block, 0, 1)


def shape_of(*dims, kind=f32):
    return jax.ShapeDtypeStruct(dims, kind)


def window_blocks(key_rows, value_rows, position_rows, count_here):
    marks = jnp.where(jnp.arange(ROWS) < count_here[0], position_rows + 1, 0)
    coded = jnp.stack([marks // 256, marks % 256]).astype(bf16)
    coded = jnp.pad(coded, ((0, MARK_ROWS - 2), (0, KD + VD - ROWS)))
    packed = jnp.concatenate([heads_first(key_rows), heads_first(value_rows)], axis=2)
    coded = jnp.broadcast_to(coded[None], (HEADS,) + coded.shape)
    own = jnp.concatenate([packed, coded], axis=1)
    blocks = [own]
    for distance in range(1, REACH + 1):
        count = lax.axis_size(SEQ)
        route = [(i, i + distance) for i in range(count - distance)]
        blocks.append(lax.ppermute(own, SEQ, route))
    return blocks


def entering_states(maps):
    exchanged = lax.all_to_all(maps, "x", 0, 0, tiled=True)
    plane_before, plane_total = call(
        compose_maps, (shape_of(3, KD, KD + VD), shape_of(KD, KD + VD))
    )(exchanged)
    transition = jnp.broadcast_to(plane_total[None, :, :KD], (4, KD, KD))
    offset = jnp.swapaxes(plane_total[:, KD:].reshape(KD, 4, PART), 0, 1)
    gathered = lax.all_to_all(
        jnp.concatenate([transition, offset], axis=2), "zl", 0, 0, tiled=True
    )
    group_before, group_total = call(
        compose_maps, (shape_of(3, KD, KD + PART), shape_of(KD, KD + PART))
    )(gathered)
    earlier = lax.ppermute(group_total, "zh", [(0, 1), (1, 2), (2, 3)])
    pair = call(step_state, shape_of(KD, PART), inputs=2)(group_total, earlier)
    one = lax.ppermute(pair, "zh", [(1, 2)])
    two = lax.ppermute(pair, "zh", [(1, 3)])
    place = lax.axis_index("zh").astype(jnp.int32).reshape(1)
    planes = call(group_states, shape_of(4, KD, PART), scalars=1, inputs=4)(
        place, earlier, one, two, group_before
    )
    parts = lax.all_to_all(planes, "zl", 0, 0, tiled=True)
    states = call(plane_states, shape_of(4, KD, VD), inputs=2)(parts, plane_before)
    return lax.all_to_all(states, "x", 0, 0, tiled=True)


def shards(
    delta_query,
    delta_key,
    delta_value,
    delta_gate,
    delta_beta,
    delta_count,
    delta_gain,
    attn_query,
    attn_key,
    attn_value,
    attn_position,
    attn_count,
):
    blocks = window_blocks(attn_key, attn_value, attn_position, attn_count)
    maps, carry, local = call(
        block_terms,
        (shape_of(HEADS, KD, KD + VD), shape_of(HEADS, ROWS, KD), shape_of(HEADS, ROWS, VD)),
        scalars=1,
        inputs=5,
        scratch=[pltpu.VMEM((HEADS, ROWS, ROWS), f32)] * 2,
    )(
        delta_count,
        heads_first(delta_query),
        heads_first(delta_key),
        heads_first(delta_value),
        delta_gate.T,
        delta_beta.T,
    )
    states = entering_states(maps)
    attn_heads = call(attend, shape_of(HEADS, ROWS, VD, kind=bf16), inputs=6)(
        heads_first(attn_query), *blocks
    )
    raw, squares = call(
        raw_rows, (shape_of(HEADS, ROWS, VD), shape_of(8, ROWS)), inputs=3
    )(carry, local, states)
    square_sum = jnp.sum(lax.all_gather(squares[0], "head"), axis=0)
    live = jnp.arange(ROWS) < delta_count[0]
    factor = jnp.where(live, lax.rsqrt(square_sum / HIDDEN + 1e-6), 0.0)
    delta_heads = (raw * factor[None, :, None] * delta_gain[:, None, :]).astype(bf16)
    return (heads_first(delta_heads), heads_first(attn_heads))


def solution(mesh):
    grid = Mesh(mesh.devices.reshape(4, 4, 4, 8), SEQ + ("head",))
    rows = P(SEQ, "head", None)
    pairs = P(SEQ, "head")
    block = P(SEQ)
    return jax.shard_map(
        shards,
        mesh=grid,
        in_specs=(rows, rows, rows, pairs, pairs, block, P("head", None), rows, rows, rows, block, block),
        out_specs=(rows, rows),
        check_vma=False,
    )
```

time: 843 us -> 217 us (0.26)
  the two profiles are of different devices: /device:TPU:486 before, /device:TPU:480 now
where the time goes in v1:
time: 217 us; the launch traced here: 215 us
  starting transfers between devices  96.4 us (44%)
  blocking collectives  52.7 us (24%)
  waiting for transfers between devices  38.7 us (18%)
  Pallas kernels  16.5 us (8%)
  local copies, waits for them, and re-layouts  7.33 us (3%)
  between operations  2.44 us (1%)
    all_to_all x1, starting transfers between devices, entering_states(): return lax.all_to_all(states, 'x', 0, 0, tiled=True)  77.9 us
    all_to_all x1, blocking collectives, entering_states(): parts = lax.all_to_all(planes, 'zl', 0, 0, tiled=True)  25.5 us
    all_to_all x1, blocking collectives, entering_states(): exchanged = lax.all_to_all(maps, 'x', 0, 0, tiled=True)  16.4 us
    ppermute x1, waiting for transfers between devices, entering_states(): earlier = lax.ppermute(group_total, 'zh', [(0, 1), (1, 2), (2, 3)])  15 us
    ppermute x1, waiting for transfers between devices, entering_states(): two = lax.ppermute(pair, 'zh', [(1, 3)])  13.8 us
    all_gather x1, blocking collectives, shards(): square_sum = jnp.sum(lax.all_gather(squares[0], 'head'), axis=0)  10.8 us
    ppermute x4, starting transfers between devices, window_blocks(): blocks.append(lax.ppermute(own, SEQ, route))  9.76 us
    pallas_call x1, Pallas kernels, shards(): call(block_terms, (shape_of(HEADS, KD, KD + VD), shape_of(HEADS, ROWS, KD...  8.27 us
  transfers between devices with their start and end apart: 9, of which 4 were waited for; matrix products, arithmetic and copies ran while one was open for 1% of the time, Pallas kernels for 3%

profile of v1, /device:TPU:480, one launch (start us, length us, event | category | flops | bytes accessed | tf_op | source)
XLA Modules:
  0.0 215.1 jit_solution(6144271852570615651)
XLA Ops:
  1.4 1.1 copy.52
  2.5 0.1 copy_bitcast_fusion.4
  2.6 8.3 %shard_map.131 = (f32[4,128,384]{2,1,0:T(8,128)S(1)}, f32[4,256,128]{2,1,0:T(8,128)S(1)}, f32[4,256,256]{2,1,0:T(8,128)S(1)}) custom-call(s32[1]{0:T(128)} %copy.55.count_ref, bf16[4,256,128]{2,1,0:T(8,128)(2,1)S(1)} %get-tuple-element.29.q_ref, bf16[4,256,128]{2,1,0:T(8,128)(2,1)S(1)} %get-tuple-element.28.k_ref, bf16[4,256,256]{2,1,0:T(8,128)(2,1)S(1)} %bitcast.32, ...), custom_call_target="tpu_custom_call" | custom-call | tf_op jit(solution)/shard_map/pallas_call | solution.py:274
  10.9 0.0 copy-start.2
  10.9 16.4 %all_to_all.20.maps_ref = f32[4,128,384]{2,1,0:T(8,128)S(1)} all-to-all(f32[4,128,384]{2,1,0:T(8,128)S(1)} %get-tuple-element.13), channel_id=1, replica_groups=mesh['zh'=4,'zl'=4,'x'=4,'head'=8] {'x'}, dimensions={0} | all-to-all | bytes 1572864 | tf_op jit(solution)/shard_map/all_to_all | solution.py:234
  27.3 0.7 shard_map.132
  28.1 0.8 copy-done
  28.9 0.1 copy.35
  29.0 0.0 copy-start.14
  29.0 0.0 copy-start.8
  29.0 0.1 copy.36
  29.1 0.8 pad_maximum_fusion.1
  29.9 5.5 %all-to-all-start.1 = ((f32[4,128,192]{1,2,0:T(8,128)}), f32[4,128,192]{1,2,0:T(8,128)S(1)}, u32[]{:S(2)}, u32[]{:S(2)}) async-start(f32[4,128,192]{1,2,0:T(8,128)} %pad_maximum_fusion.1), calls=%async_computation.1 | async-start | bytes 786432 | tf_op jit(solution)/shard_map/all_to_all | solution.py:240
  36.1 0.1 copy.51
  36.2 7.6 %all-to-all-done.1 = f32[4,128,192]{1,2,0:T(8,128)S(1)} async-done(((f32[4,128,192]{1,2,0:T(8,128)}), f32[4,128,192]{1,2,0:T(8,128)S(1)}, u32[]{:S(2)}, u32[]{:S(2)}) %all-to-all-start.1) | async-done | bytes 393248 | tf_op jit(solution)/shard_map/all_to_all | solution.py:240
  43.8 0.2 copy.37.maps_ref
  44.0 0.6 shard_map.133
  44.6 0.0 copy-start.4
  44.6 1.3 collective-permute-start
  46.0 15.0 %collective-permute-done.earlier_ref = f32[128,192]{1,0:T(8,128)S(1)} collective-permute-done((f32[128,192]{1,0:T(8,128)S(1)}, f32[128,192]{1,0:T(8,128)S(1)}, u32[]{:S(2)}, u32[]{:S(2)}) %collective-permute-start) | collective-permute-done | bytes 98336 | tf_op jit(solution)/shard_map/ppermute | solution.py:246
  60.9 0.2 shard_map.134
  61.1 0.7 collective-permute-start.1
  61.8 0.1 pad_maximum_fusion.own_ref
  61.9 2.5 %collective-permute-start.3 = (bf16[4,272,384]{2,1,0:T(8,128)(2,1)S(1)}, bf16[4,272,384]{2,1,0:T(8,128)(2,1)S(1)}, u32[]{:S(2)}, u32[]{:S(2)}) collective-permute-start(bf16[4,272,384]{2,1,0:T(8,128)(2,1)S(1)} %pad_maximum_fusion.own_ref), channel_id=1, source_target_pairs={{0,8},{8,16},{16,24},{24,32},{32,40},{40,48},{48,56},{56,64},{64,7... | collective-permute-start | bytes 2506760 | tf_op jit(solution)/shard_map/ppermute | solution.py:229
  64.4 4.1 %collective-permute-start.4 = (bf16[4,272,384]{2,1,0:T(8,128)(2,1)S(1)}, bf16[4,272,384]{2,1,0:T(8,128)(2,1)}, u32[]{:S(2)}, u32[]{:S(2)}) collective-permute-start(bf16[4,272,384]{2,1,0:T(8,128)(2,1)S(1)} %pad_maximum_fusion.own_ref), channel_id=1, source_target_pairs={{0,16},{8,24},{16,32},{24,40},{32,48},{40,56},{48,64},{56,72},{64,... | collective-permute-start | bytes 2506760 | tf_op jit(solution)/shard_map/ppermute | solution.py:229
  68.5 1.9 collective-permute-start.5
  70.4 1.3 collective-permute-start.6
  71.7 0.0 collective-permute-done.1.one_ref
  71.7 1.3 collective-permute-start.2
  73.0 13.8 %collective-permute-done.2.two_ref = f32[128,64]{1,0:T(8,128)S(1)} collective-permute-done((f32[128,64]{1,0:T(8,128)S(1)}, f32[128,64]{1,0:T(8,128)S(1)}, u32[]{:S(2)}, u32[]{:S(2)}) %collective-permute-start.2) | collective-permute-done | bytes 32800 | tf_op jit(solution)/shard_map/ppermute | solution.py:249
  86.8 1.0 copy-done.5
  87.8 0.4 shard_map.135
  88.3 0.1 copy.38
  88.4 25.5 %all_to_all.21 = f32[4,128,64]{1,2,0:T(8,128)S(1)} all-to-all(f32[4,128,64]{1,2,0:T(8,128)S(1)} %copy.38), channel_id=1, replica_groups=mesh['zh'=4,'zl'=4,'x'=4,'head'=8] {'zl'}, dimensions={0} | all-to-all | bytes 262144 | tf_op jit(solution)/shard_map/all_to_all | solution.py:254
  113.9 0.1 copy.39.parts_ref
  114.0 1.1 copy-done.1
  115.1 1.2 shard_map.136
  116.3 77.9 %all-to-all-start.3 = ((f32[4,128,256]{2,1,0:T(8,128)}), f32[4,128,256]{2,1,0:T(8,128)S(1)}, u32[]{:S(2)}, u32[]{:S(2)}) async-start(f32[4,128,256]{2,1,0:T(8,128)} %shard_map.136), calls=%async_computation.3 | async-start | bytes 1048576 | tf_op jit(solution)/shard_map/all_to_all | solution.py:256
  194.2 0.0 collective-permute-done.3.one_ref
  194.2 0.0 collective-permute-done.5.three_ref
  194.3 4.4 %shard_map.138 = bf16[4,256,256]{2,1,0:T(8,128)(2,1)S(1)} custom-call(bf16[4,256,128]{2,1,0:T(8,128)(2,1)S(1)} %bitcast.33, bf16[4,272,384]{2,1,0:T(8,128)(2,1)S(1)} %pad_maximum_fusion.own_ref, bf16[4,272,384]{2,1,0:T(8,128)(2,1)S(1)} %collective-permute-done.3.one_ref, bf16[4,272,384]{2,1,0:T(8,128)(2,1)} %collective-permute-done.4.two_ref, ...), custom_call_target="tpu_custom_call" | custom-call | tf_op jit(solution)/shard_map/pallas_call | solution.py:289
  198.6 0.0 copy-start.3
  198.7 1.2 copy.44
  199.9 2.4 %all-to-all-done.3.state_ref = f32[4,128,256]{2,1,0:T(8,128)S(1)} async-done(((f32[4,128,256]{2,1,0:T(8,128)}), f32[4,128,256]{2,1,0:T(8,128)S(1)}, u32[]{:S(2)}, u32[]{:S(2)}) %all-to-all-start.3) | async-done | bytes 524320 | tf_op jit(solution)/shard_map/all_to_all | solution.py:256
  202.3 0.6 shard_map.137
  202.9 10.8 %all-gather = f32[8,1,256]{2,1,0:T(1,128)S(1)} all-gather(f32[1,1,256]{2,1,0:T(1,128)S(1)} %slice_bitcast_fusion), channel_id=1, replica_groups=mesh['zh'=4,'zl'=4,'x'=4,'head'=8] {'head'}, dimensions={0}, use_global_device_ids=true | all-gather | bytes 9216 | tf_op jit(solution)/shard_map/all_gather | solution.py:295
  213.7 0.2 fusion
  213.9 1.2 copy.43
  (37 shorter events, 0.2 us)
Async XLA Ops:
  0.6 1.9 copy-start.12
  0.6 1.9 copy-start.11
  1.4 1.2 copy-start.6
  1.4 1.2 copy-start.7
  10.9 17.1 %copy-start.2 = (f32[4,256,128]{2,1,0:T(8,128)}, f32[4,256,128]{2,1,0:T(8,128)S(1)}, u32[]{:S(2)}) copy-start(f32[4,256,128]{2,1,0:T(8,128)S(1)} %get-tuple-element.11.carry_ref) | copy-start | bytes 1572868
  28.1 0.8 copy-start
  29.0 7.0 %copy-start.14 = (s32[256]{0:T(256)S(1)}, s32[256]{0:T(256)}, u32[]{:S(2)}) copy-start(s32[256]{0:T(256)} %param.22) | copy-start | bytes 3076
  29.0 7.1 %copy-start.8 = (bf16[256,4,256]{2,1,0:T(4,128)(2,1)S(1)}, bf16[256,4,256]{2,1,0:T(4,128)(2,1)}, u32[]{:S(2)}) copy-start(bf16[256,4,256]{2,1,0:T(4,128)(2,1)} %param.21) | copy-start | bytes 1572868
  29.9 6.3 %copy-start.9 = (bf16[256,4,128]{2,1,0:T(4,128)(2,1)S(1)}, bf16[256,4,128]{2,1,0:T(4,128)(2,1)}, u32[]{:S(2)}) copy-start(bf16[256,4,128]{2,1,0:T(4,128)(2,1)} %param.20) | copy-start | bytes 786436
  29.9 13.9 %all-to-all-start.1 = ((f32[4,128,192]{1,2,0:T(8,128)}), f32[4,128,192]{1,2,0:T(8,128)S(1)}, u32[]{:S(2)}, u32[]{:S(2)}) async-start(f32[4,128,192]{1,2,0:T(8,128)} %pad_maximum_fusion.1), calls=%async_computation.1 | async-start | bytes 786432 | tf_op jit(solution)/shard_map/all_to_all | solution.py:240
  44.6 17.2 %copy-start.4 = (f32[3,128,192]{2,1,0:T(8,128)}, f32[3,128,192]{2,1,0:T(8,128)S(1)}, u32[]{:S(2)}) copy-start(f32[3,128,192]{2,1,0:T(8,128)S(1)} %get-tuple-element.16.before_ref) | copy-start | bytes 884740
  44.6 16.3 %collective-permute-start = (f32[128,192]{1,0:T(8,128)S(1)}, f32[128,192]{1,0:T(8,128)S(1)}, u32[]{:S(2)}, u32[]{:S(2)}) collective-permute-start(f32[128,192]{1,0:T(8,128)S(1)} %get-tuple-element.15.map_ref), channel_id=1, source_target_pairs={{0,128},{128,256},{256,384},{1,129},{129,257},{257,385},{2,130},{1... | collective-permute-start | bytes 294920 | tf_op jit(solution)/shard_map/ppermute | solution.py:246
  61.1 10.6 %collective-permute-start.1 = (f32[128,64]{1,0:T(8,128)S(1)}, f32[128,64]{1,0:T(8,128)S(1)}, u32[]{:S(2)}, u32[]{:S(2)}) collective-permute-start(f32[128,64]{1,0:T(8,128)S(1)} %shard_map.134), channel_id=1, source_target_pairs={{128,256},{129,257},{130,258},{131,259},{132,260},{133,261},{134,2... | collective-permute-start | bytes 98312 | tf_op jit(solution)/shard_map/ppermute | solution.py:248
  61.9 132.3 %collective-permute-start.3 = (bf16[4,272,384]{2,1,0:T(8,128)(2,1)S(1)}, bf16[4,272,384]{2,1,0:T(8,128)(2,1)S(1)}, u32[]{:S(2)}, u32[]{:S(2)}) collective-permute-start(bf16[4,272,384]{2,1,0:T(8,128)(2,1)S(1)} %pad_maximum_fusion.own_ref), channel_id=1, source_target_pairs={{0,8},{8,16},{16,24},{24,32},{32,40},{40,48},{48,56},{56,64},{64,7... | collective-permute-start | bytes 2506760 | tf_op jit(solution)/shard_map/ppermute | solution.py:229
  64.4 129.8 %collective-permute-start.4 = (bf16[4,272,384]{2,1,0:T(8,128)(2,1)S(1)}, bf16[4,272,384]{2,1,0:T(8,128)(2,1)}, u32[]{:S(2)}, u32[]{:S(2)}) collective-permute-start(bf16[4,272,384]{2,1,0:T(8,128)(2,1)S(1)} %pad_maximum_fusion.own_ref), channel_id=1, source_target_pairs={{0,16},{8,24},{16,32},{24,40},{32,48},{40,56},{48,64},{56,72},{64,... | collective-permute-start | bytes 2506760 | tf_op jit(solution)/shard_map/ppermute | solution.py:229
  68.5 125.7 %collective-permute-start.5 = (bf16[4,272,384]{2,1,0:T(8,128)(2,1)S(1)}, bf16[4,272,384]{2,1,0:T(8,128)(2,1)}, u32[]{:S(2)}, u32[]{:S(2)}) collective-permute-start(bf16[4,272,384]{2,1,0:T(8,128)(2,1)S(1)} %pad_maximum_fusion.own_ref), channel_id=1, source_target_pairs={{0,24},{8,32},{16,40},{24,48},{32,56},{40,64},{48,72},{56,80},{64,... | collective-permute-start | bytes 2506760 | tf_op jit(solution)/shard_map/ppermute | solution.py:229
  70.4 123.8 %collective-permute-start.6 = (bf16[4,272,384]{2,1,0:T(8,128)(2,1)S(1)}, bf16[4,272,384]{2,1,0:T(8,128)(2,1)}, u32[]{:S(2)}, u32[]{:S(2)}) collective-permute-start(bf16[4,272,384]{2,1,0:T(8,128)(2,1)S(1)} %pad_maximum_fusion.own_ref), channel_id=1, source_target_pairs={{0,32},{8,40},{16,48},{24,56},{32,64},{40,72},{48,80},{56,88},{64,... | collective-permute-start | bytes 2506760 | tf_op jit(solution)/shard_map/ppermute | solution.py:229
  71.7 15.1 %collective-permute-start.2 = (f32[128,64]{1,0:T(8,128)S(1)}, f32[128,64]{1,0:T(8,128)S(1)}, u32[]{:S(2)}, u32[]{:S(2)}) collective-permute-start(f32[128,64]{1,0:T(8,128)S(1)} %shard_map.134), channel_id=1, source_target_pairs={{128,384},{129,385},{130,386},{131,387},{132,388},{133,389},{134,3... | collective-permute-start | bytes 98312 | tf_op jit(solution)/shard_map/ppermute | solution.py:249
  86.8 1.0 copy-start.5
  114.0 1.1 copy-start.1
  115.1 79.1 %copy-start.10 = (bf16[256,4,128]{2,1,0:T(4,128)(2,1)S(1)}, bf16[256,4,128]{2,1,0:T(4,128)(2,1)}, u32[]{:S(2)}) copy-start(bf16[256,4,128]{2,1,0:T(4,128)(2,1)} %param.19) | copy-start | bytes 786436
  116.3 86.0 %all-to-all-start.3 = ((f32[4,128,256]{2,1,0:T(8,128)}), f32[4,128,256]{2,1,0:T(8,128)S(1)}, u32[]{:S(2)}, u32[]{:S(2)}) async-start(f32[4,128,256]{2,1,0:T(8,128)} %shard_map.136), calls=%async_computation.3 | async-start | bytes 1048576 | tf_op jit(solution)/shard_map/all_to_all | solution.py:256
  198.6 3.6 %copy-start.3 = (f32[4,256,128]{2,1,0:T(8,128)S(1)}, f32[4,256,128]{2,1,0:T(8,128)}, u32[]{:S(2)}) copy-start(f32[4,256,128]{2,1,0:T(8,128)} %copy-done.2) | copy-start | bytes 1572868
  202.3 11.5 %copy-start.13 = (f32[4,256]{1,0:T(4,128)S(1)}, f32[4,256]{1,0:T(4,128)}, u32[]{:S(2)}) copy-start(f32[4,256]{1,0:T(4,128)} %param.18) | copy-start | bytes 12292

commit v2 on v1

v2 whole, which is shorter than its diff:
```python
import jax
import jax.numpy as jnp
from jax import lax
from jax.experimental import pallas as pl
from jax.experimental.pallas import tpu as pltpu
from jax.sharding import Mesh, PartitionSpec as P

ROWS = 256
KD = 128
VD = 256
HEADS = 4
HIDDEN = 8192
WINDOW = 2048
PART = VD // 4
MARK_ROWS = 16
VMEM_BYTES = 48 * 2**20

SEQ = ("zh", "zl", "x")
f32 = jnp.float32
bf16 = jnp.bfloat16


def halves(x):
    high = x.astype(bf16)
    return high, (x - high.astype(f32)).astype(bf16)


def dot(a, b, dims=((1,), (0,))):
    return lax.dot_general(a, b, (dims, ((), ())), preferred_element_type=f32)


def dot3(a, b):
    ah, al = halves(a)
    bh, bl = halves(b)
    return dot(ah, bh) + (dot(ah, bl) + dot(al, bh))


def dot2(a, b):
    ah, al = halves(a)
    return dot(ah, b) + dot(al, b)


def call(body, out_shape, scalars=0, inputs=1, scratch=(), flops=1e7):
    whole = pl.BlockSpec(memory_space=pltpu.VMEM)
    small = pl.BlockSpec(memory_space=pltpu.SMEM)
    return pl.pallas_call(
        body,
        in_specs=[small] * scalars + [whole] * inputs,
        out_specs=jax.tree.map(lambda _: whole, out_shape),
        out_shape=out_shape,
        scratch_shapes=list(scratch),
        cost_estimate=pl.CostEstimate(flops=int(flops), bytes_accessed=10**6, transcendentals=0),
        compiler_params=pltpu.CompilerParams(vmem_limit_bytes=VMEM_BYTES),
    )


def block_terms(
    count_ref, q_ref, k_ref, v_ref, gate_ref, beta_ref, map_ref, new_ref, mixing_ref, carry_ref, x_ref, a_ref
):
    count = count_ref[0]
    row = lax.broadcasted_iota(jnp.int32, (ROWS, ROWS), 0)
    col = lax.broadcasted_iota(jnp.int32, (ROWS, ROWS), 1)
    lane = lax.broadcasted_iota(jnp.int32, (1, ROWS), 1)
    eye = row == col
    kept = []
    for h in range(HEADS):
        k = k_ref[h]
        gate = jnp.where(lane < count, gate_ref[h : h + 1, :], 0.0)
        beta = jnp.where(lane < count, beta_ref[h : h + 1, :], 0.0)
        log_col = jnp.sum(jnp.where(col <= row, gate, 0.0), axis=1, keepdims=True)
        log_row = jnp.sum(jnp.where(eye, log_col, 0.0), axis=0, keepdims=True)
        beta_col = jnp.sum(jnp.where(eye, beta, 0.0), axis=1, keepdims=True)
        gram = dot(k, k, ((1,), (1,)))
        squares = jnp.where(eye, gram, 0.0)
        k_col = lax.rsqrt(jnp.sum(squares, axis=1, keepdims=True) + 1e-6)
        k_row = lax.rsqrt(jnp.sum(squares, axis=0, keepdims=True) + 1e-6)
        decay = jnp.where(col <= row, jnp.exp(jnp.minimum(log_col - log_row, 0.0)), 0.0)
        a = jnp.where(col < row, (beta_col * k_col) * decay * (gram * k_row), 0.0)
        a_ref[h] = a
        x_ref[h] = jnp.where(eye, 1.0, jnp.where((row >> 1) == (col >> 1), -a, 0.0))
        q = q_ref[h]
        wide = q.astype(f32)
        q_col = lax.rsqrt(jnp.sum(wide * wide, axis=1, keepdims=True) + 1e-6)
        mixing_ref[h] = (q_col * decay) * (dot(q, k, ((1,), (1,))) * k_row)
        kept.append((log_col, log_row, beta, k_col, k_row, q_col))
    step = 1
    while (2 << step) <= ROWS:
        m = 1 << step
        for h in range(HEADS):
            x = x_ref[h]
            if m < 64:
                below = ((row >> (step + 1)) == (col >> (step + 1))) & ((row >> step) != (col >> step))
                x_ref[h] = x - dot3(dot3(x, jnp.where(below, a_ref[h], 0.0)), x)
            else:
                for s in range(0, ROWS, 2 * m):
                    first = x[s : s + m, s : s + m]
                    second = x[s + m : s + 2 * m, s + m : s + 2 * m]
                    between = a_ref[h, s + m : s + 2 * m, s : s + m]
                    x_ref[h, s + m : s + 2 * m, s : s + m] = -dot3(second, dot3(between, first))
        step += 1
    row_k = lax.broadcasted_iota(jnp.int32, (KD, KD), 0)
    col_k = lax.broadcasted_iota(jnp.int32, (KD, KD), 1)
    for h in range(HEADS):
        log_col, log_row, beta, k_col, k_row, q_col = kept[h]
        k = k_ref[h]
        x = x_ref[h]
        new_value = dot2(x * beta, v_ref[h])
        new_key = dot2(x * (beta * jnp.exp(log_row) * k_row), k)
        new = jnp.concatenate([new_key, new_value], axis=1)
        last = log_col[ROWS - 1 : ROWS, :]
        high, low = halves((jnp.exp(last - log_col) * k_col) * new)
        update = dot(k, high, ((0,), (0,))) + dot(k, low, ((0,), (0,)))
        map_ref[h, :, :KD] = jnp.where(row_k == col_k, jnp.exp(last), 0.0) - update[:, :KD]
        map_ref[h, :, KD:] = update[:, KD:]
        new_ref[h] = new
        carry_ref[h] = (jnp.exp(log_col) * q_col) * q_ref[h].astype(f32)


def row_terms(new_ref, mixing_ref, straight_ref, carry_ref, local_ref):
    for h in range(HEADS):
        mixed = dot3(mixing_ref[h], new_ref[h])
        carry_ref[h] = straight_ref[h] - mixed[:, :KD]
        local_ref[h] = mixed[:, KD:]


def fold(x):
    half = KD // 2
    return jnp.concatenate([x[:half, :], x[half:, :]], axis=1)


def unfold(x):
    return jnp.concatenate([x[:, :PART], x[:, PART:]], axis=0)


def then(state, transition, offset):
    state = dot3(transition, state)
    return jnp.concatenate([state[:, :KD], state[:, KD:] + offset], axis=1)


def compose_plane(maps_ref, before_ref, send_ref):
    state = maps_ref[0]
    for i in range(1, 4):
        before_ref[i - 1] = state
        state = then(state, maps_ref[i, :, :KD], maps_ref[i, :, KD:])
    for i in range(4):
        send_ref[i, :KD, :] = state[:, :KD]
        send_ref[i, KD:, :] = fold(state[:, KD + i * PART : KD + (i + 1) * PART])


def compose_group(maps_ref, before_ref, total_ref, offset_ref):
    state = jnp.concatenate([maps_ref[0, :KD, :], unfold(maps_ref[0, KD:, :])], axis=1)
    for i in range(1, 4):
        before_ref[i - 1] = state
        state = then(state, maps_ref[i, :KD, :], unfold(maps_ref[i, KD:, :]))
    offset = fold(state[:, KD:])
    total_ref[:KD, :] = state[:, :KD]
    total_ref[KD:, :] = offset
    offset_ref[...] = offset


def step_state(map_ref, earlier_ref, out_ref):
    state = dot3(map_ref[:KD, :], unfold(earlier_ref[...]))
    out_ref[...] = fold(state) + map_ref[KD:, :]


def group_states(place_ref, first_ref, one_ref, two_ref, third_ref, before_ref, out_ref):
    place = place_ref[0]
    last = fold(dot3(third_ref[:KD, :], unfold(two_ref[...]))) + third_ref[KD:, :]
    state = jnp.where(
        place == 0,
        0.0,
        jnp.where(place == 1, first_ref[...], jnp.where(place == 2, one_ref[...], last)),
    )
    out_ref[0] = state
    state = unfold(state)
    for i in range(3):
        out_ref[i + 1] = fold(dot3(before_ref[i, :, :KD], state) + before_ref[i, :, KD:])


def plane_states(parts_ref, before_ref, attn_ref, out_ref):
    state = jnp.concatenate([unfold(parts_ref[i]) for i in range(4)], axis=1)
    for i in range(4):
        entering = state
        if i > 0:
            entering = dot3(before_ref[i - 1, :, :KD], state) + before_ref[i - 1, :, KD:]
        out_ref[i, :KD, :], out_ref[i, KD : 2 * KD, :] = halves(entering)
        out_ref[i, 2 * KD :, :] = attn_ref[i]


def raw_rows(carry_ref, local_ref, state_ref, raw_ref, square_ref):
    total = jnp.zeros((ROWS, VD), f32)
    for h in range(HEADS):
        carry_high, carry_low = halves(carry_ref[h])
        high, low = state_ref[h, :KD, :], state_ref[h, KD : 2 * KD, :]
        raw = local_ref[h] + dot(carry_high, high) + (dot(carry_high, low) + dot(carry_low, high))
        raw_ref[h] = raw
        total = total + raw * raw
    column = jnp.sum(total, axis=1, keepdims=True)
    row = lax.broadcasted_iota(jnp.int32, (ROWS, ROWS), 0)
    col = lax.broadcasted_iota(jnp.int32, (ROWS, ROWS), 1)
    square_ref[...] = jnp.broadcast_to(
        jnp.sum(jnp.where(row == col, column, 0.0), axis=0, keepdims=True), square_ref.shape
    )


def normed(count_ref, raw_ref, square_ref, gain_ref, out_ref):
    row = lax.broadcasted_iota(jnp.int32, (ROWS, ROWS), 0)
    col = lax.broadcasted_iota(jnp.int32, (ROWS, ROWS), 1)
    total = square_ref[0:1, :]
    for i in range(1, 8):
        total = total + square_ref[8 * i : 8 * i + 1, :]
    column = jnp.sum(jnp.where(row == col, total, 0.0), axis=1, keepdims=True)
    live = lax.broadcasted_iota(jnp.int32, (ROWS, 1), 0) < count_ref[0]
    factor = jnp.where(live, lax.rsqrt(column * (1.0 / HIDDEN) + 1e-6), 0.0)
    for h in range(HEADS):
        out_ref[h] = (raw_ref[h] * factor * gain_ref[h : h + 1, :]).astype(bf16)


def pack_blocks(count_ref, key_ref, value_ref, query_ref, position_ref, out_ref):
    lane = lax.broadcasted_iota(jnp.int32, (1, ROWS), 1)
    marks = jnp.where(lane < count_ref[0], position_ref[...] + 1, 0)
    spot = lax.broadcasted_iota(jnp.int32, (MARK_ROWS, ROWS), 0)
    coded = jnp.where(spot == 0, marks >> 8, jnp.where(spot == 1, marks & 255, 0))
    coded = coded.astype(f32).astype(bf16)
    for h in range(HEADS):
        out_ref[h, :ROWS, :KD] = key_ref[h]
        out_ref[h, :ROWS, KD : KD + VD] = value_ref[h]
        out_ref[h, :ROWS, KD + VD :] = query_ref[h]
        out_ref[h, ROWS:, :ROWS] = coded
        out_ref[h, ROWS:, ROWS:] = jnp.zeros((MARK_ROWS, 2 * KD + VD - ROWS), bf16)


def attend(here_ref, past_ref, out_ref):
    row = lax.broadcasted_iota(jnp.int32, (ROWS, ROWS), 0)
    col = lax.broadcasted_iota(jnp.int32, (ROWS, ROWS), 1)

    def marks_of(ref, j):
        coded = ref[j, ROWS : ROWS + MARK_ROWS, :ROWS].astype(f32)
        return coded[0:1, :] * 256.0 + coded[1:2, :]

    marks = [marks_of(here_ref, j) for j in range(4)]
    here_marks = [jnp.where(m > 0.0, m, 1e9) for m in marks]
    past_marks = [marks_of(past_ref, j) for j in range(4)]
    past_marks = [jnp.where(m > 0.0, m, 1e9) for m in past_marks]
    for j in range(4):
        query_marks = jnp.sum(jnp.where(row == col, marks[j], 0.0), axis=1, keepdims=True)
        q = here_ref[j, :ROWS, KD + VD :]
        sources = [(here_ref, i, here_marks[i]) for i in range(j + 1)]
        sources += [(past_ref, i, past_marks[i]) for i in range(j, 4)]
        scores = []
        for ref, i, key_marks in sources:
            score = dot(q, ref[i, :ROWS, :KD], ((1,), (1,))) * KD**-0.5
            allowed = (key_marks <= query_marks) & (key_marks > query_marks - float(WINDOW))
            scores.append(jnp.where(allowed, score, -1e30))
        top = scores[0]
        for score in scores[1:]:
            top = jnp.maximum(top, score)
        top = jnp.max(top, axis=1, keepdims=True)
        weight_sum = jnp.zeros((ROWS, ROWS), f32)
        mixed = jnp.zeros((ROWS, VD), f32)
        for score, (ref, i, key_marks) in zip(scores, sources):
            weights = jnp.exp(score - top)
            weight_sum = weight_sum + weights
            mixed = mixed + dot(weights.astype(bf16), ref[i, :ROWS, KD : KD + VD])
        mixed = mixed / jnp.sum(weight_sum, axis=1, keepdims=True)
        out_ref[j] = jnp.where(query_marks > 0.0, mixed, 0.0).astype(bf16)


def heads_first(block):
    return jnp.swapaxes(block, 0, 1)


def shape_of(*dims, kind=f32):
    return jax.ShapeDtypeStruct(dims, kind)


def shards(
    delta_query,
    delta_key,
    delta_value,
    delta_gate,
    delta_beta,
    delta_count,
    delta_gain,
    attn_query,
    attn_key,
    attn_value,
    attn_position,
    attn_count,
):
    packed = call(
        pack_blocks, shape_of(HEADS, ROWS + MARK_ROWS, 2 * KD + VD, kind=bf16), scalars=1, inputs=4
    )(
        attn_count,
        heads_first(attn_key),
        heads_first(attn_value),
        heads_first(attn_query),
        attn_position.reshape(1, ROWS),
    )
    here = lax.all_to_all(packed, "x", 0, 0, tiled=True)
    maps, new, mixing, straight = call(
        block_terms,
        (
            shape_of(HEADS, KD, KD + VD),
            shape_of(HEADS, ROWS, KD + VD),
            shape_of(HEADS, ROWS, ROWS),
            shape_of(HEADS, ROWS, KD),
        ),
        scalars=1,
        inputs=5,
        scratch=[pltpu.VMEM((HEADS, ROWS, ROWS), f32)] * 2,
        flops=8e9,
    )(
        delta_count,
        heads_first(delta_query),
        heads_first(delta_key),
        heads_first(delta_value),
        delta_gate.T,
        delta_beta.T,
    )
    maps, here, past = lax.optimization_barrier((maps, here, here[:, :, : KD + VD]))
    past = lax.ppermute(past, ("zh", "zl"), [(i, i + 1) for i in range(15)])
    exchanged = lax.all_to_all(maps, "x", 0, 0, tiled=True)
    carry, local = call(
        row_terms, (shape_of(HEADS, ROWS, KD), shape_of(HEADS, ROWS, VD)), inputs=3, flops=2e9
    )(new, mixing, straight)
    plane_prefix, plane_total = call(
        compose_plane, (shape_of(3, KD, KD + VD), shape_of(4, KD + PART, KD))
    )(exchanged)
    gathered = lax.all_to_all(plane_total, "zl", 0, 0, tiled=True)
    group_prefix, group_total, group_offset = call(
        compose_group,
        (shape_of(3, KD, KD + PART), shape_of(KD + PART, KD), shape_of(PART, KD)),
    )(gathered)
    first = lax.ppermute(group_offset, "zh", [(0, 1)])
    third = lax.ppermute(group_total, "zh", [(2, 3)])
    pair = call(step_state, shape_of(PART, KD), inputs=2)(group_total, first)
    one = lax.ppermute(pair, "zh", [(1, 2)])
    two = lax.ppermute(pair, "zh", [(1, 3)])
    place = lax.axis_index("zh").astype(jnp.int32).reshape(1)
    planes = call(group_states, shape_of(4, PART, KD), scalars=1, inputs=5)(
        place, first, one, two, third, group_prefix
    )
    planes, past = lax.optimization_barrier((planes, past))
    attn_heads = call(attend, shape_of(4, ROWS, VD, kind=bf16), inputs=2, flops=8e9)(here, past)
    parts = lax.all_to_all(planes, "zl", 0, 0, tiled=True)
    returned = call(plane_states, shape_of(4, 2 * KD + ROWS, VD, kind=bf16), inputs=3)(
        parts, plane_prefix, attn_heads
    )
    states = lax.all_to_all(returned, "x", 0, 0, tiled=True)
    raw, squares = call(
        raw_rows, (shape_of(HEADS, ROWS, VD), shape_of(64, ROWS)), inputs=3
    )(carry, local, states)
    squares = lax.all_to_all(squares, "head", 0, 0, tiled=True)
    delta_heads = call(normed, shape_of(HEADS, ROWS, VD, kind=bf16), scalars=1, inputs=3)(
        delta_count, raw, squares, delta_gain
    )
    return (heads_first(delta_heads), heads_first(states[:, 2 * KD :]))


def solution(mesh):
    grid = Mesh(mesh.devices.reshape(4, 4, 4, 8), SEQ + ("head",))
    rows = P(SEQ, "head", None)
    pairs = P(SEQ, "head")
    block = P(SEQ)
    return jax.shard_map(
        shards,
        mesh=grid,
        in_specs=(rows, rows, rows, pairs, pairs, block, P("head", None), rows, rows, rows, block, block),
        out_specs=(rows, rows),
        check_vma=False,
    )
```

time: 217 us -> 123 us (0.57)
  starting transfers between devices: 96.4 us -> 31.5 us
  blocking collectives: 52.7 us -> 13.8 us
  local copies, waits for them, and re-layouts: 7.33 us -> 12.2 us
  waiting for transfers between devices: 38.7 us -> 42 us
  Pallas kernels: 16.5 us -> 19.6 us
    all_to_all x2 -> x5, starting transfers between devices: 83.4 us -> 26.4 us  [the longest x1 8.36 us: shards(): parts = lax.all_to_all(planes, 'zl', 0, 0, tiled=True)]
    all_to_all x2 -> x1, blocking collectives: 41.9 us -> 13.8 us  [shards(): exchanged = lax.all_to_all(maps, 'x', 0, 0, tiled=True)]
    all_to_all x2 -> x5, waiting for transfers between devices: 9.96 us -> 24.2 us  [the longest x1 7.5 us: shards(): states = lax.all_to_all(returned, 'x', 0, 0, tiled=True)]
    ppermute x7 -> x5, waiting for transfers between devices: 28.8 us -> 17.8 us  [the longest x1 17.8 us: shards(): two = lax.ppermute(pair, 'zh', [(1, 3)])]
    all_gather x1 -> x0, blocking collectives: 10.8 us -> none  [shards(): square_sum = jnp.sum(lax.all_gather(squares[0], 'head'), axis=0)]
    ppermute x7 -> x5, starting transfers between devices: 13 us -> 5.19 us  [the longest x1 1.29 us: shards(): third = lax.ppermute(group_total, 'zh', [(2, 3)])]
    unnamed x37 -> x38, local copies, waits for them, and re-layouts: 6.6 us -> 11.1 us
    pallas_call x7 -> x10, Pallas kernels: 8.19 us -> 12.1 us  [the longest x1 3.02 us: shards(): call(attend, shape_of(4, ROWS, VD, kind=bf16), inputs=2, flops=8000000000.0)]
  transfers between devices with their start and end apart: 9 -> 10, of which waited for: 4 -> 6; matrix products, arithmetic and copies ran while one was open for 1% -> 1% of each run, Pallas kernels for 3% -> 11%
where the time goes in v2:
time: 123 us; the launch traced here: 121 us
  waiting for transfers between devices  42 us (34%)
  starting transfers between devices  31.5 us (26%)
  Pallas kernels  19.6 us (16%)
  blocking collectives  13.8 us (11%)
  local copies, waits for them, and re-layouts  12.2 us (10%)
  between operations  2.26 us (2%)
    ppermute x1, waiting for transfers between devices, shards(): two = lax.ppermute(pair, 'zh', [(1, 3)])  17.8 us
    all_to_all x1, blocking collectives, shards(): exchanged = lax.all_to_all(maps, 'x', 0, 0, tiled=True)  13.8 us
    unnamed x38, local copies, waits for them, and re-layouts  11.1 us
    all_to_all x1, starting transfers between devices, shards(): parts = lax.all_to_all(planes, 'zl', 0, 0, tiled=True)  8.36 us
    pallas_call x1, Pallas kernels, shards(): call(block_terms, (shape_of(HEADS, KD, KD + VD), shape_of(HEADS, ROWS, KD...  7.51 us
    all_to_all x1, waiting for transfers between devices, shards(): states = lax.all_to_all(returned, 'x', 0, 0, tiled=True)  7.5 us
    all_to_all x1, waiting for transfers between devices, shards(): gathered = lax.all_to_all(plane_total, 'zl', 0, 0, tiled=True)  7.4 us
    all_to_all x1, starting transfers between devices, shards(): gathered = lax.all_to_all(plane_total, 'zl', 0, 0, tiled=True)  5.33 us
  transfers between devices with their start and end apart: 10, of which 6 were waited for; matrix products, arithmetic and copies ran while one was open for 1% of the time, Pallas kernels for 11%

profile of v2, /device:TPU:480, one launch (start us, length us, event | category | flops | bytes accessed | tf_op | source)
XLA Modules:
  0.0 121.4 jit_solution(3573726695766293940)
XLA Ops:
  1.4 1.1 copy.28
  2.5 0.1 copy_bitcast_fusion.2
  2.6 1.2 shard_map.133
  3.7 4.4 %all-to-all-start = ((bf16[4,272,512]{2,1,0:T(8,128)(2,1)}), bf16[4,272,512]{2,1,0:T(8,128)(2,1)S(1)}, u32[]{:S(2)}, u32[]{:S(2)}) async-start(bf16[4,272,512]{2,1,0:T(8,128)(2,1)} %shard_map.133), calls=%async_computation | async-start | bytes 2228224 | tf_op jit(solution)/shard_map/all_to_all | solution.py:300
  8.2 0.0 copy-start.5
  8.2 0.1 copy_bitcast_fusion.4
  8.9 0.1 copy.29
  9.0 7.5 %shard_map.131 = (f32[4,128,384]{2,1,0:T(8,128)S(1)}, f32[4,256,384]{2,1,0:T(8,128)S(1)}, f32[4,256,256]{2,1,0:T(8,128)S(1)}, f32[4,256,128]{2,1,0:T(8,128)S(1)}) custom-call(s32[1]{0:T(128)S(6)} %copy.30.count_ref, bf16[4,256,128]{2,1,0:T(8,128)(2,1)S(1)} %get-tuple-element.41.q_ref, bf16[4,256,128]{2,1,0:T(8,128)(2,1)S(1)} %get-tuple-element.40.k_ref, ...), custom_call_target="tpu_custom_call" | custom-call | flops 8000000000 | bytes 1000000 | tf_op jit(solution)/shard_map/pallas_call | solution.py:301
  16.6 1.2 copy-done.6
  17.7 1.0 copy-done.8
  18.7 0.8 copy-done.10
  19.5 4.4 %all-to-all-done.here_ref = bf16[4,272,512]{2,1,0:T(8,128)(2,1)S(1)} async-done(((bf16[4,272,512]{2,1,0:T(8,128)(2,1)}), bf16[4,272,512]{2,1,0:T(8,128)(2,1)S(1)}, u32[]{:S(2)}, u32[]{:S(2)}) %all-to-all-start) | async-done | bytes 1114144 | tf_op jit(solution)/shard_map/all_to_all | solution.py:300
  24.0 1.0 slice.8
  25.0 13.8 %all_to_all.36.maps_ref = f32[4,128,384]{2,1,0:T(8,128)S(1)} all-to-all(f32[4,128,384]{2,1,0:T(8,128)S(1)} %get-tuple-element.26), channel_id=1, replica_groups=mesh['zh'=4,'zl'=4,'x'=4,'head'=8] {'x'}, dimensions={0} | all-to-all | bytes 1572864 | tf_op jit(solution)/shard_map/all_to_all | solution.py:323
  38.7 1.6 %shard_map.134 = (f32[3,128,384]{2,1,0:T(8,128)S(1)}, f32[4,192,128]{2,1,0:T(8,128)}) custom-call(f32[4,128,384]{2,1,0:T(8,128)S(1)} %all_to_all.36.maps_ref), custom_call_target="tpu_custom_call" | custom-call | flops 10000000 | bytes 1000000 | tf_op jit(solution)/shard_map/pallas_call | solution.py:327
  40.3 5.3 %all-to-all-start.2 = ((f32[4,192,128]{2,1,0:T(8,128)}), f32[4,192,128]{2,1,0:T(8,128)S(1)}, u32[]{:S(2)}, u32[]{:S(2)}) async-start(f32[4,192,128]{2,1,0:T(8,128)} %get-tuple-element.27), calls=%async_computation.2 | async-start | bytes 786432 | tf_op jit(solution)/shard_map/all_to_all | solution.py:330
  45.6 1.3 %collective-permute-start.4 = (bf16[4,272,384]{2,1,0:T(8,128)(2,1)}, bf16[4,272,384]{2,1,0:T(8,128)(2,1)S(1)}, u32[]{:S(2)}, u32[]{:S(2)}) collective-permute-start(bf16[4,272,384]{2,1,0:T(8,128)(2,1)} %slice.8), channel_id=1, source_target_pairs={{0,32},{32,64},{64,96},{96,128},{128,160},{160,192},{192,224},{224... | collective-permute-start | bytes 2506760 | tf_op jit(solution)/shard_map/ppermute | solution.py:322
  46.9 7.4 %all-to-all-done.2.maps_ref = f32[4,192,128]{2,1,0:T(8,128)S(1)} async-done(((f32[4,192,128]{2,1,0:T(8,128)}), f32[4,192,128]{2,1,0:T(8,128)S(1)}, u32[]{:S(2)}, u32[]{:S(2)}) %all-to-all-start.2) | async-done | bytes 393248 | tf_op jit(solution)/shard_map/all_to_all | solution.py:330
  54.3 0.8 shard_map.135
  55.1 1.3 %collective-permute-start.3 = (f32[192,128]{1,0:T(8,128)S(1)}, f32[192,128]{1,0:T(8,128)S(1)}, u32[]{:S(2)}, u32[]{:S(2)}) collective-permute-start(f32[192,128]{1,0:T(8,128)S(1)} %get-tuple-element.29.map_ref), channel_id=1, source_target_pairs={{256,384},{257,385},{258,386},{259,387},{260,388},{261,389},{262,3... | collective-permute-start | bytes 294920 | tf_op jit(solution)/shard_map/ppermute | solution.py:336
  56.4 0.7 collective-permute-start
  57.1 0.0 collective-permute-done.earlier_ref.first_ref
  57.1 0.3 shard_map.136
  57.4 0.7 collective-permute-start.1
  58.0 1.3 %collective-permute-start.2 = (f32[64,128]{1,0:T(8,128)S(1)}, f32[64,128]{1,0:T(8,128)S(1)}, u32[]{:S(2)}, u32[]{:S(2)}) collective-permute-start(f32[64,128]{1,0:T(8,128)S(1)} %shard_map.136), channel_id=1, source_target_pairs={{128,384},{129,385},{130,386},{131,387},{132,388},{133,389},{134,3... | collective-permute-start | bytes 98312 | tf_op jit(solution)/shard_map/ppermute | solution.py:339
  59.4 0.0 collective-permute-done.1.one_ref
  59.4 17.8 %collective-permute-done.2.two_ref = f32[64,128]{1,0:T(8,128)S(1)} collective-permute-done((f32[64,128]{1,0:T(8,128)S(1)}, f32[64,128]{1,0:T(8,128)S(1)}, u32[]{:S(2)}, u32[]{:S(2)}) %collective-permute-start.2) | collective-permute-done | bytes 32800 | tf_op jit(solution)/shard_map/ppermute | solution.py:339
  77.1 0.0 collective-permute-done.3.third_ref
  77.1 1.3 %shard_map.137 = f32[4,64,128]{2,1,0:T(8,128)} custom-call(s32[1]{0:T(128)} %bitcast.5.place_ref, f32[64,128]{1,0:T(8,128)S(1)} %collective-permute-done.earlier_ref.first_ref, f32[64,128]{1,0:T(8,128)S(1)} %collective-permute-done.1.one_ref, f32[64,128]{1,0:T(8,128)S(1)} %collective-permute-done.2.two_ref, f32[192,128]{1,0:T(8,128)S(1)} %collective-permute-done.3.third_ref, ...), custom_call_target="tpu_custom_call" | custom-call | flops 10000000 | bytes 1000000 | tf_op jit(solution)/shard_map/pallas_call | solution.py:341
  78.5 0.0 collective-permute-done.4.past_ref
  78.5 8.4 %all-to-all-start.3 = ((f32[4,64,128]{2,1,0:T(8,128)}), f32[4,64,128]{2,1,0:T(8,128)S(1)}, u32[]{:S(2)}, u32[]{:S(2)}) async-start(f32[4,64,128]{2,1,0:T(8,128)} %shard_map.137), calls=%async_computation.3 | async-start | bytes 262144 | tf_op jit(solution)/shard_map/all_to_all | solution.py:346
  86.8 3.0 %shard_map.138.attn_ref = bf16[4,256,256]{2,1,0:T(8,128)(2,1)S(1)} custom-call(bf16[4,272,512]{2,1,0:T(8,128)(2,1)S(1)} %all-to-all-done.here_ref, bf16[4,272,384]{2,1,0:T(8,128)(2,1)S(1)} %collective-permute-done.4.past_ref), custom_call_target="tpu_custom_call" | custom-call | flops 8000000000 | bytes 1000000 | tf_op jit(solution)/shard_map/pallas_call | solution.py:345
  89.9 0.5 all-to-all-done.3.parts_ref
  90.3 1.5 %shard_map.139 = bf16[4,512,256]{2,1,0:T(8,128)(2,1)} custom-call(f32[4,64,128]{2,1,0:T(8,128)S(1)} %all-to-all-done.3.parts_ref, f32[3,128,384]{2,1,0:T(8,128)S(1)} %get-tuple-element.33.before_ref, bf16[4,256,256]{2,1,0:T(8,128)(2,1)S(1)} %shard_map.138.attn_ref), custom_call_target="tpu_custom_call" | custom-call | flops 10000000 | bytes 1000000 | tf_op jit(solution)/shard_map/pallas_call | solution.py:347
  91.8 3.6 %all-to-all-start.4 = ((bf16[4,512,256]{2,1,0:T(8,128)(2,1)}), bf16[4,512,256]{2,1,0:T(8,128)(2,1)S(1)}, u32[]{:S(2)}, u32[]{:S(2)}) async-start(bf16[4,512,256]{2,1,0:T(8,128)(2,1)} %shard_map.139), calls=%async_computation.4 | async-start | bytes 2097152 | tf_op jit(solution)/shard_map/all_to_all | solution.py:350
  95.5 1.4 %copy-done.7 = f32[4,256,384]{2,1,0:T(8,128)S(1)} copy-done((f32[4,256,384]{2,1,0:T(8,128)S(1)}, f32[4,256,384]{2,1,0:T(8,128)}, u32[]{:S(2)}) %copy-start.7) | copy-done | bytes 1572888
  96.9 1.2 %copy-done.9 = f32[4,256,256]{2,1,0:T(8,128)S(1)} copy-done((f32[4,256,256]{2,1,0:T(8,128)S(1)}, f32[4,256,256]{2,1,0:T(8,128)}, u32[]{:S(2)}) %copy-start.9) | copy-done | bytes 1048600
  98.1 1.0 shard_map.132
  99.1 0.0 copy-start
  99.1 0.8 copy-done
  99.9 7.5 %all-to-all-done.4.state_ref = bf16[4,512,256]{2,1,0:T(8,128)(2,1)S(1)} async-done(((bf16[4,512,256]{2,1,0:T(8,128)(2,1)}), bf16[4,512,256]{2,1,0:T(8,128)(2,1)S(1)}, u32[]{:S(2)}, u32[]{:S(2)}) %all-to-all-start.4) | async-done | bytes 1048608 | tf_op jit(solution)/shard_map/all_to_all | solution.py:350
  107.4 1.0 copy-done.1
  108.4 1.3 %shard_map.140 = (f32[4,256,256]{2,1,0:T(8,128)S(1)}, f32[64,256]{1,0:T(8,128)}) custom-call(f32[4,256,128]{2,1,0:T(8,128)S(1)} %copy-done.1, f32[4,256,256]{2,1,0:T(8,128)S(1)} %get-tuple-element.24.local_ref, bf16[4,512,256]{2,1,0:T(8,128)(2,1)S(1)} %all-to-all-done.4.state_ref), custom_call_target="tpu_custom_call" | custom-call | flops 10000000 | bytes 1000000 | tf_op jit(solution)/shard_map/pallas_call | solution.py:351
  109.7 4.6 %all-to-all-start.5 = ((f32[8,8,256]{2,1,0:T(8,128)}), f32[8,8,256]{2,1,0:T(8,128)S(1)}, u32[]{:S(2)}, u32[]{:S(2)}) async-start(f32[8,8,256]{2,1,0:T(8,128)} %bitcast.10), calls=%async_computation.5 | async-start | bytes 131072 | tf_op jit(solution)/shard_map/all_to_all | solution.py:354
  114.4 1.2 copy.21
  115.6 4.4 %all-to-all-done.5 = f32[8,8,256]{2,1,0:T(8,128)S(1)} async-done(((f32[8,8,256]{2,1,0:T(8,128)}), f32[8,8,256]{2,1,0:T(8,128)S(1)}, u32[]{:S(2)}, u32[]{:S(2)}) %all-to-all-start.5) | async-done | bytes 65568 | tf_op jit(solution)/shard_map/all_to_all | solution.py:354
  119.9 0.2 shard_map.141
  120.2 1.2 copy.20
  (26 shorter events, 0.1 us)
Async XLA Ops:
  0.6 1.8 %copy-start.13 = (bf16[256,4,128]{2,1,0:T(4,128)(2,1)S(1)}, bf16[256,4,128]{2,1,0:T(4,128)(2,1)}, u32[]{:S(2)}) copy-start(bf16[256,4,128]{2,1,0:T(4,128)(2,1)} %param.19) | copy-start | bytes 786436
  0.6 1.8 %copy-start.14 = (bf16[256,4,128]{2,1,0:T(4,128)(2,1)S(1)}, bf16[256,4,128]{2,1,0:T(4,128)(2,1)}, u32[]{:S(2)}) copy-start(bf16[256,4,128]{2,1,0:T(4,128)(2,1)} %param.20) | copy-start | bytes 786436
  0.7 1.9 %copy-start.3 = (s32[256]{0:T(256)S(1)}, s32[256]{0:T(256)}, u32[]{:S(2)}) copy-start(s32[256]{0:T(256)} %param.22) | copy-start | bytes 3076
  3.7 4.4 %copy-start.15 = (bf16[256,4,128]{2,1,0:T(4,128)(2,1)S(1)}, bf16[256,4,128]{2,1,0:T(4,128)(2,1)}, u32[]{:S(2)}) copy-start(bf16[256,4,128]{2,1,0:T(4,128)(2,1)} %param.13) | copy-start | bytes 786436
  3.7 4.4 %copy-start.16 = (bf16[256,4,128]{2,1,0:T(4,128)(2,1)S(1)}, bf16[256,4,128]{2,1,0:T(4,128)(2,1)}, u32[]{:S(2)}) copy-start(bf16[256,4,128]{2,1,0:T(4,128)(2,1)} %param.12) | copy-start | bytes 786436
  3.7 5.2 %copy-start.12 = (bf16[256,4,256]{2,1,0:T(4,128)(2,1)S(1)}, bf16[256,4,256]{2,1,0:T(4,128)(2,1)}, u32[]{:S(2)}) copy-start(bf16[256,4,256]{2,1,0:T(4,128)(2,1)} %param.14) | copy-start | bytes 1572868
  3.7 20.2 %all-to-all-start = ((bf16[4,272,512]{2,1,0:T(8,128)(2,1)}), bf16[4,272,512]{2,1,0:T(8,128)(2,1)S(1)}, u32[]{:S(2)}, u32[]{:S(2)}) async-start(bf16[4,272,512]{2,1,0:T(8,128)(2,1)} %shard_map.133), calls=%async_computation | async-start | bytes 2228224 | tf_op jit(solution)/shard_map/all_to_all | solution.py:300
  8.2 0.8 copy-start.4
  8.2 0.8 copy-start.5
  16.5 1.2 copy-start.6
  17.7 1.0 copy-start.8
  18.7 0.8 copy-start.10
  40.3 14.0 %all-to-all-start.2 = ((f32[4,192,128]{2,1,0:T(8,128)}), f32[4,192,128]{2,1,0:T(8,128)S(1)}, u32[]{:S(2)}, u32[]{:S(2)}) async-start(f32[4,192,128]{2,1,0:T(8,128)} %get-tuple-element.27), calls=%async_computation.2 | async-start | bytes 786432 | tf_op jit(solution)/shard_map/all_to_all | solution.py:330
  45.6 32.8 %collective-permute-start.4 = (bf16[4,272,384]{2,1,0:T(8,128)(2,1)}, bf16[4,272,384]{2,1,0:T(8,128)(2,1)S(1)}, u32[]{:S(2)}, u32[]{:S(2)}) collective-permute-start(bf16[4,272,384]{2,1,0:T(8,128)(2,1)} %slice.8), channel_id=1, source_target_pairs={{0,32},{32,64},{64,96},{96,128},{128,160},{160,192},{192,224},{224... | collective-permute-start | bytes 2506760 | tf_op jit(solution)/shard_map/ppermute | solution.py:322
  55.1 22.0 %collective-permute-start.3 = (f32[192,128]{1,0:T(8,128)S(1)}, f32[192,128]{1,0:T(8,128)S(1)}, u32[]{:S(2)}, u32[]{:S(2)}) collective-permute-start(f32[192,128]{1,0:T(8,128)S(1)} %get-tuple-element.29.map_ref), channel_id=1, source_target_pairs={{256,384},{257,385},{258,386},{259,387},{260,388},{261,389},{262,3... | collective-permute-start | bytes 294920 | tf_op jit(solution)/shard_map/ppermute | solution.py:336
  56.4 0.7 collective-permute-start
  57.4 2.0 %collective-permute-start.1 = (f32[64,128]{1,0:T(8,128)S(1)}, f32[64,128]{1,0:T(8,128)S(1)}, u32[]{:S(2)}, u32[]{:S(2)}) collective-permute-start(f32[64,128]{1,0:T(8,128)S(1)} %shard_map.136), channel_id=1, source_target_pairs={{128,256},{129,257},{130,258},{131,259},{132,260},{133,261},{134,2... | collective-permute-start | bytes 98312 | tf_op jit(solution)/shard_map/ppermute | solution.py:338
  58.0 19.1 %collective-permute-start.2 = (f32[64,128]{1,0:T(8,128)S(1)}, f32[64,128]{1,0:T(8,128)S(1)}, u32[]{:S(2)}, u32[]{:S(2)}) collective-permute-start(f32[64,128]{1,0:T(8,128)S(1)} %shard_map.136), channel_id=1, source_target_pairs={{128,384},{129,385},{130,386},{131,387},{132,388},{133,389},{134,3... | collective-permute-start | bytes 98312 | tf_op jit(solution)/shard_map/ppermute | solution.py:339
  78.5 11.9 %all-to-all-start.3 = ((f32[4,64,128]{2,1,0:T(8,128)}), f32[4,64,128]{2,1,0:T(8,128)S(1)}, u32[]{:S(2)}, u32[]{:S(2)}) async-start(f32[4,64,128]{2,1,0:T(8,128)} %shard_map.137), calls=%async_computation.3 | async-start | bytes 262144 | tf_op jit(solution)/shard_map/all_to_all | solution.py:346
  91.8 3.7 %copy-start.11 = (f32[4,256,128]{2,1,0:T(8,128)S(1)}, f32[4,256,128]{2,1,0:T(8,128)}, u32[]{:S(2)}) copy-start(f32[4,256,128]{2,1,0:T(8,128)} %copy-done.10) | copy-start | bytes 1572868
  91.8 15.6 %all-to-all-start.4 = ((bf16[4,512,256]{2,1,0:T(8,128)(2,1)}), bf16[4,512,256]{2,1,0:T(8,128)(2,1)S(1)}, u32[]{:S(2)}, u32[]{:S(2)}) async-start(bf16[4,512,256]{2,1,0:T(8,128)(2,1)} %shard_map.139), calls=%async_computation.4 | async-start | bytes 2097152 | tf_op jit(solution)/shard_map/all_to_all | solution.py:350
  95.5 1.4 %copy-start.7 = (f32[4,256,384]{2,1,0:T(8,128)S(1)}, f32[4,256,384]{2,1,0:T(8,128)}, u32[]{:S(2)}) copy-start(f32[4,256,384]{2,1,0:T(8,128)} %copy-done.6) | copy-start | bytes 4718596
  96.9 1.2 %copy-start.9 = (f32[4,256,256]{2,1,0:T(8,128)S(1)}, f32[4,256,256]{2,1,0:T(8,128)}, u32[]{:S(2)}) copy-start(f32[4,256,256]{2,1,0:T(8,128)} %copy-done.8) | copy-start | bytes 3145732
  99.1 0.8 copy-start
  107.4 1.0 copy-start.1
  109.7 10.2 %copy-start.2 = (f32[4,256]{1,0:T(4,128)S(1)}, f32[4,256]{1,0:T(4,128)}, u32[]{:S(2)}) copy-start(f32[4,256]{1,0:T(4,128)} %gain_ref.1) | copy-start | bytes 12292
  109.7 10.2 %all-to-all-start.5 = ((f32[8,8,256]{2,1,0:T(8,128)}), f32[8,8,256]{2,1,0:T(8,128)S(1)}, u32[]{:S(2)}, u32[]{:S(2)}) async-start(f32[8,8,256]{2,1,0:T(8,128)} %bitcast.10), calls=%async_computation.5 | async-start | bytes 131072 | tf_op jit(solution)/shard_map/all_to_all | solution.py:354

commit v3 on v2

--- a/solution.py
+++ b/solution.py
@@ -13,7 +13,6 @@
 WINDOW = 2048
 PART = VD // 4
 MARK_ROWS = 16
-VMEM_BYTES = 48 * 2**20
 
 SEQ = ("zh", "zl", "x")
 f32 = jnp.float32
@@ -40,7 +39,7 @@
     return dot(ah, b) + dot(al, b)
 
 
-def call(body, out_shape, scalars=0, inputs=1, scratch=(), flops=1e7):
+def call(body, out_shape, scalars=0, inputs=1, scratch=(), flops=1e7, mib=8):
     whole = pl.BlockSpec(memory_space=pltpu.VMEM)
     small = pl.BlockSpec(memory_space=pltpu.SMEM)
     return pl.pallas_call(
@@ -50,7 +49,7 @@
         out_shape=out_shape,
         scratch_shapes=list(scratch),
         cost_estimate=pl.CostEstimate(flops=int(flops), bytes_accessed=10**6, transcendentals=0),
-        compiler_params=pltpu.CompilerParams(vmem_limit_bytes=VMEM_BYTES),
+        compiler_params=pltpu.CompilerParams(vmem_limit_bytes=mib * 2**20),
     )
 
 
@@ -216,7 +215,7 @@
         out_ref[h] = (raw_ref[h] * factor * gain_ref[h : h + 1, :]).astype(bf16)
 
 
-def pack_blocks(count_ref, key_ref, value_ref, query_ref, position_ref, out_ref):
+def pack_keys(count_ref, key_ref, value_ref, position_ref, out_ref):
     lane = lax.broadcasted_iota(jnp.int32, (1, ROWS), 1)
     marks = jnp.where(lane < count_ref[0], position_ref[...] + 1, 0)
     spot = lax.broadcasted_iota(jnp.int32, (MARK_ROWS, ROWS), 0)
@@ -224,32 +223,48 @@
     coded = coded.astype(f32).astype(bf16)
     for h in range(HEADS):
         out_ref[h, :ROWS, :KD] = key_ref[h]
-        out_ref[h, :ROWS, KD : KD + VD] = value_ref[h]
-        out_ref[h, :ROWS, KD + VD :] = query_ref[h]
+        out_ref[h, :ROWS, KD:] = value_ref[h]
         out_ref[h, ROWS:, :ROWS] = coded
-        out_ref[h, ROWS:, ROWS:] = jnp.zeros((MARK_ROWS, 2 * KD + VD - ROWS), bf16)
-
-
-def attend(here_ref, past_ref, out_ref):
+        out_ref[h, ROWS:, ROWS:] = jnp.zeros((MARK_ROWS, KD + VD - ROWS), bf16)
+
+
+def pack_heads(place_ref, query_ref, keys_ref, past_ref, *out_refs):
+    for d, out_ref in enumerate(out_refs):
+        h = lax.rem(place_ref[0] + d, 4)
+        out_ref[:, : KD + VD] = keys_ref[pl.ds(h, 1)][0]
+        out_ref[:ROWS, KD + VD : 2 * KD + VD] = query_ref[pl.ds(h, 1)][0]
+        out_ref[ROWS:, KD + VD : 2 * KD + VD] = jnp.zeros((MARK_ROWS, KD), bf16)
+        out_ref[:, 2 * KD + VD :] = past_ref[pl.ds(h, 1)][0]
+
+
+def attend(place_ref, own_ref, one_ref, two_ref, three_ref, out_ref):
+    here = place_ref[0]
     row = lax.broadcasted_iota(jnp.int32, (ROWS, ROWS), 0)
     col = lax.broadcasted_iota(jnp.int32, (ROWS, ROWS), 1)
-
-    def marks_of(ref, j):
-        coded = ref[j, ROWS : ROWS + MARK_ROWS, :ROWS].astype(f32)
-        return coded[0:1, :] * 256.0 + coded[1:2, :]
-
-    marks = [marks_of(here_ref, j) for j in range(4)]
-    here_marks = [jnp.where(m > 0.0, m, 1e9) for m in marks]
-    past_marks = [marks_of(past_ref, j) for j in range(4)]
-    past_marks = [jnp.where(m > 0.0, m, 1e9) for m in past_marks]
+    blocks = (own_ref, one_ref, two_ref, three_ref)
+    before = 2 * KD + VD
+
+    def marks_of(ref, start):
+        coded = ref[ROWS : ROWS + MARK_ROWS, start : start + ROWS].astype(f32)
+        marks = coded[0:1, :] * 256.0 + coded[1:2, :]
+        return marks, jnp.where(marks > 0.0, marks, 1e9)
+
+    marks = [marks_of(ref, 0) for ref in blocks]
+    past_marks = [marks_of(ref, before) for ref in blocks]
+    spots = [lax.rem(here - j + 4, 4) for j in range(4)]
     for j in range(4):
-        query_marks = jnp.sum(jnp.where(row == col, marks[j], 0.0), axis=1, keepdims=True)
-        q = here_ref[j, :ROWS, KD + VD :]
-        sources = [(here_ref, i, here_marks[i]) for i in range(j + 1)]
-        sources += [(past_ref, i, past_marks[i]) for i in range(j, 4)]
+        query_marks = jnp.sum(jnp.where(row == col, marks[j][0], 0.0), axis=1, keepdims=True)
+        q = blocks[j][:ROWS, KD + VD : before]
+        both = (blocks[j][:ROWS, : KD + VD], blocks[j][:ROWS, before:])
+        sources = [(both[0], marks[j][1]), (both[1], past_marks[j][1])]
+        for i in range(4):
+            if i != j:
+                same = spots[i] < spots[j]
+                keys = jnp.where(same, blocks[i][:ROWS, : KD + VD], blocks[i][:ROWS, before:])
+                sources.append((keys, jnp.where(same, marks[i][1], past_marks[i][1])))
         scores = []
-        for ref, i, key_marks in sources:
-            score = dot(q, ref[i, :ROWS, :KD], ((1,), (1,))) * KD**-0.5
+        for keys, key_marks in sources:
+            score = dot(q, keys[:, :KD], ((1,), (1,))) * KD**-0.5
             allowed = (key_marks <= query_marks) & (key_marks > query_marks - float(WINDOW))
             scores.append(jnp.where(allowed, score, -1e30))
         top = scores[0]
@@ -258,12 +273,12 @@
         top = jnp.max(top, axis=1, keepdims=True)
         weight_sum = jnp.zeros((ROWS, ROWS), f32)
         mixed = jnp.zeros((ROWS, VD), f32)
-        for score, (ref, i, key_marks) in zip(scores, sources):
+        for score, (keys, key_marks) in zip(scores, sources):
             weights = jnp.exp(score - top)
             weight_sum = weight_sum + weights
-            mixed = mixed + dot(weights.astype(bf16), ref[i, :ROWS, KD : KD + VD])
+            mixed = mixed + dot(weights.astype(bf16), keys[:, KD:])
         mixed = mixed / jnp.sum(weight_sum, axis=1, keepdims=True)
-        out_ref[j] = jnp.where(query_marks > 0.0, mixed, 0.0).astype(bf16)
+        out_ref[pl.ds(spots[j], 1)] = jnp.where(query_marks > 0.0, mixed, 0.0).astype(bf16)[None]
 
 
 def heads_first(block):
@@ -288,16 +303,6 @@
     attn_position,
     attn_count,
 ):
-    packed = call(
-        pack_blocks, shape_of(HEADS, ROWS + MARK_ROWS, 2 * KD + VD, kind=bf16), scalars=1, inputs=4
-    )(
-        attn_count,
-        heads_first(attn_key),
-        heads_first(attn_value),
-        heads_first(attn_query),
-        attn_position.reshape(1, ROWS),
-    )
-    here = lax.all_to_all(packed, "x", 0, 0, tiled=True)
     maps, new, mixing, straight = call(
         block_terms,
         (
@@ -310,6 +315,7 @@
         inputs=5,
         scratch=[pltpu.VMEM((HEADS, ROWS, ROWS), f32)] * 2,
         flops=8e9,
+        mib=16,
     )(
         delta_count,
         heads_first(delta_query),
@@ -318,15 +324,30 @@
         delta_gate.T,
         delta_beta.T,
     )
-    maps, here, past = lax.optimization_barrier((maps, here, here[:, :, : KD + VD]))
-    past = lax.ppermute(past, ("zh", "zl"), [(i, i + 1) for i in range(15)])
+    maps, attn_key, attn_value, attn_query = lax.optimization_barrier(
+        (maps, attn_key, attn_value, attn_query)
+    )
     exchanged = lax.all_to_all(maps, "x", 0, 0, tiled=True)
+    keys = call(
+        pack_keys, shape_of(HEADS, ROWS + MARK_ROWS, KD + VD, kind=bf16), scalars=1, inputs=3
+    )(attn_count, heads_first(attn_key), heads_first(attn_value), attn_position.reshape(1, ROWS))
+    past = lax.ppermute(keys, ("zh", "zl"), [(i, i + 1) for i in range(15)])
+    spot = lax.axis_index("x").astype(jnp.int32).reshape(1)
     carry, local = call(
         row_terms, (shape_of(HEADS, ROWS, KD), shape_of(HEADS, ROWS, VD)), inputs=3, flops=2e9
     )(new, mixing, straight)
     plane_prefix, plane_total = call(
         compose_plane, (shape_of(3, KD, KD + VD), shape_of(4, KD + PART, KD))
     )(exchanged)
+    _, past = lax.optimization_barrier((plane_total, past))
+    width = 3 * KD + 2 * VD
+    blocks = call(
+        pack_heads, (shape_of(ROWS + MARK_ROWS, width, kind=bf16),) * 4, scalars=1, inputs=3
+    )(spot, heads_first(attn_query), keys, past)
+    blocks = [
+        lax.ppermute(block, "x", [(i, (i + d) % 4) for i in range(4)]) if d else block
+        for d, block in enumerate(blocks)
+    ]
     gathered = lax.all_to_all(plane_total, "zl", 0, 0, tiled=True)
     group_prefix, group_total, group_offset = call(
         compose_group,
@@ -335,14 +356,17 @@
     first = lax.ppermute(group_offset, "zh", [(0, 1)])
     third = lax.ppermute(group_total, "zh", [(2, 3)])
     pair = call(step_state, shape_of(PART, KD), inputs=2)(group_total, first)
+    pair, third = lax.optimization_barrier((pair, third))
     one = lax.ppermute(pair, "zh", [(1, 2)])
     two = lax.ppermute(pair, "zh", [(1, 3)])
     place = lax.axis_index("zh").astype(jnp.int32).reshape(1)
     planes = call(group_states, shape_of(4, PART, KD), scalars=1, inputs=5)(
         place, first, one, two, third, group_prefix
     )
-    planes, past = lax.optimization_barrier((planes, past))
-    attn_heads = call(attend, shape_of(4, ROWS, VD, kind=bf16), inputs=2, flops=8e9)(here, past)
+    planes, *blocks = lax.optimization_barrier((planes, *blocks))
+    attn_heads = call(
+        attend, shape_of(4, ROWS, VD, kind=bf16), scalars=1, inputs=4, flops=8e9, mib=16
+    )(spot, *blocks)
     parts = lax.all_to_all(planes, "zl", 0, 0, tiled=True)
     returned = call(plane_states, shape_of(4, 2 * KD + ROWS, VD, kind=bf16), inputs=3)(
         parts, plane_prefix, attn_heads

time: 123 us -> 126 us (1.024)
  blocking collectives: 13.8 us -> 0 us
  starting transfers between devices: 31.5 us -> 42.6 us
  waiting for transfers between devices: 42 us -> 46.3 us
  Pallas kernels: 19.6 us -> 21.8 us
    all_to_all x1 -> x0, blocking collectives: 13.8 us -> none  [shards(): exchanged = lax.all_to_all(maps, 'x', 0, 0, tiled=True)]
    ppermute x1 -> x4, starting transfers between devices: 1.28 us -> 13.1 us  [the longest x3 11.8 us: shards(): lax.ppermute(block, 'x', [(i, (i + d) % 4) for i in range(4)])]
    ppermute x1, waiting for transfers between devices: 0.01 us -> 8.13 us  [shards(): third = lax.ppermute(group_total, 'zh', [(2, 3)])]
    all_to_all x1, waiting for transfers between devices: 7.4 us -> 0.01 us  [shards(): gathered = lax.all_to_all(plane_total, 'zl', 0, 0, tiled=True)]
    all_to_all x1, waiting for transfers between devices: 4.44 us -> 10.1 us  [shards(): exchanged = lax.all_to_all(maps, 'x', 0, 0, tiled=True)]
    ppermute x1, waiting for transfers between devices: 17.8 us -> 12.5 us  [shards(): two = lax.ppermute(pair, 'zh', [(1, 3)])]
    ppermute x1 -> x4, waiting for transfers between devices: 0.01 us -> 4.69 us  [the longest x1 4.68 us: shards(): past = lax.ppermute(keys, ('zh', 'zl'), [(i, i + 1) for i in range(15)])]
    pallas_call x2 -> x3, Pallas kernels: 4.17 us -> 5.55 us  [the longest x1 4.23 us: shards(): call(attend, shape_of(4, ROWS, VD, kind=bf16), scalars=1, inputs=4, flops...]
  transfers between devices with their start and end apart: 10 -> 13, of which waited for: 6 -> 6; matrix products, arithmetic and copies ran while one was open for 1% -> 1% of each run, Pallas kernels for 11% -> 8%
where the time goes in v3:
time: 126 us; the launch traced here: 125 us
  waiting for transfers between devices  46.3 us (37%)
  starting transfers between devices  42.6 us (34%)
  Pallas kernels  21.8 us (17%)
  local copies, waits for them, and re-layouts  12.3 us (10%)
  between operations  2.23 us (2%)
    ppermute x1, waiting for transfers between devices, shards(): two = lax.ppermute(pair, 'zh', [(1, 3)])  12.5 us
    ppermute x3, starting transfers between devices, shards(): lax.ppermute(block, 'x', [(i, (i + d) % 4) for i in range(4)])  11.8 us
    unnamed x33, local copies, waits for them, and re-layouts  11 us
    all_to_all x1, waiting for transfers between devices, shards(): exchanged = lax.all_to_all(maps, 'x', 0, 0, tiled=True)  10.1 us
    pallas_call x1, Pallas kernels, shards(): call(block_terms, (shape_of(HEADS, KD, KD + VD), shape_of(HEADS, ROWS, KD...  8.38 us
    ppermute x1, waiting for transfers between devices, shards(): third = lax.ppermute(group_total, 'zh', [(2, 3)])  8.13 us
    all_to_all x1, starting transfers between devices, shards(): parts = lax.all_to_all(planes, 'zl', 0, 0, tiled=True)  7.58 us
    all_to_all x1, waiting for transfers between devices, shards(): states = lax.all_to_all(returned, 'x', 0, 0, tiled=True)  6.43 us
  transfers between devices with their start and end apart: 13, of which 6 were waited for; matrix products, arithmetic and copies ran while one was open for 1% of the time, Pallas kernels for 8%

profile of v3, /device:TPU:480, one launch (start us, length us, event | category | flops | bytes accessed | tf_op | source)
XLA Modules:
  0.0 125.2 jit_solution(2353526373473269894)
XLA Ops:
  1.3 1.1 copy.29
  2.4 1.1 copy_bitcast_fusion.4
  3.6 8.4 %shard_map.131 = (f32[4,128,384]{2,1,0:T(8,128)}, f32[4,256,384]{2,1,0:T(8,128)S(1)}, f32[4,256,256]{2,1,0:T(8,128)S(1)}, f32[4,256,128]{2,1,0:T(8,128)S(1)}) custom-call(s32[1]{0:T(128)S(6)} %copy.32.count_ref, bf16[4,256,128]{2,1,0:T(8,128)(2,1)S(1)} %get-tuple-element.63.q_ref, bf16[4,256,128]{2,1,0:T(8,128)(2,1)S(1)} %get-tuple-element.62.k_ref, ...), custom_call_target="tpu_custom_call" | custom-call | flops 8000000000 | bytes 1000000 | tf_op jit(solution)/shard_map/pallas_call | solution.py:306
  11.9 1.2 copy-done.6
  13.1 1.0 copy-done.8
  14.1 0.8 copy-done.10
  14.9 4.4 %all-to-all-start = ((f32[4,128,384]{2,1,0:T(8,128)}), f32[4,128,384]{2,1,0:T(8,128)S(1)}, u32[]{:S(2)}, u32[]{:S(2)}) async-start(f32[4,128,384]{2,1,0:T(8,128)} %get-tuple-element.37), calls=%async_computation | async-start | bytes 1572864 | tf_op jit(solution)/shard_map/all_to_all | solution.py:330
  20.0 0.1 copy.28
  20.1 0.0 copy-start.14
  20.1 0.1 shard_map.137.keys_ref
  20.2 1.3 %collective-permute-start.4 = (bf16[4,272,384]{2,1,0:T(8,128)(2,1)S(1)}, bf16[4,272,384]{2,1,0:T(8,128)(2,1)S(1)}, u32[]{:S(2)}, u32[]{:S(2)}) collective-permute-start(bf16[4,272,384]{2,1,0:T(8,128)(2,1)S(1)} %shard_map.137.keys_ref), channel_id=1, source_target_pairs={{0,32},{32,64},{64,96},{96,128},{128,160},{160,192},{192,224},{224... | collective-permute-start | bytes 2506760 | tf_op jit(solution)/shard_map/ppermute | solution.py:334
  21.5 10.1 %all-to-all-done.maps_ref = f32[4,128,384]{2,1,0:T(8,128)S(1)} async-done(((f32[4,128,384]{2,1,0:T(8,128)}), f32[4,128,384]{2,1,0:T(8,128)S(1)}, u32[]{:S(2)}, u32[]{:S(2)}) %all-to-all-start) | async-done | bytes 786464 | tf_op jit(solution)/shard_map/all_to_all | solution.py:330
  31.6 1.6 %shard_map.133 = (f32[3,128,384]{2,1,0:T(8,128)S(1)}, f32[4,192,128]{2,1,0:T(8,128)}) custom-call(f32[4,128,384]{2,1,0:T(8,128)S(1)} %all-to-all-done.maps_ref), custom_call_target="tpu_custom_call" | custom-call | flops 10000000 | bytes 1000000 | tf_op jit(solution)/shard_map/pallas_call | solution.py:339
  33.2 5.3 %all-to-all-start.1 = ((f32[4,192,128]{2,1,0:T(8,128)}), f32[4,192,128]{2,1,0:T(8,128)S(1)}, u32[]{:S(2)}, u32[]{:S(2)}) async-start(f32[4,192,128]{2,1,0:T(8,128)} %get-tuple-element.38), calls=%async_computation.1 | async-start | bytes 786432 | tf_op jit(solution)/shard_map/all_to_all | solution.py:351
  38.6 4.7 %collective-permute-done.4.past_ref = bf16[4,272,384]{2,1,0:T(8,128)(2,1)S(1)} collective-permute-done((bf16[4,272,384]{2,1,0:T(8,128)(2,1)S(1)}, bf16[4,272,384]{2,1,0:T(8,128)(2,1)S(1)}, u32[]{:S(2)}, u32[]{:S(2)}) %collective-permute-start.4) | collective-permute-done | bytes 835616 | tf_op jit(solution)/shard_map/ppermute | solution.py:334
  43.2 1.2 shard_map.138
  44.5 3.9 %collective-permute-start.5 = (bf16[272,896]{1,0:T(8,128)(2,1)}, bf16[272,896]{1,0:T(8,128)(2,1)S(1)}, u32[]{:S(2)}, u32[]{:S(2)}) collective-permute-start(bf16[272,896]{1,0:T(8,128)(2,1)} %get-tuple-element.49), channel_id=1, source_target_pairs={{0,8},{8,16},{16,24},{24,0},{1,9},{9,17},{17,25},{25,1},{2,10},{10... | collective-permute-start | bytes 1462280 | tf_op jit(solution)/shard_map/ppermute | solution.py:348
  48.4 4.6 %collective-permute-start.6 = (bf16[272,896]{1,0:T(8,128)(2,1)}, bf16[272,896]{1,0:T(8,128)(2,1)S(1)}, u32[]{:S(2)}, u32[]{:S(2)}) collective-permute-start(bf16[272,896]{1,0:T(8,128)(2,1)} %get-tuple-element.50), channel_id=1, source_target_pairs={{0,16},{8,24},{16,0},{24,8},{1,17},{9,25},{17,1},{25,9},{2,18},{10... | collective-permute-start | bytes 1462280 | tf_op jit(solution)/shard_map/ppermute | solution.py:348
  52.9 3.4 %collective-permute-start.7 = (bf16[272,896]{1,0:T(8,128)(2,1)}, bf16[272,896]{1,0:T(8,128)(2,1)}, u32[]{:S(2)}, u32[]{:S(2)}) collective-permute-start(bf16[272,896]{1,0:T(8,128)(2,1)} %get-tuple-element.51), channel_id=1, source_target_pairs={{0,24},{8,0},{16,8},{24,16},{1,25},{9,1},{17,9},{25,17},{2,26},{10... | collective-permute-start | bytes 1462280 | tf_op jit(solution)/shard_map/ppermute | solution.py:348
  56.3 0.8 shard_map.134
  57.1 1.3 %collective-permute-start.1 = (f32[192,128]{1,0:T(8,128)S(1)}, f32[192,128]{1,0:T(8,128)S(1)}, u32[]{:S(2)}, u32[]{:S(2)}) collective-permute-start(f32[192,128]{1,0:T(8,128)S(1)} %get-tuple-element.40.map_ref), channel_id=1, source_target_pairs={{256,384},{257,385},{258,386},{259,387},{260,388},{261,389},{262,3... | collective-permute-start | bytes 294920 | tf_op jit(solution)/shard_map/ppermute | solution.py:357
  58.4 0.7 collective-permute-start
  59.1 0.0 collective-permute-done.earlier_ref.first_ref
  59.1 0.3 shard_map.135
  59.4 8.1 %collective-permute-done.1.third_ref = f32[192,128]{1,0:T(8,128)S(1)} collective-permute-done((f32[192,128]{1,0:T(8,128)S(1)}, f32[192,128]{1,0:T(8,128)S(1)}, u32[]{:S(2)}, u32[]{:S(2)}) %collective-permute-start.1) | collective-permute-done | bytes 98336 | tf_op jit(solution)/shard_map/ppermute | solution.py:357
  67.5 1.3 %collective-permute-start.3 = (f32[64,128]{1,0:T(8,128)S(1)}, f32[64,128]{1,0:T(8,128)S(1)}, u32[]{:S(2)}, u32[]{:S(2)}) collective-permute-start(f32[64,128]{1,0:T(8,128)S(1)} %shard_map.135), channel_id=1, source_target_pairs={{128,384},{129,385},{130,386},{131,387},{132,388},{133,389},{134,3... | collective-permute-start | bytes 98312 | tf_op jit(solution)/shard_map/ppermute | solution.py:361
  68.8 0.7 collective-permute-start.2
  69.5 12.5 %collective-permute-done.3.two_ref = f32[64,128]{1,0:T(8,128)S(1)} collective-permute-done((f32[64,128]{1,0:T(8,128)S(1)}, f32[64,128]{1,0:T(8,128)S(1)}, u32[]{:S(2)}, u32[]{:S(2)}) %collective-permute-start.3) | collective-permute-done | bytes 32800 | tf_op jit(solution)/shard_map/ppermute | solution.py:361
  82.0 0.0 collective-permute-done.2.one_ref
  82.0 1.3 %shard_map.136 = f32[4,64,128]{2,1,0:T(8,128)} custom-call(s32[1]{0:T(128)} %bitcast.5.place_ref, f32[64,128]{1,0:T(8,128)S(1)} %collective-permute-done.earlier_ref.first_ref, f32[64,128]{1,0:T(8,128)S(1)} %collective-permute-done.2.one_ref, f32[64,128]{1,0:T(8,128)S(1)} %collective-permute-done.3.two_ref, f32[192,128]{1,0:T(8,128)S(1)} %collective-permute-done.1.third_ref, ...), custom_call_target="tpu_custom_call" | custom-call | flops 10000000 | bytes 1000000 | tf_op jit(solution)/shard_map/pallas_call | solution.py:363
  83.4 0.0 collective-permute-done.7.three_ref
  83.4 7.6 %all-to-all-start.2 = ((f32[4,64,128]{2,1,0:T(8,128)}), f32[4,64,128]{2,1,0:T(8,128)S(1)}, u32[]{:S(2)}, u32[]{:S(2)}) async-start(f32[4,64,128]{2,1,0:T(8,128)} %shard_map.136), calls=%async_computation.2 | async-start | bytes 262144 | tf_op jit(solution)/shard_map/all_to_all | solution.py:370
  91.0 4.2 %shard_map.139.attn_ref = bf16[4,256,256]{2,1,0:T(8,128)(2,1)S(1)} custom-call(s32[1]{0:T(128)} %bitcast.6.place_ref, bf16[272,896]{1,0:T(8,128)(2,1)S(1)} %get-tuple-element.54.own_ref, bf16[272,896]{1,0:T(8,128)(2,1)S(1)} %collective-permute-done.5.one_ref, bf16[272,896]{1,0:T(8,128)(2,1)S(1)} %collective-permute-done.6.two_ref, ...), custom_call_target="tpu_custom_call" | custom-call | flops 8000000000 | bytes 1000000 | tf_op jit(solution)/shard_map/pallas_call | solution.py:367
  95.2 1.4 %shard_map.140 = bf16[4,512,256]{2,1,0:T(8,128)(2,1)} custom-call(f32[4,64,128]{2,1,0:T(8,128)S(1)} %all-to-all-done.2.parts_ref, f32[3,128,384]{2,1,0:T(8,128)S(1)} %get-tuple-element.53.before_ref, bf16[4,256,256]{2,1,0:T(8,128)(2,1)S(1)} %shard_map.139.attn_ref), custom_call_target="tpu_custom_call" | custom-call | flops 10000000 | bytes 1000000 | tf_op jit(solution)/shard_map/pallas_call | solution.py:371
  96.7 3.6 %all-to-all-start.3 = ((bf16[4,512,256]{2,1,0:T(8,128)(2,1)}), bf16[4,512,256]{2,1,0:T(8,128)(2,1)S(1)}, u32[]{:S(2)}, u32[]{:S(2)}) async-start(bf16[4,512,256]{2,1,0:T(8,128)(2,1)} %shard_map.140), calls=%async_computation.3 | async-start | bytes 2097152 | tf_op jit(solution)/shard_map/all_to_all | solution.py:374
  100.3 1.4 %copy-done.7 = f32[4,256,384]{2,1,0:T(8,128)S(1)} copy-done((f32[4,256,384]{2,1,0:T(8,128)S(1)}, f32[4,256,384]{2,1,0:T(8,128)}, u32[]{:S(2)}) %copy-start.7) | copy-done | bytes 1572888
  101.8 1.2 copy-done.9
  103.0 1.0 shard_map.132
  104.0 0.0 copy-start
  104.0 0.8 copy-done
  104.8 6.4 %all-to-all-done.3.state_ref = bf16[4,512,256]{2,1,0:T(8,128)(2,1)S(1)} async-done(((bf16[4,512,256]{2,1,0:T(8,128)(2,1)}), bf16[4,512,256]{2,1,0:T(8,128)(2,1)S(1)}, u32[]{:S(2)}, u32[]{:S(2)}) %all-to-all-start.3) | async-done | bytes 1048608 | tf_op jit(solution)/shard_map/all_to_all | solution.py:374
  111.2 1.0 copy-done.1
  112.2 1.3 %shard_map.141 = (f32[4,256,256]{2,1,0:T(8,128)S(1)}, f32[64,256]{1,0:T(8,128)}) custom-call(f32[4,256,128]{2,1,0:T(8,128)S(1)} %copy-done.1, f32[4,256,256]{2,1,0:T(8,128)S(1)} %get-tuple-element.35.local_ref, bf16[4,512,256]{2,1,0:T(8,128)(2,1)S(1)} %all-to-all-done.3.state_ref), custom_call_target="tpu_custom_call" | custom-call | flops 10000000 | bytes 1000000 | tf_op jit(solution)/shard_map/pallas_call | solution.py:375
  113.5 4.6 %all-to-all-start.4 = ((f32[8,8,256]{2,1,0:T(8,128)}), f32[8,8,256]{2,1,0:T(8,128)S(1)}, u32[]{:S(2)}, u32[]{:S(2)}) async-start(f32[8,8,256]{2,1,0:T(8,128)} %bitcast.11), calls=%async_computation.4 | async-start | bytes 131072 | tf_op jit(solution)/shard_map/all_to_all | solution.py:378
  118.2 1.2 copy.21
  119.4 4.4 %all-to-all-done.4 = f32[8,8,256]{2,1,0:T(8,128)S(1)} async-done(((f32[8,8,256]{2,1,0:T(8,128)}), f32[8,8,256]{2,1,0:T(8,128)S(1)}, u32[]{:S(2)}, u32[]{:S(2)}) %all-to-all-start.4) | async-done | bytes 65568 | tf_op jit(solution)/shard_map/all_to_all | solution.py:378
  123.8 0.2 shard_map.142
  124.0 1.2 copy.20
  (28 shorter events, 0.2 us)
Async XLA Ops:
  0.6 2.9 %copy-start.5 = (f32[256,4]{0,1:T(4,128)S(1)}, f32[256,4]{0,1:T(4,128)}, u32[]{:S(2)}) copy-start(f32[256,4]{0,1:T(4,128)} %param.16) | copy-start | bytes 12292
  0.6 2.9 %copy-start.4 = (f32[256,4]{0,1:T(4,128)S(1)}, f32[256,4]{0,1:T(4,128)}, u32[]{:S(2)}) copy-start(f32[256,4]{0,1:T(4,128)} %param.15) | copy-start | bytes 12292
  11.9 1.2 copy-start.6
  13.1 1.0 copy-start.8
  14.1 0.8 copy-start.10
  14.9 5.1 %copy-start.13 = (bf16[256,4,128]{2,1,0:T(4,128)(2,1)S(1)}, bf16[256,4,128]{2,1,0:T(4,128)(2,1)}, u32[]{:S(2)}) copy-start(bf16[256,4,128]{2,1,0:T(4,128)(2,1)} %param.20) | copy-start | bytes 786436
  14.9 5.1 %copy-start.12 = (bf16[256,4,256]{2,1,0:T(4,128)(2,1)S(1)}, bf16[256,4,256]{2,1,0:T(4,128)(2,1)}, u32[]{:S(2)}) copy-start(bf16[256,4,256]{2,1,0:T(4,128)(2,1)} %param.21) | copy-start | bytes 1572868
  14.9 5.2 %copy-start.3 = (s32[256]{0:T(256)S(1)}, s32[256]{0:T(256)}, u32[]{:S(2)}) copy-start(s32[256]{0:T(256)} %param.22) | copy-start | bytes 3076
  14.9 16.7 %all-to-all-start = ((f32[4,128,384]{2,1,0:T(8,128)}), f32[4,128,384]{2,1,0:T(8,128)S(1)}, u32[]{:S(2)}, u32[]{:S(2)}) async-start(f32[4,128,384]{2,1,0:T(8,128)} %get-tuple-element.37), calls=%async_computation | async-start | bytes 1572864 | tf_op jit(solution)/shard_map/all_to_all | solution.py:330
  20.1 18.4 %copy-start.14 = (bf16[256,4,128]{2,1,0:T(4,128)(2,1)S(1)}, bf16[256,4,128]{2,1,0:T(4,128)(2,1)}, u32[]{:S(2)}) copy-start(bf16[256,4,128]{2,1,0:T(4,128)(2,1)} %param.19) | copy-start | bytes 786436
  20.2 23.0 %collective-permute-start.4 = (bf16[4,272,384]{2,1,0:T(8,128)(2,1)S(1)}, bf16[4,272,384]{2,1,0:T(8,128)(2,1)S(1)}, u32[]{:S(2)}, u32[]{:S(2)}) collective-permute-start(bf16[4,272,384]{2,1,0:T(8,128)(2,1)S(1)} %shard_map.137.keys_ref), channel_id=1, source_target_pairs={{0,32},{32,64},{64,96},{96,128},{128,160},{160,192},{192,224},{224... | collective-permute-start | bytes 2506760 | tf_op jit(solution)/shard_map/ppermute | solution.py:334
  33.2 23.1 %all-to-all-start.1 = ((f32[4,192,128]{2,1,0:T(8,128)}), f32[4,192,128]{2,1,0:T(8,128)S(1)}, u32[]{:S(2)}, u32[]{:S(2)}) async-start(f32[4,192,128]{2,1,0:T(8,128)} %get-tuple-element.38), calls=%async_computation.1 | async-start | bytes 786432 | tf_op jit(solution)/shard_map/all_to_all | solution.py:351
  44.5 38.9 %collective-permute-start.5 = (bf16[272,896]{1,0:T(8,128)(2,1)}, bf16[272,896]{1,0:T(8,128)(2,1)S(1)}, u32[]{:S(2)}, u32[]{:S(2)}) collective-permute-start(bf16[272,896]{1,0:T(8,128)(2,1)} %get-tuple-element.49), channel_id=1, source_target_pairs={{0,8},{8,16},{16,24},{24,0},{1,9},{9,17},{17,25},{25,1},{2,10},{10... | collective-permute-start | bytes 1462280 | tf_op jit(solution)/shard_map/ppermute | solution.py:348
  48.4 35.0 %collective-permute-start.6 = (bf16[272,896]{1,0:T(8,128)(2,1)}, bf16[272,896]{1,0:T(8,128)(2,1)S(1)}, u32[]{:S(2)}, u32[]{:S(2)}) collective-permute-start(bf16[272,896]{1,0:T(8,128)(2,1)} %get-tuple-element.50), channel_id=1, source_target_pairs={{0,16},{8,24},{16,0},{24,8},{1,17},{9,25},{17,1},{25,9},{2,18},{10... | collective-permute-start | bytes 1462280 | tf_op jit(solution)/shard_map/ppermute | solution.py:348
  52.9 30.5 %collective-permute-start.7 = (bf16[272,896]{1,0:T(8,128)(2,1)}, bf16[272,896]{1,0:T(8,128)(2,1)}, u32[]{:S(2)}, u32[]{:S(2)}) collective-permute-start(bf16[272,896]{1,0:T(8,128)(2,1)} %get-tuple-element.51), channel_id=1, source_target_pairs={{0,24},{8,0},{16,8},{24,16},{1,25},{9,1},{17,9},{25,17},{2,26},{10... | collective-permute-start | bytes 1462280 | tf_op jit(solution)/shard_map/ppermute | solution.py:348
  57.1 10.4 %collective-permute-start.1 = (f32[192,128]{1,0:T(8,128)S(1)}, f32[192,128]{1,0:T(8,128)S(1)}, u32[]{:S(2)}, u32[]{:S(2)}) collective-permute-start(f32[192,128]{1,0:T(8,128)S(1)} %get-tuple-element.40.map_ref), channel_id=1, source_target_pairs={{256,384},{257,385},{258,386},{259,387},{260,388},{261,389},{262,3... | collective-permute-start | bytes 294920 | tf_op jit(solution)/shard_map/ppermute | solution.py:357
  58.4 0.7 collective-permute-start
  67.5 14.5 %collective-permute-start.3 = (f32[64,128]{1,0:T(8,128)S(1)}, f32[64,128]{1,0:T(8,128)S(1)}, u32[]{:S(2)}, u32[]{:S(2)}) collective-permute-start(f32[64,128]{1,0:T(8,128)S(1)} %shard_map.135), channel_id=1, source_target_pairs={{128,384},{129,385},{130,386},{131,387},{132,388},{133,389},{134,3... | collective-permute-start | bytes 98312 | tf_op jit(solution)/shard_map/ppermute | solution.py:361
  68.8 13.2 %collective-permute-start.2 = (f32[64,128]{1,0:T(8,128)S(1)}, f32[64,128]{1,0:T(8,128)S(1)}, u32[]{:S(2)}, u32[]{:S(2)}) collective-permute-start(f32[64,128]{1,0:T(8,128)S(1)} %shard_map.135), channel_id=1, source_target_pairs={{128,256},{129,257},{130,258},{131,259},{132,260},{133,261},{134,2... | collective-permute-start | bytes 98312 | tf_op jit(solution)/shard_map/ppermute | solution.py:360
  83.4 11.8 %all-to-all-start.2 = ((f32[4,64,128]{2,1,0:T(8,128)}), f32[4,64,128]{2,1,0:T(8,128)S(1)}, u32[]{:S(2)}, u32[]{:S(2)}) async-start(f32[4,64,128]{2,1,0:T(8,128)} %shard_map.136), calls=%async_computation.2 | async-start | bytes 262144 | tf_op jit(solution)/shard_map/all_to_all | solution.py:370
  96.7 3.7 %copy-start.11 = (f32[4,256,128]{2,1,0:T(8,128)S(1)}, f32[4,256,128]{2,1,0:T(8,128)}, u32[]{:S(2)}) copy-start(f32[4,256,128]{2,1,0:T(8,128)} %copy-done.10) | copy-start | bytes 1572868
  96.7 14.5 %all-to-all-start.3 = ((bf16[4,512,256]{2,1,0:T(8,128)(2,1)}), bf16[4,512,256]{2,1,0:T(8,128)(2,1)S(1)}, u32[]{:S(2)}, u32[]{:S(2)}) async-start(bf16[4,512,256]{2,1,0:T(8,128)(2,1)} %shard_map.140), calls=%async_computation.3 | async-start | bytes 2097152 | tf_op jit(solution)/shard_map/all_to_all | solution.py:374
  100.3 1.4 %copy-start.7 = (f32[4,256,384]{2,1,0:T(8,128)S(1)}, f32[4,256,384]{2,1,0:T(8,128)}, u32[]{:S(2)}) copy-start(f32[4,256,384]{2,1,0:T(8,128)} %copy-done.6) | copy-start | bytes 4718596
  101.7 1.2 copy-start.9
  104.0 0.8 copy-start
  111.2 1.0 copy-start.1
  113.5 10.2 %copy-start.2 = (f32[4,256]{1,0:T(4,128)S(1)}, f32[4,256]{1,0:T(4,128)}, u32[]{:S(2)}) copy-start(f32[4,256]{1,0:T(4,128)} %gain_ref.1) | copy-start | bytes 12292
  113.5 10.2 %all-to-all-start.4 = ((f32[8,8,256]{2,1,0:T(8,128)}), f32[8,8,256]{2,1,0:T(8,128)S(1)}, u32[]{:S(2)}, u32[]{:S(2)}) async-start(f32[8,8,256]{2,1,0:T(8,128)} %bitcast.11), calls=%async_computation.4 | async-start | bytes 131072 | tf_op jit(solution)/shard_map/all_to_all | solution.py:378

commit v4 on v2

--- a/solution.py
+++ b/solution.py
@@ -13,7 +13,6 @@
 WINDOW = 2048
 PART = VD // 4
 MARK_ROWS = 16
-VMEM_BYTES = 48 * 2**20
 
 SEQ = ("zh", "zl", "x")
 f32 = jnp.float32
@@ -40,7 +39,7 @@
     return dot(ah, b) + dot(al, b)
 
 
-def call(body, out_shape, scalars=0, inputs=1, scratch=(), flops=1e7):
+def call(body, out_shape, scalars=0, inputs=1, scratch=(), flops=1e7, mib=8):
     whole = pl.BlockSpec(memory_space=pltpu.VMEM)
     small = pl.BlockSpec(memory_space=pltpu.SMEM)
     return pl.pallas_call(
@@ -50,12 +49,12 @@
         out_shape=out_shape,
         scratch_shapes=list(scratch),
         cost_estimate=pl.CostEstimate(flops=int(flops), bytes_accessed=10**6, transcendentals=0),
-        compiler_params=pltpu.CompilerParams(vmem_limit_bytes=VMEM_BYTES),
+        compiler_params=pltpu.CompilerParams(vmem_limit_bytes=mib * 2**20),
     )
 
 
 def block_terms(
-    count_ref, q_ref, k_ref, v_ref, gate_ref, beta_ref, map_ref, new_ref, mixing_ref, carry_ref, x_ref, a_ref
+    count_ref, q_ref, k_ref, v_ref, gate_ref, beta_ref, map_ref, carry_ref, local_ref, x_ref, a_ref
 ):
     count = count_ref[0]
     row = lax.broadcasted_iota(jnp.int32, (ROWS, ROWS), 0)
@@ -81,7 +80,7 @@
         q = q_ref[h]
         wide = q.astype(f32)
         q_col = lax.rsqrt(jnp.sum(wide * wide, axis=1, keepdims=True) + 1e-6)
-        mixing_ref[h] = (q_col * decay) * (dot(q, k, ((1,), (1,))) * k_row)
+        local_ref[h] = (q_col * decay) * (dot(q, k, ((1,), (1,))) * k_row)
         kept.append((log_col, log_row, beta, k_col, k_row, q_col))
     step = 1
     while (2 << step) <= ROWS:
@@ -112,14 +111,8 @@
         update = dot(k, high, ((0,), (0,))) + dot(k, low, ((0,), (0,)))
         map_ref[h, :, :KD] = jnp.where(row_k == col_k, jnp.exp(last), 0.0) - update[:, :KD]
         map_ref[h, :, KD:] = update[:, KD:]
-        new_ref[h] = new
-        carry_ref[h] = (jnp.exp(log_col) * q_col) * q_ref[h].astype(f32)
-
-
-def row_terms(new_ref, mixing_ref, straight_ref, carry_ref, local_ref):
-    for h in range(HEADS):
-        mixed = dot3(mixing_ref[h], new_ref[h])
-        carry_ref[h] = straight_ref[h] - mixed[:, :KD]
+        mixed = dot3(local_ref[h], new)
+        carry_ref[h] = (jnp.exp(log_col) * q_col) * q_ref[h].astype(f32) - mixed[:, :KD]
         local_ref[h] = mixed[:, KD:]
 
 
@@ -137,17 +130,37 @@
     return jnp.concatenate([state[:, :KD], state[:, KD:] + offset], axis=1)
 
 
-def compose_plane(maps_ref, before_ref, send_ref):
+def pick(index, choices):
+    picked = choices[0]
+    for i in range(1, len(choices)):
+        picked = jnp.where(index == i, choices[i], picked)
+    return picked
+
+
+def ahead(place, shift):
+    return lax.rem(place + shift, 4)
+
+
+def compose_plane(place_ref, maps_ref, before_ref, *send_refs):
     state = maps_ref[0]
     for i in range(1, 4):
         before_ref[i - 1] = state
         state = then(state, maps_ref[i, :, :KD], maps_ref[i, :, KD:])
-    for i in range(4):
-        send_ref[i, :KD, :] = state[:, :KD]
-        send_ref[i, KD:, :] = fold(state[:, KD + i * PART : KD + (i + 1) * PART])
-
-
-def compose_group(maps_ref, before_ref, total_ref, offset_ref):
+    quarters = [fold(state[:, KD + i * PART : KD + (i + 1) * PART]) for i in range(4)]
+    for d, send_ref in enumerate(send_refs):
+        send_ref[:KD, :] = state[:, :KD]
+        send_ref[KD:, :] = pick(ahead(place_ref[0], d), quarters)
+
+
+def in_order(place, refs, ordered_ref):
+    for d, ref in enumerate(refs):
+        ordered_ref[pl.ds(ahead(place, 4 - d), 1)] = ref[...][None]
+
+
+def compose_group(
+    place_ref, own_ref, one_ref, two_ref, three_ref, before_ref, total_ref, offset_ref, maps_ref
+):
+    in_order(place_ref[0], (own_ref, one_ref, two_ref, three_ref), maps_ref)
     state = jnp.concatenate([maps_ref[0, :KD, :], unfold(maps_ref[0, KD:, :])], axis=1)
     for i in range(1, 4):
         before_ref[i - 1] = state
@@ -163,36 +176,32 @@
     out_ref[...] = fold(state) + map_ref[KD:, :]
 
 
-def group_states(place_ref, first_ref, one_ref, two_ref, third_ref, before_ref, out_ref):
-    place = place_ref[0]
+def group_states(place_ref, first_ref, one_ref, two_ref, third_ref, before_ref, *out_refs):
+    group = place_ref[0]
     last = fold(dot3(third_ref[:KD, :], unfold(two_ref[...]))) + third_ref[KD:, :]
-    state = jnp.where(
-        place == 0,
-        0.0,
-        jnp.where(place == 1, first_ref[...], jnp.where(place == 2, one_ref[...], last)),
-    )
+    entering = pick(group, [jnp.zeros_like(last), first_ref[...], one_ref[...], last])
+    state = unfold(entering)
+    planes = [entering]
+    for i in range(3):
+        planes.append(fold(dot3(before_ref[i, :, :KD], state) + before_ref[i, :, KD:]))
+    for d, out_ref in enumerate(out_refs):
+        out_ref[...] = pick(ahead(place_ref[1], d), planes)
+
+
+def plane_states(
+    place_ref, own_ref, one_ref, two_ref, three_ref, before_ref, out_ref, parts_ref
+):
+    in_order(place_ref[0], (own_ref, one_ref, two_ref, three_ref), parts_ref)
+    state = jnp.concatenate([unfold(parts_ref[i]) for i in range(4)], axis=1)
     out_ref[0] = state
-    state = unfold(state)
     for i in range(3):
-        out_ref[i + 1] = fold(dot3(before_ref[i, :, :KD], state) + before_ref[i, :, KD:])
-
-
-def plane_states(parts_ref, before_ref, attn_ref, out_ref):
-    state = jnp.concatenate([unfold(parts_ref[i]) for i in range(4)], axis=1)
-    for i in range(4):
-        entering = state
-        if i > 0:
-            entering = dot3(before_ref[i - 1, :, :KD], state) + before_ref[i - 1, :, KD:]
-        out_ref[i, :KD, :], out_ref[i, KD : 2 * KD, :] = halves(entering)
-        out_ref[i, 2 * KD :, :] = attn_ref[i]
+        out_ref[i + 1] = dot3(before_ref[i, :, :KD], state) + before_ref[i, :, KD:]
 
 
 def raw_rows(carry_ref, local_ref, state_ref, raw_ref, square_ref):
     total = jnp.zeros((ROWS, VD), f32)
     for h in range(HEADS):
-        carry_high, carry_low = halves(carry_ref[h])
-        high, low = state_ref[h, :KD, :], state_ref[h, KD : 2 * KD, :]
-        raw = local_ref[h] + dot(carry_high, high) + (dot(carry_high, low) + dot(carry_low, high))
+        raw = local_ref[h] + dot3(carry_ref[h], state_ref[h])
         raw_ref[h] = raw
         total = total + raw * raw
     column = jnp.sum(total, axis=1, keepdims=True)
@@ -230,7 +239,8 @@
         out_ref[h, ROWS:, ROWS:] = jnp.zeros((MARK_ROWS, 2 * KD + VD - ROWS), bf16)
 
 
-def attend(here_ref, past_ref, out_ref):
+def attend(place_ref, here_ref, past_ref, *refs):
+    out_refs, rows_ref = refs[:4], refs[4]
     row = lax.broadcasted_iota(jnp.int32, (ROWS, ROWS), 0)
     col = lax.broadcasted_iota(jnp.int32, (ROWS, ROWS), 1)
 
@@ -263,11 +273,24 @@
             weight_sum = weight_sum + weights
             mixed = mixed + dot(weights.astype(bf16), ref[i, :ROWS, KD : KD + VD])
         mixed = mixed / jnp.sum(weight_sum, axis=1, keepdims=True)
-        out_ref[j] = jnp.where(query_marks > 0.0, mixed, 0.0).astype(bf16)
+        rows_ref[j] = jnp.where(query_marks > 0.0, mixed, 0.0).astype(bf16)
+    for d, out_ref in enumerate(out_refs):
+        out_ref[...] = rows_ref[pl.ds(ahead(place_ref[0], d), 1)][0]
+
+
+def gather_heads(place_ref, own_ref, one_ref, two_ref, three_ref, out_ref):
+    in_order(place_ref[0], (own_ref, one_ref, two_ref, three_ref), out_ref)
 
 
 def heads_first(block):
     return jnp.swapaxes(block, 0, 1)
+
+
+def around(parts, axis):
+    return [
+        lax.ppermute(part, axis, [(i, (i + d) % 4) for i in range(4)]) if d else part
+        for d, part in enumerate(parts)
+    ]
 
 
 def shape_of(*dims, kind=f32):
@@ -288,6 +311,27 @@
     attn_position,
     attn_count,
 ):
+    zh, zl, x = (lax.axis_index(name).astype(jnp.int32).reshape(1) for name in SEQ)
+    maps, carry, local = call(
+        block_terms,
+        (shape_of(HEADS, KD, KD + VD), shape_of(HEADS, ROWS, KD), shape_of(HEADS, ROWS, VD)),
+        scalars=1,
+        inputs=5,
+        scratch=[pltpu.VMEM((HEADS, ROWS, ROWS), f32)] * 2,
+        flops=8e9,
+        mib=16,
+    )(
+        delta_count,
+        heads_first(delta_query),
+        heads_first(delta_key),
+        heads_first(delta_value),
+        delta_gate.T,
+        delta_beta.T,
+    )
+    maps, attn_key, attn_value, attn_query = lax.optimization_barrier(
+        (maps, attn_key, attn_value, attn_query)
+    )
+    exchanged = lax.all_to_all(maps, "x", 0, 0, tiled=True)
     packed = call(
         pack_blocks, shape_of(HEADS, ROWS + MARK_ROWS, 2 * KD + VD, kind=bf16), scalars=1, inputs=4
     )(
@@ -297,65 +341,62 @@
         heads_first(attn_query),
         attn_position.reshape(1, ROWS),
     )
+    plane_prefix, *plane_totals = call(
+        compose_plane,
+        (shape_of(3, KD, KD + VD),) + (shape_of(KD + PART, KD),) * 4,
+        scalars=1,
+    )(zl, exchanged)
+    _, packed = lax.optimization_barrier((plane_totals[0], packed))
+    plane_totals = around(plane_totals, "zl")
     here = lax.all_to_all(packed, "x", 0, 0, tiled=True)
-    maps, new, mixing, straight = call(
-        block_terms,
-        (
-            shape_of(HEADS, KD, KD + VD),
-            shape_of(HEADS, ROWS, KD + VD),
-            shape_of(HEADS, ROWS, ROWS),
-            shape_of(HEADS, ROWS, KD),
-        ),
-        scalars=1,
-        inputs=5,
-        scratch=[pltpu.VMEM((HEADS, ROWS, ROWS), f32)] * 2,
-        flops=8e9,
-    )(
-        delta_count,
-        heads_first(delta_query),
-        heads_first(delta_key),
-        heads_first(delta_value),
-        delta_gate.T,
-        delta_beta.T,
-    )
-    maps, here, past = lax.optimization_barrier((maps, here, here[:, :, : KD + VD]))
-    past = lax.ppermute(past, ("zh", "zl"), [(i, i + 1) for i in range(15)])
-    exchanged = lax.all_to_all(maps, "x", 0, 0, tiled=True)
-    carry, local = call(
-        row_terms, (shape_of(HEADS, ROWS, KD), shape_of(HEADS, ROWS, VD)), inputs=3, flops=2e9
-    )(new, mixing, straight)
-    plane_prefix, plane_total = call(
-        compose_plane, (shape_of(3, KD, KD + VD), shape_of(4, KD + PART, KD))
-    )(exchanged)
-    gathered = lax.all_to_all(plane_total, "zl", 0, 0, tiled=True)
     group_prefix, group_total, group_offset = call(
         compose_group,
         (shape_of(3, KD, KD + PART), shape_of(KD + PART, KD), shape_of(PART, KD)),
-    )(gathered)
+        scalars=1,
+        inputs=4,
+        scratch=[pltpu.VMEM((4, KD + PART, KD), f32)],
+    )(zl, *plane_totals)
     first = lax.ppermute(group_offset, "zh", [(0, 1)])
     third = lax.ppermute(group_total, "zh", [(2, 3)])
+    _, here = lax.optimization_barrier((first, here))
+    past = lax.ppermute(here[:, :, : KD + VD], ("zh", "zl"), [(i, i + 1) for i in range(15)])
     pair = call(step_state, shape_of(PART, KD), inputs=2)(group_total, first)
     one = lax.ppermute(pair, "zh", [(1, 2)])
     two = lax.ppermute(pair, "zh", [(1, 3)])
-    place = lax.axis_index("zh").astype(jnp.int32).reshape(1)
-    planes = call(group_states, shape_of(4, PART, KD), scalars=1, inputs=5)(
-        place, first, one, two, third, group_prefix
-    )
-    planes, past = lax.optimization_barrier((planes, past))
-    attn_heads = call(attend, shape_of(4, ROWS, VD, kind=bf16), inputs=2, flops=8e9)(here, past)
-    parts = lax.all_to_all(planes, "zl", 0, 0, tiled=True)
-    returned = call(plane_states, shape_of(4, 2 * KD + ROWS, VD, kind=bf16), inputs=3)(
-        parts, plane_prefix, attn_heads
-    )
-    states = lax.all_to_all(returned, "x", 0, 0, tiled=True)
+    planes = call(group_states, (shape_of(PART, KD),) * 4, scalars=1, inputs=5)(
+        jnp.concatenate([zh, zl]), first, one, two, third, group_prefix
+    )
+    states = call(
+        plane_states,
+        shape_of(4, KD, VD),
+        scalars=1,
+        inputs=5,
+        scratch=[pltpu.VMEM((4, PART, KD), f32)],
+    )(zl, *around(planes, "zl"), plane_prefix)
+    _, here, past = lax.optimization_barrier((states, here, past))
+    attn_rows = call(
+        attend,
+        (shape_of(ROWS, VD, kind=bf16),) * 4,
+        scalars=1,
+        inputs=2,
+        scratch=[pltpu.VMEM((4, ROWS, VD), bf16)],
+        flops=8e9,
+        mib=16,
+    )(x, here, past)
+    attn_rows = around(attn_rows, "x")
+    states = lax.all_to_all(states, "x", 0, 0, tiled=True)
     raw, squares = call(
         raw_rows, (shape_of(HEADS, ROWS, VD), shape_of(64, ROWS)), inputs=3
     )(carry, local, states)
     squares = lax.all_to_all(squares, "head", 0, 0, tiled=True)
+    attn_heads = call(
+        gather_heads, shape_of(HEADS, ROWS, VD, kind=bf16), scalars=1, inputs=4
+    )(x, *attn_rows)
+    squares, attn_heads = lax.optimization_barrier((squares, attn_heads))
     delta_heads = call(normed, shape_of(HEADS, ROWS, VD, kind=bf16), scalars=1, inputs=3)(
         delta_count, raw, squares, delta_gain
     )
-    return (heads_first(delta_heads), heads_first(states[:, 2 * KD :]))
+    return (heads_first(delta_heads), heads_first(attn_heads))
 
 
 def solution(mesh):

time: 123 us -> 139 us (1.13)
  starting transfers between devices: 31.5 us -> 54.9 us
  blocking collectives: 13.8 us -> 0 us
  waiting for transfers between devices: 42 us -> 53.1 us
  local copies, waits for them, and re-layouts: 12.2 us -> 6.95 us
  Pallas kernels: 19.6 us -> 21 us
    ppermute x1 -> x10, starting transfers between devices: 1.28 us -> 34.5 us  [the longest x9 33.3 us: around(): lax.ppermute(part, axis, [(i, (i + d) % 4) for i in range(4)])]
    all_to_all x1 -> x0, blocking collectives: 13.8 us -> none  [shards(): exchanged = lax.all_to_all(maps, 'x', 0, 0, tiled=True)]
    ppermute x1, waiting for transfers between devices: 0.01 us -> 12.6 us  [shards(): third = lax.ppermute(group_total, 'zh', [(2, 3)])]
    ppermute x1 -> x10, waiting for transfers between devices: 0.01 us -> 11 us  [the longest x9 11 us: around(): lax.ppermute(part, axis, [(i, (i + d) % 4) for i in range(4)])]
    all_to_all x3 -> x2, starting transfers between devices: 17.3 us -> 8.37 us  [the longest x1 4.41 us: shards(): exchanged = lax.all_to_all(maps, 'x', 0, 0, tiled=True)]
    unnamed x38 -> x25, local copies, waits for them, and re-layouts: 11.1 us -> 5.74 us
    all_to_all x3 -> x2, waiting for transfers between devices: 15.4 us -> 10.3 us  [the longest x1 10.3 us: shards(): exchanged = lax.all_to_all(maps, 'x', 0, 0, tiled=True)]
    all_to_all x1, waiting for transfers between devices: 4.44 us -> 0.01 us  [shards(): here = lax.all_to_all(packed, 'x', 0, 0, tiled=True)]
  transfers between devices with their start and end apart: 10 -> 18, of which waited for: 6 -> 7; matrix products, arithmetic and copies ran while one was open for 1% -> 0% of each run, Pallas kernels for 11% -> 8%
where the time goes in v4:
time: 139 us; the launch traced here: 138 us
  starting transfers between devices  54.9 us (39%)
  waiting for transfers between devices  53.1 us (38%)
  Pallas kernels  21 us (15%)
  local copies, waits for them, and re-layouts  6.95 us (5%)
  between operations  2.39 us (2%)
    ppermute x9, starting transfers between devices, around(): lax.ppermute(part, axis, [(i, (i + d) % 4) for i in range(4)])  33.3 us
    ppermute x1, waiting for transfers between devices, shards(): two = lax.ppermute(pair, 'zh', [(1, 3)])  13.7 us
    ppermute x1, waiting for transfers between devices, shards(): third = lax.ppermute(group_total, 'zh', [(2, 3)])  12.6 us
    ppermute x9, waiting for transfers between devices, around(): lax.ppermute(part, axis, [(i, (i + d) % 4) for i in range(4)])  11 us
    all_to_all x1, waiting for transfers between devices, shards(): exchanged = lax.all_to_all(maps, 'x', 0, 0, tiled=True)  10.3 us
    pallas_call x1, Pallas kernels, shards(): call(block_terms, (shape_of(HEADS, KD, KD + VD), shape_of(HEADS, ROWS, KD...  8.99 us
    unnamed x25, local copies, waits for them, and re-layouts  5.74 us
    all_to_all x1, waiting for transfers between devices, shards(): squares = lax.all_to_all(squares, 'head', 0, 0, tiled=True)  5.55 us
  transfers between devices with their start and end apart: 18, of which 7 were waited for; matrix products, arithmetic and copies ran while one was open for 0% of the time, Pallas kernels for 8%

profile of v4, /device:TPU:480, one launch (start us, length us, event | category | flops | bytes accessed | tf_op | source)
XLA Modules:
  0.0 138.5 jit_solution(12397286991584191293)
XLA Ops:
  1.4 1.1 copy.29
  2.5 0.1 copy_bitcast_fusion.4
  2.6 9.0 %shard_map.131 = (f32[4,128,384]{2,1,0:T(8,128)}, f32[4,256,128]{2,1,0:T(8,128)S(1)}, f32[4,256,256]{2,1,0:T(8,128)S(1)}) custom-call(s32[1]{0:T(128)S(6)} %copy.32.count_ref, bf16[4,256,128]{2,1,0:T(8,128)(2,1)S(1)} %get-tuple-element.67.q_ref, bf16[4,256,128]{2,1,0:T(8,128)(2,1)S(1)} %get-tuple-element.66.k_ref, bf16[4,256,256]{2,1,0:T(8,128)(2,1)S(1)} %bitcast.31, ...), custom_call_target="tpu_custom_call" | custom-call | flops 8000000000 | bytes 1000000 | tf_op jit(solution)/shard_map/pallas_call | solution.py:315
  11.6 1.0 copy-done
  12.6 4.4 %all-to-all-start = ((f32[4,128,384]{2,1,0:T(8,128)}), f32[4,128,384]{2,1,0:T(8,128)S(1)}, u32[]{:S(2)}, u32[]{:S(2)}) async-start(f32[4,128,384]{2,1,0:T(8,128)} %get-tuple-element.36), calls=%async_computation | async-start | bytes 1572864 | tf_op jit(solution)/shard_map/all_to_all | solution.py:334
  17.8 0.1 copy.28
  17.9 1.1 shard_map.138
  19.0 10.3 %all-to-all-done.maps_ref = f32[4,128,384]{2,1,0:T(8,128)S(1)} async-done(((f32[4,128,384]{2,1,0:T(8,128)}), f32[4,128,384]{2,1,0:T(8,128)S(1)}, u32[]{:S(2)}, u32[]{:S(2)}) %all-to-all-start) | async-done | bytes 786464 | tf_op jit(solution)/shard_map/all_to_all | solution.py:334
  29.3 0.8 shard_map.132
  30.1 3.5 %all-to-all-start.3 = ((bf16[4,272,512]{2,1,0:T(8,128)(2,1)}), bf16[4,272,512]{2,1,0:T(8,128)(2,1)S(1)}, u32[]{:S(2)}, u32[]{:S(2)}) async-start(bf16[4,272,512]{2,1,0:T(8,128)(2,1)} %shard_map.138), calls=%async_computation.3 | async-start | bytes 2228224 | tf_op jit(solution)/shard_map/all_to_all | solution.py:351
  33.7 3.8 %collective-permute-start = (f32[192,128]{1,0:T(8,128)S(1)}, f32[192,128]{1,0:T(8,128)S(1)}, u32[]{:S(2)}, u32[]{:S(2)}) collective-permute-start(f32[192,128]{1,0:T(8,128)S(1)} %get-tuple-element.38), channel_id=1, source_target_pairs={{0,32},{32,64},{64,96},{96,0},{1,33},{33,65},{65,97},{97,1},{2,34}... | collective-permute-start | bytes 294920 | tf_op jit(solution)/shard_map/ppermute | solution.py:291
  37.5 2.5 %collective-permute-start.1 = (f32[192,128]{1,0:T(8,128)S(1)}, f32[192,128]{1,0:T(8,128)S(1)}, u32[]{:S(2)}, u32[]{:S(2)}) collective-permute-start(f32[192,128]{1,0:T(8,128)S(1)} %get-tuple-element.39), channel_id=1, source_target_pairs={{0,64},{32,96},{64,0},{96,32},{1,65},{33,97},{65,1},{97,33},{2,66}... | collective-permute-start | bytes 294920 | tf_op jit(solution)/shard_map/ppermute | solution.py:291
  39.9 2.9 %collective-permute-start.2 = (f32[192,128]{1,0:T(8,128)S(1)}, f32[192,128]{1,0:T(8,128)S(1)}, u32[]{:S(2)}, u32[]{:S(2)}) collective-permute-start(f32[192,128]{1,0:T(8,128)S(1)} %get-tuple-element.40), channel_id=1, source_target_pairs={{0,96},{32,0},{64,32},{96,64},{1,97},{33,1},{65,33},{97,65},{2,98}... | collective-permute-start | bytes 294920 | tf_op jit(solution)/shard_map/ppermute | solution.py:291
  42.9 3.6 %collective-permute-done.1.two_ref = f32[192,128]{1,0:T(8,128)S(1)} collective-permute-done((f32[192,128]{1,0:T(8,128)S(1)}, f32[192,128]{1,0:T(8,128)S(1)}, u32[]{:S(2)}, u32[]{:S(2)}) %collective-permute-start.1) | collective-permute-done | bytes 98336 | tf_op jit(solution)/shard_map/ppermute | solution.py:291
  46.6 1.7 %collective-permute-done.2.three_ref = f32[192,128]{1,0:T(8,128)S(1)} collective-permute-done((f32[192,128]{1,0:T(8,128)S(1)}, f32[192,128]{1,0:T(8,128)S(1)}, u32[]{:S(2)}, u32[]{:S(2)}) %collective-permute-start.2) | collective-permute-done | bytes 98336 | tf_op jit(solution)/shard_map/ppermute | solution.py:291
  48.3 0.8 shard_map.133
  49.1 0.7 collective-permute-start.3
  49.7 0.0 all-to-all-done.3.here_ref
  49.8 1.0 slice.3
  50.7 1.3 collective-permute-start.10
  52.0 1.3 collective-permute-start.6
  53.3 0.3 shard_map.134
  53.6 1.3 collective-permute-start.5
  54.9 0.7 collective-permute-start.4
  55.6 0.1 pad_add_fusion.place_ref
  55.7 13.7 %collective-permute-done.5.two_ref = f32[64,128]{1,0:T(8,128)S(1)} collective-permute-done((f32[64,128]{1,0:T(8,128)S(1)}, f32[64,128]{1,0:T(8,128)S(1)}, u32[]{:S(2)}, u32[]{:S(2)}) %collective-permute-start.5) | collective-permute-done | bytes 32800 | tf_op jit(solution)/shard_map/ppermute | solution.py:365
  69.4 12.6 %collective-permute-done.6.third_ref = f32[192,128]{1,0:T(8,128)S(1)} collective-permute-done((f32[192,128]{1,0:T(8,128)S(1)}, f32[192,128]{1,0:T(8,128)S(1)}, u32[]{:S(2)}, u32[]{:S(2)}) %collective-permute-start.6) | collective-permute-done | bytes 98336 | tf_op jit(solution)/shard_map/ppermute | solution.py:360
  82.0 1.2 shard_map.135
  83.2 4.7 %collective-permute-start.7 = (f32[64,128]{1,0:T(8,128)S(1)}, f32[64,128]{1,0:T(8,128)S(1)}, u32[]{:S(2)}, u32[]{:S(2)}) collective-permute-start(f32[64,128]{1,0:T(8,128)S(1)} %get-tuple-element.45), channel_id=1, source_target_pairs={{0,32},{32,64},{64,96},{96,0},{1,33},{33,65},{65,97},{97,1},{2,34}... | collective-permute-start | bytes 98312 | tf_op jit(solution)/shard_map/ppermute | solution.py:291
  87.9 5.5 %collective-permute-start.8 = (f32[64,128]{1,0:T(8,128)S(1)}, f32[64,128]{1,0:T(8,128)S(1)}, u32[]{:S(2)}, u32[]{:S(2)}) collective-permute-start(f32[64,128]{1,0:T(8,128)S(1)} %get-tuple-element.46), channel_id=1, source_target_pairs={{0,64},{32,96},{64,0},{96,32},{1,65},{33,97},{65,1},{97,33},{2,66}... | collective-permute-start | bytes 98312 | tf_op jit(solution)/shard_map/ppermute | solution.py:291
  93.5 1.9 %collective-permute-start.9 = (f32[64,128]{1,0:T(8,128)S(1)}, f32[64,128]{1,0:T(8,128)S(1)}, u32[]{:S(2)}, u32[]{:S(2)}) collective-permute-start(f32[64,128]{1,0:T(8,128)S(1)} %get-tuple-element.47), channel_id=1, source_target_pairs={{0,96},{32,0},{64,32},{96,64},{1,97},{33,1},{65,33},{97,65},{2,98}... | collective-permute-start | bytes 98312 | tf_op jit(solution)/shard_map/ppermute | solution.py:291
  95.4 0.0 collective-permute-done.7.one_ref
  95.4 0.0 collective-permute-done.8.two_ref
  95.4 5.7 %collective-permute-done.9.three_ref = f32[64,128]{1,0:T(8,128)S(1)} collective-permute-done((f32[64,128]{1,0:T(8,128)S(1)}, f32[64,128]{1,0:T(8,128)S(1)}, u32[]{:S(2)}, u32[]{:S(2)}) %collective-permute-start.9) | collective-permute-done | bytes 32800 | tf_op jit(solution)/shard_map/ppermute | solution.py:291
  101.1 1.3 shard_map.136
  102.3 4.0 %all-to-all-start.1 = ((f32[4,128,256]{2,1,0:T(8,128)}), f32[4,128,256]{2,1,0:T(8,128)S(1)}, u32[]{:S(2)}, u32[]{:S(2)}) async-start(f32[4,128,256]{2,1,0:T(8,128)} %shard_map.136), calls=%async_computation.1 | async-start | bytes 1048576 | tf_op jit(solution)/shard_map/all_to_all | solution.py:387
  106.3 0.0 collective-permute-done.10.past_ref
  106.3 4.9 %shard_map.139 = (bf16[256,256]{1,0:T(8,128)(2,1)S(1)}, bf16[256,256]{1,0:T(8,128)(2,1)}, bf16[256,256]{1,0:T(8,128)(2,1)}, bf16[256,256]{1,0:T(8,128)(2,1)S(1)}) custom-call(s32[1]{0:T(128)} %bitcast.9.place_ref, bf16[4,272,512]{2,1,0:T(8,128)(2,1)S(1)} %all-to-all-done.3.here_ref, bf16[4,272,384]{2,1,0:T(8,128)(2,1)} %collective-permute-done.10.past_ref), custom_call_target="tpu_custom_call" | custom-call | flops 8000000000 | bytes 1000000 | tf_op jit(solution)/shard_map/pallas_call | solution.py:377
  111.2 3.9 %collective-permute-start.11 = (bf16[256,256]{1,0:T(8,128)(2,1)}, bf16[256,256]{1,0:T(8,128)(2,1)S(1)}, u32[]{:S(2)}, u32[]{:S(2)}) collective-permute-start(bf16[256,256]{1,0:T(8,128)(2,1)} %get-tuple-element.59), channel_id=1, source_target_pairs={{0,8},{8,16},{16,24},{24,0},{1,9},{9,17},{17,25},{25,1},{2,10},{10... | collective-permute-start | bytes 393224 | tf_op jit(solution)/shard_map/ppermute | solution.py:291
  115.2 4.6 %collective-permute-start.12 = (bf16[256,256]{1,0:T(8,128)(2,1)}, bf16[256,256]{1,0:T(8,128)(2,1)S(1)}, u32[]{:S(2)}, u32[]{:S(2)}) collective-permute-start(bf16[256,256]{1,0:T(8,128)(2,1)} %get-tuple-element.60), channel_id=1, source_target_pairs={{0,16},{8,24},{16,0},{24,8},{1,17},{9,25},{17,1},{25,9},{2,18},{10... | collective-permute-start | bytes 393224 | tf_op jit(solution)/shard_map/ppermute | solution.py:291
  119.7 3.4 %collective-permute-start.13 = (bf16[256,256]{1,0:T(8,128)(2,1)S(1)}, bf16[256,256]{1,0:T(8,128)(2,1)S(1)}, u32[]{:S(2)}, u32[]{:S(2)}) collective-permute-start(bf16[256,256]{1,0:T(8,128)(2,1)S(1)} %get-tuple-element.61), channel_id=1, source_target_pairs={{0,24},{8,0},{16,8},{24,16},{1,25},{9,1},{17,9},{25,17},{2,26},{10... | collective-permute-start | bytes 393224 | tf_op jit(solution)/shard_map/ppermute | solution.py:291
  123.1 1.2 copy-done.1
  124.4 1.3 shard_map.137
  125.6 4.6 %all-to-all-start.2 = ((f32[8,8,256]{2,1,0:T(8,128)}), f32[8,8,256]{2,1,0:T(8,128)S(1)}, u32[]{:S(2)}, u32[]{:S(2)}) async-start(f32[8,8,256]{2,1,0:T(8,128)} %bitcast.7), calls=%async_computation.2 | async-start | bytes 131072 | tf_op jit(solution)/shard_map/all_to_all | solution.py:391
  130.3 5.5 %all-to-all-done.2 = f32[8,8,256]{2,1,0:T(8,128)S(1)} async-done(((f32[8,8,256]{2,1,0:T(8,128)}), f32[8,8,256]{2,1,0:T(8,128)S(1)}, u32[]{:S(2)}, u32[]{:S(2)}) %all-to-all-start.2) | async-done | bytes 65568 | tf_op jit(solution)/shard_map/all_to_all | solution.py:391
  135.9 0.2 shard_map.141
  136.1 1.2 copy.20
  137.3 1.2 copy.21
  (30 shorter events, 0.2 us)
Async XLA Ops:
  0.6 1.9 %copy-start.9 = (bf16[256,4,128]{2,1,0:T(4,128)(2,1)S(1)}, bf16[256,4,128]{2,1,0:T(4,128)(2,1)}, u32[]{:S(2)}) copy-start(bf16[256,4,128]{2,1,0:T(4,128)(2,1)} %param.13) | copy-start | bytes 786436
  0.6 1.9 %copy-start.10 = (bf16[256,4,128]{2,1,0:T(4,128)(2,1)S(1)}, bf16[256,4,128]{2,1,0:T(4,128)(2,1)}, u32[]{:S(2)}) copy-start(bf16[256,4,128]{2,1,0:T(4,128)(2,1)} %param.12) | copy-start | bytes 786436
  0.7 1.9 %copy-start.5 = (f32[256,4]{0,1:T(4,128)S(1)}, f32[256,4]{0,1:T(4,128)}, u32[]{:S(2)}) copy-start(f32[256,4]{0,1:T(4,128)} %param.16) | copy-start | bytes 12292
  0.7 1.9 %copy-start.4 = (f32[256,4]{0,1:T(4,128)S(1)}, f32[256,4]{0,1:T(4,128)}, u32[]{:S(2)}) copy-start(f32[256,4]{0,1:T(4,128)} %param.15) | copy-start | bytes 12292
  11.6 1.0 copy-start
  12.6 5.1 %copy-start.7 = (bf16[256,4,128]{2,1,0:T(4,128)(2,1)S(1)}, bf16[256,4,128]{2,1,0:T(4,128)(2,1)}, u32[]{:S(2)}) copy-start(bf16[256,4,128]{2,1,0:T(4,128)(2,1)} %param.20) | copy-start | bytes 786436
  12.6 5.1 %copy-start.8 = (bf16[256,4,128]{2,1,0:T(4,128)(2,1)S(1)}, bf16[256,4,128]{2,1,0:T(4,128)(2,1)}, u32[]{:S(2)}) copy-start(bf16[256,4,128]{2,1,0:T(4,128)(2,1)} %param.19) | copy-start | bytes 786436
  12.6 5.2 %copy-start.6 = (bf16[256,4,256]{2,1,0:T(4,128)(2,1)S(1)}, bf16[256,4,256]{2,1,0:T(4,128)(2,1)}, u32[]{:S(2)}) copy-start(bf16[256,4,256]{2,1,0:T(4,128)(2,1)} %param.21) | copy-start | bytes 1572868
  12.6 16.7 %all-to-all-start = ((f32[4,128,384]{2,1,0:T(8,128)}), f32[4,128,384]{2,1,0:T(8,128)S(1)}, u32[]{:S(2)}, u32[]{:S(2)}) async-start(f32[4,128,384]{2,1,0:T(8,128)} %get-tuple-element.36), calls=%async_computation | async-start | bytes 1572864 | tf_op jit(solution)/shard_map/all_to_all | solution.py:334
  17.0 0.9 copy-start.3
  30.1 19.6 %all-to-all-start.3 = ((bf16[4,272,512]{2,1,0:T(8,128)(2,1)}), bf16[4,272,512]{2,1,0:T(8,128)(2,1)S(1)}, u32[]{:S(2)}, u32[]{:S(2)}) async-start(bf16[4,272,512]{2,1,0:T(8,128)(2,1)} %shard_map.138), calls=%async_computation.3 | async-start | bytes 2228224 | tf_op jit(solution)/shard_map/all_to_all | solution.py:351
  33.7 9.2 %collective-permute-start = (f32[192,128]{1,0:T(8,128)S(1)}, f32[192,128]{1,0:T(8,128)S(1)}, u32[]{:S(2)}, u32[]{:S(2)}) collective-permute-start(f32[192,128]{1,0:T(8,128)S(1)} %get-tuple-element.38), channel_id=1, source_target_pairs={{0,32},{32,64},{64,96},{96,0},{1,33},{33,65},{65,97},{97,1},{2,34}... | collective-permute-start | bytes 294920 | tf_op jit(solution)/shard_map/ppermute | solution.py:291
  37.5 9.1 %collective-permute-start.1 = (f32[192,128]{1,0:T(8,128)S(1)}, f32[192,128]{1,0:T(8,128)S(1)}, u32[]{:S(2)}, u32[]{:S(2)}) collective-permute-start(f32[192,128]{1,0:T(8,128)S(1)} %get-tuple-element.39), channel_id=1, source_target_pairs={{0,64},{32,96},{64,0},{96,32},{1,65},{33,97},{65,1},{97,33},{2,66}... | collective-permute-start | bytes 294920 | tf_op jit(solution)/shard_map/ppermute | solution.py:291
  39.9 8.3 %collective-permute-start.2 = (f32[192,128]{1,0:T(8,128)S(1)}, f32[192,128]{1,0:T(8,128)S(1)}, u32[]{:S(2)}, u32[]{:S(2)}) collective-permute-start(f32[192,128]{1,0:T(8,128)S(1)} %get-tuple-element.40), channel_id=1, source_target_pairs={{0,96},{32,0},{64,32},{96,64},{1,97},{33,1},{65,33},{97,65},{2,98}... | collective-permute-start | bytes 294920 | tf_op jit(solution)/shard_map/ppermute | solution.py:291
  49.1 0.7 collective-permute-start.3
  50.7 55.6 %collective-permute-start.10 = (bf16[4,272,384]{2,1,0:T(8,128)(2,1)}, bf16[4,272,384]{2,1,0:T(8,128)(2,1)}, u32[]{:S(2)}, u32[]{:S(2)}) collective-permute-start(bf16[4,272,384]{2,1,0:T(8,128)(2,1)} %slice.3), channel_id=1, source_target_pairs={{0,32},{32,64},{64,96},{96,128},{128,160},{160,192},{192,224},{224... | collective-permute-start | bytes 2506760 | tf_op jit(solution)/shard_map/ppermute | solution.py:362
  52.0 29.9 %collective-permute-start.6 = (f32[192,128]{1,0:T(8,128)S(1)}, f32[192,128]{1,0:T(8,128)S(1)}, u32[]{:S(2)}, u32[]{:S(2)}) collective-permute-start(f32[192,128]{1,0:T(8,128)S(1)} %get-tuple-element.42.map_ref), channel_id=1, source_target_pairs={{256,384},{257,385},{258,386},{259,387},{260,388},{261,389},{262,3... | collective-permute-start | bytes 294920 | tf_op jit(solution)/shard_map/ppermute | solution.py:360
  53.6 15.7 %collective-permute-start.5 = (f32[64,128]{1,0:T(8,128)S(1)}, f32[64,128]{1,0:T(8,128)S(1)}, u32[]{:S(2)}, u32[]{:S(2)}) collective-permute-start(f32[64,128]{1,0:T(8,128)S(1)} %shard_map.134), channel_id=1, source_target_pairs={{128,384},{129,385},{130,386},{131,387},{132,388},{133,389},{134,3... | collective-permute-start | bytes 98312 | tf_op jit(solution)/shard_map/ppermute | solution.py:365
  54.9 14.4 %collective-permute-start.4 = (f32[64,128]{1,0:T(8,128)S(1)}, f32[64,128]{1,0:T(8,128)S(1)}, u32[]{:S(2)}, u32[]{:S(2)}) collective-permute-start(f32[64,128]{1,0:T(8,128)S(1)} %shard_map.134), channel_id=1, source_target_pairs={{128,256},{129,257},{130,258},{131,259},{132,260},{133,261},{134,2... | collective-permute-start | bytes 98312 | tf_op jit(solution)/shard_map/ppermute | solution.py:364
  83.2 12.2 %collective-permute-start.7 = (f32[64,128]{1,0:T(8,128)S(1)}, f32[64,128]{1,0:T(8,128)S(1)}, u32[]{:S(2)}, u32[]{:S(2)}) collective-permute-start(f32[64,128]{1,0:T(8,128)S(1)} %get-tuple-element.45), channel_id=1, source_target_pairs={{0,32},{32,64},{64,96},{96,0},{1,33},{33,65},{65,97},{97,1},{2,34}... | collective-permute-start | bytes 98312 | tf_op jit(solution)/shard_map/ppermute | solution.py:291
  87.9 7.5 %collective-permute-start.8 = (f32[64,128]{1,0:T(8,128)S(1)}, f32[64,128]{1,0:T(8,128)S(1)}, u32[]{:S(2)}, u32[]{:S(2)}) collective-permute-start(f32[64,128]{1,0:T(8,128)S(1)} %get-tuple-element.46), channel_id=1, source_target_pairs={{0,64},{32,96},{64,0},{96,32},{1,65},{33,97},{65,1},{97,33},{2,66}... | collective-permute-start | bytes 98312 | tf_op jit(solution)/shard_map/ppermute | solution.py:291
  93.5 7.6 %collective-permute-start.9 = (f32[64,128]{1,0:T(8,128)S(1)}, f32[64,128]{1,0:T(8,128)S(1)}, u32[]{:S(2)}, u32[]{:S(2)}) collective-permute-start(f32[64,128]{1,0:T(8,128)S(1)} %get-tuple-element.47), channel_id=1, source_target_pairs={{0,96},{32,0},{64,32},{96,64},{1,97},{33,1},{65,33},{97,65},{2,98}... | collective-permute-start | bytes 98312 | tf_op jit(solution)/shard_map/ppermute | solution.py:291
  102.3 20.8 %all-to-all-start.1 = ((f32[4,128,256]{2,1,0:T(8,128)}), f32[4,128,256]{2,1,0:T(8,128)S(1)}, u32[]{:S(2)}, u32[]{:S(2)}) async-start(f32[4,128,256]{2,1,0:T(8,128)} %shard_map.136), calls=%async_computation.1 | async-start | bytes 1048576 | tf_op jit(solution)/shard_map/all_to_all | solution.py:387
  111.2 19.0 %collective-permute-start.11 = (bf16[256,256]{1,0:T(8,128)(2,1)}, bf16[256,256]{1,0:T(8,128)(2,1)S(1)}, u32[]{:S(2)}, u32[]{:S(2)}) collective-permute-start(bf16[256,256]{1,0:T(8,128)(2,1)} %get-tuple-element.59), channel_id=1, source_target_pairs={{0,8},{8,16},{16,24},{24,0},{1,9},{9,17},{17,25},{25,1},{2,10},{10... | collective-permute-start | bytes 393224 | tf_op jit(solution)/shard_map/ppermute | solution.py:291
  115.2 15.1 %collective-permute-start.12 = (bf16[256,256]{1,0:T(8,128)(2,1)}, bf16[256,256]{1,0:T(8,128)(2,1)S(1)}, u32[]{:S(2)}, u32[]{:S(2)}) collective-permute-start(bf16[256,256]{1,0:T(8,128)(2,1)} %get-tuple-element.60), channel_id=1, source_target_pairs={{0,16},{8,24},{16,0},{24,8},{1,17},{9,25},{17,1},{25,9},{2,18},{10... | collective-permute-start | bytes 393224 | tf_op jit(solution)/shard_map/ppermute | solution.py:291
  119.7 10.5 %collective-permute-start.13 = (bf16[256,256]{1,0:T(8,128)(2,1)S(1)}, bf16[256,256]{1,0:T(8,128)(2,1)S(1)}, u32[]{:S(2)}, u32[]{:S(2)}) collective-permute-start(bf16[256,256]{1,0:T(8,128)(2,1)S(1)} %get-tuple-element.61), channel_id=1, source_target_pairs={{0,24},{8,0},{16,8},{24,16},{1,25},{9,1},{17,9},{25,17},{2,26},{10... | collective-permute-start | bytes 393224 | tf_op jit(solution)/shard_map/ppermute | solution.py:291
  123.1 1.2 copy-start.1
  125.6 10.2 %copy-start.2 = (f32[4,256]{1,0:T(4,128)S(1)}, f32[4,256]{1,0:T(4,128)}, u32[]{:S(2)}) copy-start(f32[4,256]{1,0:T(4,128)} %gain_ref.1) | copy-start | bytes 12292
  125.6 10.2 %all-to-all-start.2 = ((f32[8,8,256]{2,1,0:T(8,128)}), f32[8,8,256]{2,1,0:T(8,128)S(1)}, u32[]{:S(2)}, u32[]{:S(2)}) async-start(f32[8,8,256]{2,1,0:T(8,128)} %bitcast.7), calls=%async_computation.2 | async-start | bytes 131072 | tf_op jit(solution)/shard_map/all_to_all | solution.py:391

commit v5 on v2

--- a/solution.py
+++ b/solution.py
@@ -13,7 +13,6 @@
 WINDOW = 2048
 PART = VD // 4
 MARK_ROWS = 16
-VMEM_BYTES = 48 * 2**20
 
 SEQ = ("zh", "zl", "x")
 f32 = jnp.float32
@@ -40,7 +39,7 @@
     return dot(ah, b) + dot(al, b)
 
 
-def call(body, out_shape, scalars=0, inputs=1, scratch=(), flops=1e7):
+def call(body, out_shape, scalars=0, inputs=1, scratch=(), flops=1e7, mib=8):
     whole = pl.BlockSpec(memory_space=pltpu.VMEM)
     small = pl.BlockSpec(memory_space=pltpu.SMEM)
     return pl.pallas_call(
@@ -50,12 +49,12 @@
         out_shape=out_shape,
         scratch_shapes=list(scratch),
         cost_estimate=pl.CostEstimate(flops=int(flops), bytes_accessed=10**6, transcendentals=0),
-        compiler_params=pltpu.CompilerParams(vmem_limit_bytes=VMEM_BYTES),
+        compiler_params=pltpu.CompilerParams(vmem_limit_bytes=mib * 2**20),
     )
 
 
 def block_terms(
-    count_ref, q_ref, k_ref, v_ref, gate_ref, beta_ref, map_ref, new_ref, mixing_ref, carry_ref, x_ref, a_ref
+    count_ref, q_ref, k_ref, v_ref, gate_ref, beta_ref, map_ref, carry_ref, local_ref, x_ref, a_ref
 ):
     count = count_ref[0]
     row = lax.broadcasted_iota(jnp.int32, (ROWS, ROWS), 0)
@@ -81,23 +80,31 @@
         q = q_ref[h]
         wide = q.astype(f32)
         q_col = lax.rsqrt(jnp.sum(wide * wide, axis=1, keepdims=True) + 1e-6)
-        mixing_ref[h] = (q_col * decay) * (dot(q, k, ((1,), (1,))) * k_row)
+        local_ref[h] = (q_col * decay) * (dot(q, k, ((1,), (1,))) * k_row)
         kept.append((log_col, log_row, beta, k_col, k_row, q_col))
     step = 1
     while (2 << step) <= ROWS:
         m = 1 << step
         for h in range(HEADS):
-            x = x_ref[h]
             if m < 64:
+                x = x_ref[h]
                 below = ((row >> (step + 1)) == (col >> (step + 1))) & ((row >> step) != (col >> step))
-                x_ref[h] = x - dot3(dot3(x, jnp.where(below, a_ref[h], 0.0)), x)
+                coarse = x.astype(bf16)
+                between = jnp.where(below, a_ref[h], 0.0).astype(bf16)
+                x_ref[h] = x - dot(dot(coarse, between).astype(bf16), coarse)
             else:
                 for s in range(0, ROWS, 2 * m):
-                    first = x[s : s + m, s : s + m]
-                    second = x[s + m : s + 2 * m, s + m : s + 2 * m]
-                    between = a_ref[h, s + m : s + 2 * m, s : s + m]
-                    x_ref[h, s + m : s + 2 * m, s : s + m] = -dot3(second, dot3(between, first))
+                    first = x_ref[h, s : s + m, s : s + m].astype(bf16)
+                    second = x_ref[h, s + m : s + 2 * m, s + m : s + 2 * m].astype(bf16)
+                    between = a_ref[h, s + m : s + 2 * m, s : s + m].astype(bf16)
+                    x_ref[h, s + m : s + 2 * m, s : s + m] = -dot(
+                        second, dot(between, first).astype(bf16)
+                    )
         step += 1
+    for h in range(HEADS):
+        x = x_ref[h]
+        left = jnp.where(eye, 1.0, 0.0) - x - dot3(a_ref[h], x)
+        x_ref[h] = x + dot(x.astype(bf16), left.astype(bf16))
     row_k = lax.broadcasted_iota(jnp.int32, (KD, KD), 0)
     col_k = lax.broadcasted_iota(jnp.int32, (KD, KD), 1)
     for h in range(HEADS):
@@ -112,14 +119,8 @@
         update = dot(k, high, ((0,), (0,))) + dot(k, low, ((0,), (0,)))
         map_ref[h, :, :KD] = jnp.where(row_k == col_k, jnp.exp(last), 0.0) - update[:, :KD]
         map_ref[h, :, KD:] = update[:, KD:]
-        new_ref[h] = new
-        carry_ref[h] = (jnp.exp(log_col) * q_col) * q_ref[h].astype(f32)
-
-
-def row_terms(new_ref, mixing_ref, straight_ref, carry_ref, local_ref):
-    for h in range(HEADS):
-        mixed = dot3(mixing_ref[h], new_ref[h])
-        carry_ref[h] = straight_ref[h] - mixed[:, :KD]
+        mixed = dot3(local_ref[h], new)
+        carry_ref[h] = (jnp.exp(log_col) * q_col) * q_ref[h].astype(f32) - mixed[:, :KD]
         local_ref[h] = mixed[:, KD:]
 
 
@@ -298,18 +299,14 @@
         attn_position.reshape(1, ROWS),
     )
     here = lax.all_to_all(packed, "x", 0, 0, tiled=True)
-    maps, new, mixing, straight = call(
+    maps, carry, local = call(
         block_terms,
-        (
-            shape_of(HEADS, KD, KD + VD),
-            shape_of(HEADS, ROWS, KD + VD),
-            shape_of(HEADS, ROWS, ROWS),
-            shape_of(HEADS, ROWS, KD),
-        ),
+        (shape_of(HEADS, KD, KD + VD), shape_of(HEADS, ROWS, KD), shape_of(HEADS, ROWS, VD)),
         scalars=1,
         inputs=5,
         scratch=[pltpu.VMEM((HEADS, ROWS, ROWS), f32)] * 2,
         flops=8e9,
+        mib=16,
     )(
         delta_count,
         heads_first(delta_query),
@@ -318,12 +315,9 @@
         delta_gate.T,
         delta_beta.T,
     )
-    maps, here, past = lax.optimization_barrier((maps, here, here[:, :, : KD + VD]))
-    past = lax.ppermute(past, ("zh", "zl"), [(i, i + 1) for i in range(15)])
+    maps, here = lax.optimization_barrier((maps, here))
+    past = lax.ppermute(here[:, :, : KD + VD], ("zh", "zl"), [(i, i + 1) for i in range(15)])
     exchanged = lax.all_to_all(maps, "x", 0, 0, tiled=True)
-    carry, local = call(
-        row_terms, (shape_of(HEADS, ROWS, KD), shape_of(HEADS, ROWS, VD)), inputs=3, flops=2e9
-    )(new, mixing, straight)
     plane_prefix, plane_total = call(
         compose_plane, (shape_of(3, KD, KD + VD), shape_of(4, KD + PART, KD))
     )(exchanged)
@@ -342,7 +336,7 @@
         place, first, one, two, third, group_prefix
     )
     planes, past = lax.optimization_barrier((planes, past))
-    attn_heads = call(attend, shape_of(4, ROWS, VD, kind=bf16), inputs=2, flops=8e9)(here, past)
+    attn_heads = call(attend, shape_of(4, ROWS, VD, kind=bf16), inputs=2, flops=8e9, mib=16)(here, past)
     parts = lax.all_to_all(planes, "zl", 0, 0, tiled=True)
     returned = call(plane_states, shape_of(4, 2 * KD + ROWS, VD, kind=bf16), inputs=3)(
         parts, plane_prefix, attn_heads

time: 123 us -> 121 us (0.984)
  blocking collectives: 13.8 us -> 28.3 us
  waiting for transfers between devices: 42 us -> 35.9 us
  starting transfers between devices: 31.5 us -> 26.6 us
  local copies, waits for them, and re-layouts: 12.2 us -> 7.43 us
    all_to_all x0 -> x1, blocking collectives: none -> 14.6 us  [shards(): states = lax.all_to_all(returned, 'x', 0, 0, tiled=True)]
    all_to_all x1 -> x0, waiting for transfers between devices: 7.5 us -> none  [shards(): states = lax.all_to_all(returned, 'x', 0, 0, tiled=True)]
    unnamed x38 -> x30, local copies, waits for them, and re-layouts: 11.1 us -> 6.25 us
    all_to_all x1 -> x0, starting transfers between devices: 3.65 us -> none  [shards(): states = lax.all_to_all(returned, 'x', 0, 0, tiled=True)]
    all_to_all x1, waiting for transfers between devices: 4.44 us -> 7.4 us  [shards(): here = lax.all_to_all(packed, 'x', 0, 0, tiled=True)]
    all_to_all x1, starting transfers between devices: 8.36 us -> 7.02 us  [shards(): parts = lax.all_to_all(planes, 'zl', 0, 0, tiled=True)]
    pallas_call x2 -> x1, Pallas kernels: 4 us -> 4.16 us  [shards(): call(attend, shape_of(4, ROWS, VD, kind=bf16), inputs=2, flops=8000000000...]
  transfers between devices with their start and end apart: 10 -> 9, of which waited for: 6 -> 4; matrix products, arithmetic and copies ran while one was open for 1% -> 2% of each run, Pallas kernels for 11% -> 12%
where the time goes in v5:
time: 121 us; the launch traced here: 120 us
  waiting for transfers between devices  35.9 us (30%)
  blocking collectives  28.3 us (23%)
  starting transfers between devices  26.6 us (22%)
  Pallas kernels  19.5 us (16%)
  local copies, waits for them, and re-layouts  7.43 us (6%)
  between operations  2.22 us (2%)
    ppermute x1, waiting for transfers between devices, shards(): two = lax.ppermute(pair, 'zh', [(1, 3)])  17.7 us
    all_to_all x1, blocking collectives, shards(): states = lax.all_to_all(returned, 'x', 0, 0, tiled=True)  14.6 us
    all_to_all x1, blocking collectives, shards(): exchanged = lax.all_to_all(maps, 'x', 0, 0, tiled=True)  13.8 us
    all_to_all x1, waiting for transfers between devices, shards(): here = lax.all_to_all(packed, 'x', 0, 0, tiled=True)  7.4 us
    all_to_all x1, starting transfers between devices, shards(): parts = lax.all_to_all(planes, 'zl', 0, 0, tiled=True)  7.02 us
    pallas_call x1, Pallas kernels, shards(): call(block_terms, (shape_of(HEADS, KD, KD + VD), shape_of(HEADS, ROWS, KD...  6.73 us
    all_to_all x1, waiting for transfers between devices, shards(): gathered = lax.all_to_all(plane_total, 'zl', 0, 0, tiled=True)  6.4 us
    unnamed x30, local copies, waits for them, and re-layouts  6.25 us
  transfers between devices with their start and end apart: 9, of which 4 were waited for; matrix products, arithmetic and copies ran while one was open for 2% of the time, Pallas kernels for 12%

profile of v5, /device:TPU:480, one launch (start us, length us, event | category | flops | bytes accessed | tf_op | source)
XLA Modules:
  0.0 119.9 jit_solution(6485185537633914460)
XLA Ops:
  0.6 0.0 copy-start.10
  0.6 0.0 copy-start.9
  0.7 0.0 copy-start.5
  1.4 1.1 copy.28
  2.5 0.1 copy_bitcast_fusion.2
  2.6 1.1 shard_map.132
  3.7 4.4 %all-to-all-start = ((bf16[4,272,512]{2,1,0:T(8,128)(2,1)}), bf16[4,272,512]{2,1,0:T(8,128)(2,1)S(1)}, u32[]{:S(2)}, u32[]{:S(2)}) async-start(bf16[4,272,512]{2,1,0:T(8,128)(2,1)} %shard_map.132), calls=%async_computation | async-start | bytes 2228224 | tf_op jit(solution)/shard_map/all_to_all | solution.py:301
  8.2 0.0 copy-start.7
  8.2 0.1 copy_bitcast_fusion.4
  8.9 0.1 copy.29
  9.0 6.7 %shard_map.131 = (f32[4,128,384]{2,1,0:T(8,128)S(1)}, f32[4,256,128]{2,1,0:T(8,128)S(1)}, f32[4,256,256]{2,1,0:T(8,128)S(1)}) custom-call(s32[1]{0:T(128)S(6)} %copy.30.count_ref, bf16[4,256,128]{2,1,0:T(8,128)(2,1)S(1)} %get-tuple-element.33.q_ref, bf16[4,256,128]{2,1,0:T(8,128)(2,1)S(1)} %get-tuple-element.32.k_ref, bf16[4,256,256]{2,1,0:T(8,128)(2,1)S(1)} %bitcast.25, ...), custom_call_target="tpu_custom_call" | custom-call | flops 8000000000 | bytes 1000000 | tf_op jit(solution)/shard_map/pallas_call | solution.py:302
  15.8 0.0 copy-start
  15.8 0.8 copy-done
  16.6 7.4 %all-to-all-done.here_ref = bf16[4,272,512]{2,1,0:T(8,128)(2,1)S(1)} async-done(((bf16[4,272,512]{2,1,0:T(8,128)(2,1)}), bf16[4,272,512]{2,1,0:T(8,128)(2,1)S(1)}, u32[]{:S(2)}, u32[]{:S(2)}) %all-to-all-start) | async-done | bytes 1114144 | tf_op jit(solution)/shard_map/all_to_all | solution.py:301
  24.0 13.8 %all_to_all.36.maps_ref = f32[4,128,384]{2,1,0:T(8,128)S(1)} all-to-all(f32[4,128,384]{2,1,0:T(8,128)S(1)} %get-tuple-element.19), channel_id=1, replica_groups=mesh['zh'=4,'zl'=4,'x'=4,'head'=8] {'x'}, dimensions={0} | all-to-all | bytes 1572864 | tf_op jit(solution)/shard_map/all_to_all | solution.py:320
  37.7 1.6 %shard_map.133 = (f32[3,128,384]{2,1,0:T(8,128)S(1)}, f32[4,192,128]{2,1,0:T(8,128)}) custom-call(f32[4,128,384]{2,1,0:T(8,128)S(1)} %all_to_all.36.maps_ref), custom_call_target="tpu_custom_call" | custom-call | flops 10000000 | bytes 1000000 | tf_op jit(solution)/shard_map/pallas_call | solution.py:321
  39.3 5.3 %all-to-all-start.2 = ((f32[4,192,128]{2,1,0:T(8,128)}), f32[4,192,128]{2,1,0:T(8,128)S(1)}, u32[]{:S(2)}, u32[]{:S(2)}) async-start(f32[4,192,128]{2,1,0:T(8,128)} %get-tuple-element.20), calls=%async_computation.2 | async-start | bytes 786432 | tf_op jit(solution)/shard_map/all_to_all | solution.py:324
  44.6 1.0 slice.6
  45.6 1.3 %collective-permute-start.4 = (bf16[4,272,384]{2,1,0:T(8,128)(2,1)}, bf16[4,272,384]{2,1,0:T(8,128)(2,1)}, u32[]{:S(2)}, u32[]{:S(2)}) collective-permute-start(bf16[4,272,384]{2,1,0:T(8,128)(2,1)} %slice.6), channel_id=1, source_target_pairs={{0,32},{32,64},{64,96},{96,128},{128,160},{160,192},{192,224},{224... | collective-permute-start | bytes 2506760 | tf_op jit(solution)/shard_map/ppermute | solution.py:319
  46.9 6.4 %all-to-all-done.2.maps_ref = f32[4,192,128]{2,1,0:T(8,128)S(1)} async-done(((f32[4,192,128]{2,1,0:T(8,128)}), f32[4,192,128]{2,1,0:T(8,128)S(1)}, u32[]{:S(2)}, u32[]{:S(2)}) %all-to-all-start.2) | async-done | bytes 393248 | tf_op jit(solution)/shard_map/all_to_all | solution.py:324
  53.3 1.4 %shard_map.134 = (f32[3,128,192]{2,1,0:T(8,128)S(1)}, f32[192,128]{1,0:T(8,128)}, f32[64,128]{1,0:T(8,128)S(1)}) custom-call(f32[4,192,128]{2,1,0:T(8,128)S(1)} %all-to-all-done.2.maps_ref), custom_call_target="tpu_custom_call" | custom-call | flops 10000000 | bytes 1000000 | tf_op jit(solution)/shard_map/pallas_call | solution.py:325
  54.7 1.3 %collective-permute-start.3 = (f32[192,128]{1,0:T(8,128)}, f32[192,128]{1,0:T(8,128)S(1)}, u32[]{:S(2)}, u32[]{:S(2)}) collective-permute-start(f32[192,128]{1,0:T(8,128)} %get-tuple-element.22.map_ref), channel_id=1, source_target_pairs={{256,384},{257,385},{258,386},{259,387},{260,388},{261,389},{262,3... | collective-permute-start | bytes 294920 | tf_op jit(solution)/shard_map/ppermute | solution.py:330
  56.0 0.7 collective-permute-start
  56.7 0.0 collective-permute-done.earlier_ref.first_ref
  56.7 1.2 shard_map.135
  57.9 1.3 %collective-permute-start.2 = (f32[64,128]{1,0:T(8,128)S(1)}, f32[64,128]{1,0:T(8,128)S(1)}, u32[]{:S(2)}, u32[]{:S(2)}) collective-permute-start(f32[64,128]{1,0:T(8,128)S(1)} %shard_map.135), channel_id=1, source_target_pairs={{128,384},{129,385},{130,386},{131,387},{132,388},{133,389},{134,3... | collective-permute-start | bytes 98312 | tf_op jit(solution)/shard_map/ppermute | solution.py:333
  59.2 0.7 collective-permute-start.1
  59.9 17.7 %collective-permute-done.2.two_ref = f32[64,128]{1,0:T(8,128)S(1)} collective-permute-done((f32[64,128]{1,0:T(8,128)S(1)}, f32[64,128]{1,0:T(8,128)S(1)}, u32[]{:S(2)}, u32[]{:S(2)}) %collective-permute-start.2) | collective-permute-done | bytes 32800 | tf_op jit(solution)/shard_map/ppermute | solution.py:333
  77.5 0.0 collective-permute-done.1.one_ref
  77.5 0.0 collective-permute-done.3.third_ref
  77.5 1.3 %shard_map.136 = f32[4,64,128]{2,1,0:T(8,128)} custom-call(s32[1]{0:T(128)} %bitcast.5.place_ref, f32[64,128]{1,0:T(8,128)S(1)} %collective-permute-done.earlier_ref.first_ref, f32[64,128]{1,0:T(8,128)S(1)} %collective-permute-done.1.one_ref, f32[64,128]{1,0:T(8,128)S(1)} %collective-permute-done.2.two_ref, f32[192,128]{1,0:T(8,128)S(1)} %collective-permute-done.3.third_ref, ...), custom_call_target="tpu_custom_call" | custom-call | flops 10000000 | bytes 1000000 | tf_op jit(solution)/shard_map/pallas_call | solution.py:335
  78.9 0.0 collective-permute-done.4.past_ref
  78.9 7.0 %all-to-all-start.3 = ((f32[4,64,128]{2,1,0:T(8,128)}), f32[4,64,128]{2,1,0:T(8,128)S(1)}, u32[]{:S(2)}, u32[]{:S(2)}) async-start(f32[4,64,128]{2,1,0:T(8,128)} %shard_map.136), calls=%async_computation.3 | async-start | bytes 262144 | tf_op jit(solution)/shard_map/all_to_all | solution.py:340
  85.9 4.2 %shard_map.137.attn_ref = bf16[4,256,256]{2,1,0:T(8,128)(2,1)S(1)} custom-call(bf16[4,272,512]{2,1,0:T(8,128)(2,1)S(1)} %all-to-all-done.here_ref, bf16[4,272,384]{2,1,0:T(8,128)(2,1)} %collective-permute-done.4.past_ref), custom_call_target="tpu_custom_call" | custom-call | flops 8000000000 | bytes 1000000 | tf_op jit(solution)/shard_map/pallas_call | solution.py:339
  90.1 0.0 copy-start.2
  90.1 0.8 copy-done.2
  90.9 0.0 all-to-all-done.3.parts_ref
  90.9 1.0 copy-done.3
  91.9 0.5 shard_map.138
  92.4 0.0 copy-start.1
  92.4 14.6 %all_to_all.37.state_ref = bf16[4,512,256]{2,1,0:T(8,128)(2,1)S(1)} all-to-all(bf16[4,512,256]{2,1,0:T(8,128)(2,1)S(1)} %shard_map.138), channel_id=1, replica_groups=mesh['zh'=4,'zl'=4,'x'=4,'head'=8] {'x'}, dimensions={0} | all-to-all | bytes 2097152 | tf_op jit(solution)/shard_map/all_to_all | solution.py:344
  107.0 1.3 %shard_map.139 = (f32[4,256,256]{2,1,0:T(8,128)S(1)}, f32[64,256]{1,0:T(8,128)}) custom-call(f32[4,256,128]{2,1,0:T(8,128)S(1)} %copy-done.1, f32[4,256,256]{2,1,0:T(8,128)S(1)} %get-tuple-element.17.local_ref, bf16[4,512,256]{2,1,0:T(8,128)(2,1)S(1)} %all_to_all.37.state_ref), custom_call_target="tpu_custom_call" | custom-call | flops 10000000 | bytes 1000000 | tf_op jit(solution)/shard_map/pallas_call | solution.py:345
  108.2 4.6 %all-to-all-start.5 = ((f32[8,8,256]{2,1,0:T(8,128)}), f32[8,8,256]{2,1,0:T(8,128)S(1)}, u32[]{:S(2)}, u32[]{:S(2)}) async-start(f32[8,8,256]{2,1,0:T(8,128)} %bitcast.10), calls=%async_computation.5 | async-start | bytes 131072 | tf_op jit(solution)/shard_map/all_to_all | solution.py:348
  112.9 1.2 %copy.21 = bf16[256,4,256]{2,1,0:T(4,128)(2,1)} copy(bf16[256,4,256]{2,0,1:T(8,128)(2,1)S(1)} %slice_bitcast_fusion) | data formatting | bytes 1048576
  114.1 4.4 %all-to-all-done.5 = f32[8,8,256]{2,1,0:T(8,128)S(1)} async-done(((f32[8,8,256]{2,1,0:T(8,128)}), f32[8,8,256]{2,1,0:T(8,128)S(1)}, u32[]{:S(2)}, u32[]{:S(2)}) %all-to-all-start.5) | async-done | bytes 65568 | tf_op jit(solution)/shard_map/all_to_all | solution.py:348
  118.5 0.0 copy-done.4
  118.5 0.2 shard_map.140
  118.7 1.2 %copy.20 = bf16[256,4,256]{2,1,0:T(4,128)(2,1)} copy(bf16[256,4,256]{2,0,1:T(8,128)(2,1)S(1)} %bitcast.24) | data formatting | bytes 1048576
  (16 shorter events, 0.1 us)
Async XLA Ops:
  0.6 1.8 %copy-start.10 = (bf16[256,4,128]{2,1,0:T(4,128)(2,1)S(1)}, bf16[256,4,128]{2,1,0:T(4,128)(2,1)}, u32[]{:S(2)}) copy-start(bf16[256,4,128]{2,1,0:T(4,128)(2,1)} %param.20) | copy-start | bytes 786436
  0.6 1.8 %copy-start.9 = (bf16[256,4,128]{2,1,0:T(4,128)(2,1)S(1)}, bf16[256,4,128]{2,1,0:T(4,128)(2,1)}, u32[]{:S(2)}) copy-start(bf16[256,4,128]{2,1,0:T(4,128)(2,1)} %param.19) | copy-start | bytes 786436
  0.7 1.9 %copy-start.5 = (s32[256]{0:T(256)S(1)}, s32[256]{0:T(256)}, u32[]{:S(2)}) copy-start(s32[256]{0:T(256)} %param.22) | copy-start | bytes 3076
  3.7 4.4 %copy-start.11 = (bf16[256,4,128]{2,1,0:T(4,128)(2,1)S(1)}, bf16[256,4,128]{2,1,0:T(4,128)(2,1)}, u32[]{:S(2)}) copy-start(bf16[256,4,128]{2,1,0:T(4,128)(2,1)} %param.13) | copy-start | bytes 786436
  3.7 4.4 %copy-start.12 = (bf16[256,4,128]{2,1,0:T(4,128)(2,1)S(1)}, bf16[256,4,128]{2,1,0:T(4,128)(2,1)}, u32[]{:S(2)}) copy-start(bf16[256,4,128]{2,1,0:T(4,128)(2,1)} %param.12) | copy-start | bytes 786436
  3.7 5.2 %copy-start.8 = (bf16[256,4,256]{2,1,0:T(4,128)(2,1)S(1)}, bf16[256,4,256]{2,1,0:T(4,128)(2,1)}, u32[]{:S(2)}) copy-start(bf16[256,4,256]{2,1,0:T(4,128)(2,1)} %param.14) | copy-start | bytes 1572868
  3.7 20.2 %all-to-all-start = ((bf16[4,272,512]{2,1,0:T(8,128)(2,1)}), bf16[4,272,512]{2,1,0:T(8,128)(2,1)S(1)}, u32[]{:S(2)}, u32[]{:S(2)}) async-start(bf16[4,272,512]{2,1,0:T(8,128)(2,1)} %shard_map.132), calls=%async_computation | async-start | bytes 2228224 | tf_op jit(solution)/shard_map/all_to_all | solution.py:301
  8.2 0.8 copy-start.6
  8.2 0.8 copy-start.7
  15.8 0.8 copy-start
  39.3 14.0 %all-to-all-start.2 = ((f32[4,192,128]{2,1,0:T(8,128)}), f32[4,192,128]{2,1,0:T(8,128)S(1)}, u32[]{:S(2)}, u32[]{:S(2)}) async-start(f32[4,192,128]{2,1,0:T(8,128)} %get-tuple-element.20), calls=%async_computation.2 | async-start | bytes 786432 | tf_op jit(solution)/shard_map/all_to_all | solution.py:324
  45.6 33.3 %collective-permute-start.4 = (bf16[4,272,384]{2,1,0:T(8,128)(2,1)}, bf16[4,272,384]{2,1,0:T(8,128)(2,1)}, u32[]{:S(2)}, u32[]{:S(2)}) collective-permute-start(bf16[4,272,384]{2,1,0:T(8,128)(2,1)} %slice.6), channel_id=1, source_target_pairs={{0,32},{32,64},{64,96},{96,128},{128,160},{160,192},{192,224},{224... | collective-permute-start | bytes 2506760 | tf_op jit(solution)/shard_map/ppermute | solution.py:319
  54.7 22.8 %collective-permute-start.3 = (f32[192,128]{1,0:T(8,128)}, f32[192,128]{1,0:T(8,128)S(1)}, u32[]{:S(2)}, u32[]{:S(2)}) collective-permute-start(f32[192,128]{1,0:T(8,128)} %get-tuple-element.22.map_ref), channel_id=1, source_target_pairs={{256,384},{257,385},{258,386},{259,387},{260,388},{261,389},{262,3... | collective-permute-start | bytes 294920 | tf_op jit(solution)/shard_map/ppermute | solution.py:330
  56.0 0.7 collective-permute-start
  57.9 19.6 %collective-permute-start.2 = (f32[64,128]{1,0:T(8,128)S(1)}, f32[64,128]{1,0:T(8,128)S(1)}, u32[]{:S(2)}, u32[]{:S(2)}) collective-permute-start(f32[64,128]{1,0:T(8,128)S(1)} %shard_map.135), channel_id=1, source_target_pairs={{128,384},{129,385},{130,386},{131,387},{132,388},{133,389},{134,3... | collective-permute-start | bytes 98312 | tf_op jit(solution)/shard_map/ppermute | solution.py:333
  59.2 18.3 %collective-permute-start.1 = (f32[64,128]{1,0:T(8,128)S(1)}, f32[64,128]{1,0:T(8,128)S(1)}, u32[]{:S(2)}, u32[]{:S(2)}) collective-permute-start(f32[64,128]{1,0:T(8,128)S(1)} %shard_map.135), channel_id=1, source_target_pairs={{128,256},{129,257},{130,258},{131,259},{132,260},{133,261},{134,2... | collective-permute-start | bytes 98312 | tf_op jit(solution)/shard_map/ppermute | solution.py:332
  78.9 12.0 %all-to-all-start.3 = ((f32[4,64,128]{2,1,0:T(8,128)}), f32[4,64,128]{2,1,0:T(8,128)S(1)}, u32[]{:S(2)}, u32[]{:S(2)}) async-start(f32[4,64,128]{2,1,0:T(8,128)} %shard_map.136), calls=%async_computation.3 | async-start | bytes 262144 | tf_op jit(solution)/shard_map/all_to_all | solution.py:340
  90.1 0.8 copy-start.2
  90.9 1.0 copy-start.3
  92.4 14.6 %copy-start.1 = (f32[4,256,128]{2,1,0:T(8,128)S(1)}, f32[4,256,128]{2,1,0:T(8,128)}, u32[]{:S(2)}) copy-start(f32[4,256,128]{2,1,0:T(8,128)} %copy-done) | copy-start | bytes 1572868
  108.2 10.2 %copy-start.4 = (f32[4,256]{1,0:T(4,128)S(1)}, f32[4,256]{1,0:T(4,128)}, u32[]{:S(2)}) copy-start(f32[4,256]{1,0:T(4,128)} %gain_ref.1) | copy-start | bytes 12292
  108.2 10.2 %all-to-all-start.5 = ((f32[8,8,256]{2,1,0:T(8,128)}), f32[8,8,256]{2,1,0:T(8,128)S(1)}, u32[]{:S(2)}, u32[]{:S(2)}) async-start(f32[8,8,256]{2,1,0:T(8,128)} %bitcast.10), calls=%async_computation.5 | async-start | bytes 131072 | tf_op jit(solution)/shard_map/all_to_all | solution.py:348

commit v6 on v5

--- a/solution.py
+++ b/solution.py
@@ -13,6 +13,7 @@
 WINDOW = 2048
 PART = VD // 4
 MARK_ROWS = 16
+BEFORE = 2 * KD + VD
 
 SEQ = ("zh", "zl", "x")
 f32 = jnp.float32
@@ -138,17 +139,37 @@
     return jnp.concatenate([state[:, :KD], state[:, KD:] + offset], axis=1)
 
 
-def compose_plane(maps_ref, before_ref, send_ref):
+def pick(index, choices):
+    picked = choices[0]
+    for i in range(1, len(choices)):
+        picked = jnp.where(index == i, choices[i], picked)
+    return picked
+
+
+def ahead(place, shift):
+    return lax.rem(place + shift, 4)
+
+
+def compose_plane(place_ref, maps_ref, before_ref, *send_refs):
     state = maps_ref[0]
     for i in range(1, 4):
         before_ref[i - 1] = state
         state = then(state, maps_ref[i, :, :KD], maps_ref[i, :, KD:])
-    for i in range(4):
-        send_ref[i, :KD, :] = state[:, :KD]
-        send_ref[i, KD:, :] = fold(state[:, KD + i * PART : KD + (i + 1) * PART])
-
-
-def compose_group(maps_ref, before_ref, total_ref, offset_ref):
+    quarters = [fold(state[:, KD + i * PART : KD + (i + 1) * PART]) for i in range(4)]
+    for d, send_ref in enumerate(send_refs):
+        send_ref[:KD, :] = state[:, :KD]
+        send_ref[KD:, :] = pick(ahead(place_ref[0], d), quarters)
+
+
+def in_order(place, refs, ordered_ref):
+    for d, ref in enumerate(refs):
+        ordered_ref[pl.ds(ahead(place, 4 - d), 1)] = ref[...][None]
+
+
+def compose_group(
+    place_ref, own_ref, one_ref, two_ref, three_ref, before_ref, total_ref, offset_ref, maps_ref
+):
+    in_order(place_ref[0], (own_ref, one_ref, two_ref, three_ref), maps_ref)
     state = jnp.concatenate([maps_ref[0, :KD, :], unfold(maps_ref[0, KD:, :])], axis=1)
     for i in range(1, 4):
         before_ref[i - 1] = state
@@ -217,7 +238,7 @@
         out_ref[h] = (raw_ref[h] * factor * gain_ref[h : h + 1, :]).astype(bf16)
 
 
-def pack_blocks(count_ref, key_ref, value_ref, query_ref, position_ref, out_ref):
+def pack_keys(count_ref, key_ref, value_ref, position_ref, out_ref):
     lane = lax.broadcasted_iota(jnp.int32, (1, ROWS), 1)
     marks = jnp.where(lane < count_ref[0], position_ref[...] + 1, 0)
     spot = lax.broadcasted_iota(jnp.int32, (MARK_ROWS, ROWS), 0)
@@ -225,32 +246,39 @@
     coded = coded.astype(f32).astype(bf16)
     for h in range(HEADS):
         out_ref[h, :ROWS, :KD] = key_ref[h]
-        out_ref[h, :ROWS, KD : KD + VD] = value_ref[h]
-        out_ref[h, :ROWS, KD + VD :] = query_ref[h]
+        out_ref[h, :ROWS, KD:] = value_ref[h]
         out_ref[h, ROWS:, :ROWS] = coded
-        out_ref[h, ROWS:, ROWS:] = jnp.zeros((MARK_ROWS, 2 * KD + VD - ROWS), bf16)
-
-
-def attend(here_ref, past_ref, out_ref):
+        out_ref[h, ROWS:, ROWS:] = jnp.zeros((MARK_ROWS, KD + VD - ROWS), bf16)
+
+
+def pack_heads(query_ref, keys_ref, past_ref, out_ref):
+    for h in range(HEADS):
+        out_ref[h, :, : KD + VD] = keys_ref[h]
+        out_ref[h, :ROWS, KD + VD : BEFORE] = query_ref[h]
+        out_ref[h, ROWS:, KD + VD : BEFORE] = jnp.zeros((MARK_ROWS, KD), bf16)
+        out_ref[h, :, BEFORE:] = past_ref[h]
+
+
+def attend(blocks_ref, out_ref):
     row = lax.broadcasted_iota(jnp.int32, (ROWS, ROWS), 0)
     col = lax.broadcasted_iota(jnp.int32, (ROWS, ROWS), 1)
 
-    def marks_of(ref, j):
-        coded = ref[j, ROWS : ROWS + MARK_ROWS, :ROWS].astype(f32)
+    def marks_of(start, j):
+        coded = blocks_ref[j, ROWS : ROWS + MARK_ROWS, start : start + ROWS].astype(f32)
         return coded[0:1, :] * 256.0 + coded[1:2, :]
 
-    marks = [marks_of(here_ref, j) for j in range(4)]
+    marks = [marks_of(0, j) for j in range(4)]
     here_marks = [jnp.where(m > 0.0, m, 1e9) for m in marks]
-    past_marks = [marks_of(past_ref, j) for j in range(4)]
+    past_marks = [marks_of(BEFORE, j) for j in range(4)]
     past_marks = [jnp.where(m > 0.0, m, 1e9) for m in past_marks]
     for j in range(4):
         query_marks = jnp.sum(jnp.where(row == col, marks[j], 0.0), axis=1, keepdims=True)
-        q = here_ref[j, :ROWS, KD + VD :]
-        sources = [(here_ref, i, here_marks[i]) for i in range(j + 1)]
-        sources += [(past_ref, i, past_marks[i]) for i in range(j, 4)]
+        q = blocks_ref[j, :ROWS, KD + VD : BEFORE]
+        sources = [(0, i, here_marks[i]) for i in range(j + 1)]
+        sources += [(BEFORE, i, past_marks[i]) for i in range(j, 4)]
         scores = []
-        for ref, i, key_marks in sources:
-            score = dot(q, ref[i, :ROWS, :KD], ((1,), (1,))) * KD**-0.5
+        for start, i, key_marks in sources:
+            score = dot(q, blocks_ref[i, :ROWS, start : start + KD], ((1,), (1,))) * KD**-0.5
             allowed = (key_marks <= query_marks) & (key_marks > query_marks - float(WINDOW))
             scores.append(jnp.where(allowed, score, -1e30))
         top = scores[0]
@@ -259,16 +287,24 @@
         top = jnp.max(top, axis=1, keepdims=True)
         weight_sum = jnp.zeros((ROWS, ROWS), f32)
         mixed = jnp.zeros((ROWS, VD), f32)
-        for score, (ref, i, key_marks) in zip(scores, sources):
+        for score, (start, i, key_marks) in zip(scores, sources):
             weights = jnp.exp(score - top)
             weight_sum = weight_sum + weights
-            mixed = mixed + dot(weights.astype(bf16), ref[i, :ROWS, KD : KD + VD])
+            values = blocks_ref[i, :ROWS, start + KD : start + KD + VD]
+            mixed = mixed + dot(weights.astype(bf16), values)
         mixed = mixed / jnp.sum(weight_sum, axis=1, keepdims=True)
         out_ref[j] = jnp.where(query_marks > 0.0, mixed, 0.0).astype(bf16)
 
 
 def heads_first(block):
     return jnp.swapaxes(block, 0, 1)
+
+
+def around(parts, axis):
+    return [
+        lax.ppermute(part, axis, [(i, (i + d) % 4) for i in range(4)]) if d else part
+        for d, part in enumerate(parts)
+    ]
 
 
 def shape_of(*dims, kind=f32):
@@ -289,16 +325,10 @@
     attn_position,
     attn_count,
 ):
-    packed = call(
-        pack_blocks, shape_of(HEADS, ROWS + MARK_ROWS, 2 * KD + VD, kind=bf16), scalars=1, inputs=4
-    )(
-        attn_count,
-        heads_first(attn_key),
-        heads_first(attn_value),
-        heads_first(attn_query),
-        attn_position.reshape(1, ROWS),
-    )
-    here = lax.all_to_all(packed, "x", 0, 0, tiled=True)
+    keys = call(
+        pack_keys, shape_of(HEADS, ROWS + MARK_ROWS, KD + VD, kind=bf16), scalars=1, inputs=3
+    )(attn_count, heads_first(attn_key), heads_first(attn_value), attn_position.reshape(1, ROWS))
+    past = lax.ppermute(keys, ("zh", "zl"), [(i, i + 1) for i in range(15)])
     maps, carry, local = call(
         block_terms,
         (shape_of(HEADS, KD, KD + VD), shape_of(HEADS, ROWS, KD), shape_of(HEADS, ROWS, VD)),
@@ -315,17 +345,27 @@
         delta_gate.T,
         delta_beta.T,
     )
-    maps, here = lax.optimization_barrier((maps, here))
-    past = lax.ppermute(here[:, :, : KD + VD], ("zh", "zl"), [(i, i + 1) for i in range(15)])
+    maps, attn_query = lax.optimization_barrier((maps, attn_query))
     exchanged = lax.all_to_all(maps, "x", 0, 0, tiled=True)
-    plane_prefix, plane_total = call(
-        compose_plane, (shape_of(3, KD, KD + VD), shape_of(4, KD + PART, KD))
-    )(exchanged)
-    gathered = lax.all_to_all(plane_total, "zl", 0, 0, tiled=True)
+    packed = call(
+        pack_heads, shape_of(HEADS, ROWS + MARK_ROWS, BEFORE + KD + VD, kind=bf16), inputs=3
+    )(heads_first(attn_query), keys, past)
+    exchanged, packed = lax.optimization_barrier((exchanged, packed))
+    zl = lax.axis_index("zl").astype(jnp.int32).reshape(1)
+    plane_prefix, *plane_totals = call(
+        compose_plane,
+        (shape_of(3, KD, KD + VD),) + (shape_of(KD + PART, KD),) * 4,
+        scalars=1,
+    )(zl, exchanged)
+    _, packed = lax.optimization_barrier((plane_totals[0], packed))
+    blocks = lax.all_to_all(packed, "x", 0, 0, tiled=True)
     group_prefix, group_total, group_offset = call(
         compose_group,
         (shape_of(3, KD, KD + PART), shape_of(KD + PART, KD), shape_of(PART, KD)),
-    )(gathered)
+        scalars=1,
+        inputs=4,
+        scratch=[pltpu.VMEM((4, KD + PART, KD), f32)],
+    )(zl, *around(plane_totals, "zl"))
     first = lax.ppermute(group_offset, "zh", [(0, 1)])
     third = lax.ppermute(group_total, "zh", [(2, 3)])
     pair = call(step_state, shape_of(PART, KD), inputs=2)(group_total, first)
@@ -335,8 +375,8 @@
     planes = call(group_states, shape_of(4, PART, KD), scalars=1, inputs=5)(
         place, first, one, two, third, group_prefix
     )
-    planes, past = lax.optimization_barrier((planes, past))
-    attn_heads = call(attend, shape_of(4, ROWS, VD, kind=bf16), inputs=2, flops=8e9, mib=16)(here, past)
+    planes, blocks = lax.optimization_barrier((planes, blocks))
+    attn_heads = call(attend, shape_of(4, ROWS, VD, kind=bf16), flops=8e9, mib=16)(blocks)
     parts = lax.all_to_all(planes, "zl", 0, 0, tiled=True)
     returned = call(plane_states, shape_of(4, 2 * KD + ROWS, VD, kind=bf16), inputs=3)(
         parts, plane_prefix, attn_heads

time: 121 us -> 119 us (0.983)
  blocking collectives: 28.3 us -> 15.4 us
  starting transfers between devices: 26.6 us -> 33.2 us
  local copies, waits for them, and re-layouts: 7.43 us -> 10 us
  Pallas kernels: 19.5 us -> 21.3 us
    all_to_all x1 -> x0, blocking collectives: 13.8 us -> none  [shards(): exchanged = lax.all_to_all(maps, 'x', 0, 0, tiled=True)]
    ppermute x1 -> x4, waiting for transfers between devices: 0.01 us -> 13 us  [the longest x1 7.57 us: shards(): past = lax.ppermute(keys, ('zh', 'zl'), [(i, i + 1) for i in range(15)])]
    all_to_all x2, waiting for transfers between devices: 13.8 us -> 2.04 us  [the longest x1 2.03 us: shards(): exchanged = lax.all_to_all(maps, 'x', 0, 0, tiled=True)]
    ppermute x1 -> x4, starting transfers between devices: 1.28 us -> 11.8 us  [the longest x3 10.6 us: around(): lax.ppermute(part, axis, [(i, (i + d) % 4) for i in range(4)])]
    unnamed x30 -> x33, local copies, waits for them, and re-layouts: 6.25 us -> 9.88 us
    all_to_all x1, starting transfers between devices: 7.02 us -> 5.09 us  [shards(): parts = lax.all_to_all(planes, 'zl', 0, 0, tiled=True)]
    all_to_all x2, starting transfers between devices: 9.75 us -> 7.89 us  [the longest x1 4.3 us: shards(): exchanged = lax.all_to_all(maps, 'x', 0, 0, tiled=True)]
    ppermute x1, waiting for transfers between devices: 17.7 us -> 16.3 us  [shards(): two = lax.ppermute(pair, 'zh', [(1, 3)])]
  transfers between devices with their start and end apart: 9 -> 12, of which waited for: 4 -> 6; matrix products, arithmetic and copies ran while one was open for 2% -> 1% of each run, Pallas kernels for 12% -> 16%
where the time goes in v6:
time: 119 us; the launch traced here: 118 us
  waiting for transfers between devices  35.7 us (30%)
  starting transfers between devices  33.2 us (28%)
  Pallas kernels  21.3 us (18%)
  blocking collectives  15.4 us (13%)
  local copies, waits for them, and re-layouts  10 us (8%)
  between operations  2.23 us (2%)
    ppermute x1, waiting for transfers between devices, shards(): two = lax.ppermute(pair, 'zh', [(1, 3)])  16.3 us
    all_to_all x1, blocking collectives, shards(): states = lax.all_to_all(returned, 'x', 0, 0, tiled=True)  15.4 us
    ppermute x3, starting transfers between devices, around(): lax.ppermute(part, axis, [(i, (i + d) % 4) for i in range(4)])  10.6 us
    unnamed x33, local copies, waits for them, and re-layouts  9.88 us
    ppermute x1, waiting for transfers between devices, shards(): past = lax.ppermute(keys, ('zh', 'zl'), [(i, i + 1) for i in range(15)])  7.57 us
    pallas_call x1, Pallas kernels, shards(): call(block_terms, (shape_of(HEADS, KD, KD + VD), shape_of(HEADS, ROWS, KD...  7.45 us
    ppermute x3, waiting for transfers between devices, around(): lax.ppermute(part, axis, [(i, (i + d) % 4) for i in range(4)])  5.39 us
    all_to_all x1, starting transfers between devices, shards(): parts = lax.all_to_all(planes, 'zl', 0, 0, tiled=True)  5.09 us
  transfers between devices with their start and end apart: 12, of which 6 were waited for; matrix products, arithmetic and copies ran while one was open for 1% of the time, Pallas kernels for 16%

profile of v6, /device:TPU:480, one launch (start us, length us, event | category | flops | bytes accessed | tf_op | source)
XLA Modules:
  0.0 117.8 jit_solution(17444565685857028621)
XLA Ops:
  0.7 1.2 %copy.28 = bf16[256,4,256]{2,0,1:T(8,128)(2,1)S(1)} copy(bf16[256,4,256]{2,1,0:T(4,128)(2,1)} %param.21) | data formatting | bytes 1048576 | tf_op args[9]
  1.9 0.0 copy-start.9
  1.9 1.0 copy.30
  2.9 0.0 copy-start.8
  3.5 0.0 copy-start.7
  3.5 0.7 copy-done.7
  4.2 0.1 shard_map.132.keys_ref
  4.3 1.3 %collective-permute-start = (bf16[4,272,384]{2,1,0:T(8,128)(2,1)S(1)}, bf16[4,272,384]{2,1,0:T(8,128)(2,1)}, u32[]{:S(2)}, u32[]{:S(2)}) collective-permute-start(bf16[4,272,384]{2,1,0:T(8,128)(2,1)S(1)} %shard_map.132.keys_ref), channel_id=1, source_target_pairs={{0,32},{32,64},{64,96},{96,128},{128,160},{160,192},{192,224},{224... | collective-permute-start | bytes 2506760 | tf_op jit(solution)/shard_map/ppermute | solution.py:331
  6.3 0.1 copy.29
  6.4 0.1 copy_bitcast_fusion.4
  6.5 0.0 copy-start.11
  6.5 7.5 %shard_map.131 = (f32[4,128,384]{2,1,0:T(8,128)}, f32[4,256,128]{2,1,0:T(8,128)S(1)}, f32[4,256,256]{2,1,0:T(8,128)S(1)}) custom-call(s32[1]{0:T(128)S(6)} %copy.32.count_ref, bf16[4,256,128]{2,1,0:T(8,128)(2,1)S(1)} %get-tuple-element.45.q_ref, bf16[4,256,128]{2,1,0:T(8,128)(2,1)S(1)} %get-tuple-element.44.k_ref, bf16[4,256,256]{2,1,0:T(8,128)(2,1)S(1)} %bitcast.30, ...), custom_call_target="tpu_custom_call" | custom-call | flops 8000000000 | bytes 1000000 | tf_op jit(solution)/shard_map/pallas_call | solution.py:332
  13.9 0.8 copy-done.2
  14.7 4.3 %all-to-all-start = ((f32[4,128,384]{2,1,0:T(8,128)}), f32[4,128,384]{2,1,0:T(8,128)S(1)}, u32[]{:S(2)}, u32[]{:S(2)}) async-start(f32[4,128,384]{2,1,0:T(8,128)} %get-tuple-element.25), calls=%async_computation | async-start | bytes 1572864 | tf_op jit(solution)/shard_map/all_to_all | solution.py:349
  19.1 7.6 %collective-permute-done.past_ref = bf16[4,272,384]{2,1,0:T(8,128)(2,1)} collective-permute-done((bf16[4,272,384]{2,1,0:T(8,128)(2,1)S(1)}, bf16[4,272,384]{2,1,0:T(8,128)(2,1)}, u32[]{:S(2)}, u32[]{:S(2)}) %collective-permute-start) | collective-permute-done | bytes 835616 | tf_op jit(solution)/shard_map/ppermute | solution.py:331
  26.6 2.6 %shard_map.133 = bf16[4,272,896]{2,1,0:T(8,128)(2,1)} custom-call(bf16[4,256,128]{2,1,0:T(8,128)(2,1)S(1)} %bitcast.29, bf16[4,272,384]{2,1,0:T(8,128)(2,1)S(1)} %shard_map.132.keys_ref, bf16[4,272,384]{2,1,0:T(8,128)(2,1)} %collective-permute-done.past_ref), custom_call_target="tpu_custom_call" | custom-call | flops 10000000 | bytes 1000000 | tf_op jit(solution)/shard_map/pallas_call | solution.py:350
  29.3 2.0 %all-to-all-done.maps_ref = f32[4,128,384]{2,1,0:T(8,128)S(1)} async-done(((f32[4,128,384]{2,1,0:T(8,128)}), f32[4,128,384]{2,1,0:T(8,128)S(1)}, u32[]{:S(2)}, u32[]{:S(2)}) %all-to-all-start) | async-done | bytes 786464 | tf_op jit(solution)/shard_map/all_to_all | solution.py:349
  31.3 0.8 shard_map.134
  32.1 0.8 copy-done
  33.0 3.6 %all-to-all-start.1 = ((bf16[4,272,896]{2,1,0:T(8,128)(2,1)}), bf16[4,272,896]{2,1,0:T(8,128)(2,1)S(1)}, u32[]{:S(2)}, u32[]{:S(2)}) async-start(bf16[4,272,896]{2,1,0:T(8,128)(2,1)} %shard_map.133), calls=%async_computation.1 | async-start | bytes 3899392 | tf_op jit(solution)/shard_map/all_to_all | solution.py:361
  36.6 5.2 %collective-permute-start.1 = (f32[192,128]{1,0:T(8,128)S(1)}, f32[192,128]{1,0:T(8,128)S(1)}, u32[]{:S(2)}, u32[]{:S(2)}) collective-permute-start(f32[192,128]{1,0:T(8,128)S(1)} %get-tuple-element.29), channel_id=1, source_target_pairs={{0,32},{32,64},{64,96},{96,0},{1,33},{33,65},{65,97},{97,1},{2,34}... | collective-permute-start | bytes 294920 | tf_op jit(solution)/shard_map/ppermute | solution.py:305
  41.7 2.5 %collective-permute-start.2 = (f32[192,128]{1,0:T(8,128)S(1)}, f32[192,128]{1,0:T(8,128)S(1)}, u32[]{:S(2)}, u32[]{:S(2)}) collective-permute-start(f32[192,128]{1,0:T(8,128)S(1)} %get-tuple-element.30), channel_id=1, source_target_pairs={{0,64},{32,96},{64,0},{96,32},{1,65},{33,97},{65,1},{97,33},{2,66}... | collective-permute-start | bytes 294920 | tf_op jit(solution)/shard_map/ppermute | solution.py:305
  44.2 2.9 %collective-permute-start.3 = (f32[192,128]{1,0:T(8,128)S(1)}, f32[192,128]{1,0:T(8,128)S(1)}, u32[]{:S(2)}, u32[]{:S(2)}) collective-permute-start(f32[192,128]{1,0:T(8,128)S(1)} %get-tuple-element.31), channel_id=1, source_target_pairs={{0,96},{32,0},{64,32},{96,64},{1,97},{33,1},{65,33},{97,65},{2,98}... | collective-permute-start | bytes 294920 | tf_op jit(solution)/shard_map/ppermute | solution.py:305
  47.1 0.0 collective-permute-done.1.one_ref
  47.2 3.0 %collective-permute-done.2.two_ref = f32[192,128]{1,0:T(8,128)S(1)} collective-permute-done((f32[192,128]{1,0:T(8,128)S(1)}, f32[192,128]{1,0:T(8,128)S(1)}, u32[]{:S(2)}, u32[]{:S(2)}) %collective-permute-start.2) | collective-permute-done | bytes 98336 | tf_op jit(solution)/shard_map/ppermute | solution.py:305
  50.2 2.3 %collective-permute-done.3.three_ref = f32[192,128]{1,0:T(8,128)S(1)} collective-permute-done((f32[192,128]{1,0:T(8,128)S(1)}, f32[192,128]{1,0:T(8,128)S(1)}, u32[]{:S(2)}, u32[]{:S(2)}) %collective-permute-start.3) | collective-permute-done | bytes 98336 | tf_op jit(solution)/shard_map/ppermute | solution.py:305
  52.5 1.4 %shard_map.135 = (f32[3,128,192]{2,1,0:T(8,128)S(1)}, f32[192,128]{1,0:T(8,128)}, f32[64,128]{1,0:T(8,128)S(1)}) custom-call(s32[1]{0:T(128)} %bitcast.6.place_ref, f32[192,128]{1,0:T(8,128)S(1)} %get-tuple-element.28.own_ref, f32[192,128]{1,0:T(8,128)S(1)} %collective-permute-done.1.one_ref, f32[192,128]{1,0:T(8,128)S(1)} %collective-permute-done.2.two_ref, ...), custom_call_target="tpu_custom_call" | custom-call | flops 10000000 | bytes 1000000 | tf_op jit(solution)/shard_map/pallas_call | solution.py:362
  54.0 1.3 %collective-permute-start.7 = (f32[192,128]{1,0:T(8,128)}, f32[192,128]{1,0:T(8,128)S(1)}, u32[]{:S(2)}, u32[]{:S(2)}) collective-permute-start(f32[192,128]{1,0:T(8,128)} %get-tuple-element.33.map_ref), channel_id=1, source_target_pairs={{256,384},{257,385},{258,386},{259,387},{260,388},{261,389},{262,3... | collective-permute-start | bytes 294920 | tf_op jit(solution)/shard_map/ppermute | solution.py:370
  55.3 0.7 collective-permute-start.4
  56.0 1.8 %shard_map.136 = f32[64,128]{1,0:T(8,128)} custom-call(f32[192,128]{1,0:T(8,128)} %get-tuple-element.33.map_ref, f32[64,128]{1,0:T(8,128)S(1)} %collective-permute-done.4.earlier_ref.first_ref), custom_call_target="tpu_custom_call" | custom-call | flops 10000000 | bytes 1000000 | tf_op jit(solution)/shard_map/pallas_call | solution.py:371
  57.7 0.7 collective-permute-start.5
  58.4 1.3 %collective-permute-start.6 = (f32[64,128]{1,0:T(8,128)}, f32[64,128]{1,0:T(8,128)}, u32[]{:S(2)}, u32[]{:S(2)}) collective-permute-start(f32[64,128]{1,0:T(8,128)} %shard_map.136), channel_id=1, source_target_pairs={{128,384},{129,385},{130,386},{131,387},{132,388},{133,389},{134,3... | collective-permute-start | bytes 98312 | tf_op jit(solution)/shard_map/ppermute | solution.py:373
  59.7 16.3 %collective-permute-done.6.two_ref = f32[64,128]{1,0:T(8,128)} collective-permute-done((f32[64,128]{1,0:T(8,128)}, f32[64,128]{1,0:T(8,128)}, u32[]{:S(2)}, u32[]{:S(2)}) %collective-permute-start.6) | collective-permute-done | bytes 32800 | tf_op jit(solution)/shard_map/ppermute | solution.py:373
  76.0 2.1 %shard_map.137 = f32[4,64,128]{2,1,0:T(8,128)} custom-call(s32[1]{0:T(128)} %bitcast.5.place_ref, f32[64,128]{1,0:T(8,128)S(1)} %collective-permute-done.4.earlier_ref.first_ref, f32[64,128]{1,0:T(8,128)S(1)} %collective-permute-done.5.one_ref, f32[64,128]{1,0:T(8,128)} %collective-permute-done.6.two_ref, f32[192,128]{1,0:T(8,128)S(1)} %collective-permute-done.7.third_ref, ...), custom_call_target="tpu_custom_call" | custom-call | flops 10000000 | bytes 1000000 | tf_op jit(solution)/shard_map/pallas_call | solution.py:375
  78.1 5.1 %all-to-all-start.2 = ((f32[4,64,128]{2,1,0:T(8,128)}), f32[4,64,128]{2,1,0:T(8,128)S(1)}, u32[]{:S(2)}, u32[]{:S(2)}) async-start(f32[4,64,128]{2,1,0:T(8,128)} %shard_map.137), calls=%async_computation.2 | async-start | bytes 262144 | tf_op jit(solution)/shard_map/all_to_all | solution.py:380
  83.2 3.0 %shard_map.138.attn_ref = bf16[4,256,256]{2,1,0:T(8,128)(2,1)S(1)} custom-call(bf16[4,272,896]{2,1,0:T(8,128)(2,1)S(1)} %all-to-all-done.1.blocks_ref), custom_call_target="tpu_custom_call" | custom-call | flops 8000000000 | bytes 1000000 | tf_op jit(solution)/shard_map/pallas_call | solution.py:379
  86.2 0.0 copy-start.4
  86.2 0.8 copy-done.4
  87.0 1.1 copy-done.1
  88.1 1.0 copy-done.5
  89.1 0.5 shard_map.139
  89.6 15.4 %all_to_all.31.state_ref = bf16[4,512,256]{2,1,0:T(8,128)(2,1)S(1)} all-to-all(bf16[4,512,256]{2,1,0:T(8,128)(2,1)S(1)} %shard_map.139), channel_id=1, replica_groups=mesh['zh'=4,'zl'=4,'x'=4,'head'=8] {'x'}, dimensions={0} | all-to-all | bytes 2097152 | tf_op jit(solution)/shard_map/all_to_all | solution.py:384
  105.0 1.3 %shard_map.140 = (f32[4,256,256]{2,1,0:T(8,128)S(1)}, f32[64,256]{1,0:T(8,128)}) custom-call(f32[4,256,128]{2,1,0:T(8,128)S(1)} %copy-done.3, f32[4,256,256]{2,1,0:T(8,128)S(1)} %get-tuple-element.23.local_ref, bf16[4,512,256]{2,1,0:T(8,128)(2,1)S(1)} %all_to_all.31.state_ref), custom_call_target="tpu_custom_call" | custom-call | flops 10000000 | bytes 1000000 | tf_op jit(solution)/shard_map/pallas_call | solution.py:385
  106.3 4.5 %all-to-all-start.4 = ((f32[8,8,256]{2,1,0:T(8,128)}), f32[8,8,256]{2,1,0:T(8,128)S(1)}, u32[]{:S(2)}, u32[]{:S(2)}) async-start(f32[8,8,256]{2,1,0:T(8,128)} %bitcast.11), calls=%async_computation.4 | async-start | bytes 131072 | tf_op jit(solution)/shard_map/all_to_all | solution.py:388
  110.8 1.2 %copy.21 = bf16[256,4,256]{2,1,0:T(4,128)(2,1)} copy(bf16[256,4,256]{2,0,1:T(8,128)(2,1)S(1)} %slice_bitcast_fusion) | data formatting | bytes 1048576
  112.0 4.4 %all-to-all-done.4 = f32[8,8,256]{2,1,0:T(8,128)S(1)} async-done(((f32[8,8,256]{2,1,0:T(8,128)}), f32[8,8,256]{2,1,0:T(8,128)S(1)}, u32[]{:S(2)}, u32[]{:S(2)}) %all-to-all-start.4) | async-done | bytes 65568 | tf_op jit(solution)/shard_map/all_to_all | solution.py:388
  116.4 0.2 shard_map.141
  116.6 1.2 %copy.20 = bf16[256,4,256]{2,1,0:T(4,128)(2,1)} copy(bf16[256,4,256]{2,0,1:T(8,128)(2,1)S(1)} %bitcast.26) | data formatting | bytes 1048576
  (24 shorter events, 0.1 us)
Async XLA Ops:
  0.6 5.6 %copy-start.10 = (bf16[256,4,256]{2,1,0:T(4,128)(2,1)S(1)}, bf16[256,4,256]{2,1,0:T(4,128)(2,1)}, u32[]{:S(2)}) copy-start(bf16[256,4,256]{2,1,0:T(4,128)(2,1)} %param.14) | copy-start | bytes 1572868
  0.6 5.7 %copy-start.13 = (bf16[256,4,128]{2,1,0:T(4,128)(2,1)S(1)}, bf16[256,4,128]{2,1,0:T(4,128)(2,1)}, u32[]{:S(2)}) copy-start(bf16[256,4,128]{2,1,0:T(4,128)(2,1)} %param.12) | copy-start | bytes 786436
  0.7 5.7 %copy-start.12 = (bf16[256,4,128]{2,1,0:T(4,128)(2,1)S(1)}, bf16[256,4,128]{2,1,0:T(4,128)(2,1)}, u32[]{:S(2)}) copy-start(bf16[256,4,128]{2,1,0:T(4,128)(2,1)} %param.13) | copy-start | bytes 786436
  1.9 4.6 %copy-start.9 = (f32[256,4]{0,1:T(4,128)S(1)}, f32[256,4]{0,1:T(4,128)}, u32[]{:S(2)}) copy-start(f32[256,4]{0,1:T(4,128)} %param.16) | copy-start | bytes 12292
  2.9 3.6 %copy-start.8 = (f32[256,4]{0,1:T(4,128)S(1)}, f32[256,4]{0,1:T(4,128)}, u32[]{:S(2)}) copy-start(f32[256,4]{0,1:T(4,128)} %param.15) | copy-start | bytes 12292
  3.5 0.7 copy-start.7
  4.3 22.3 %collective-permute-start = (bf16[4,272,384]{2,1,0:T(8,128)(2,1)S(1)}, bf16[4,272,384]{2,1,0:T(8,128)(2,1)}, u32[]{:S(2)}, u32[]{:S(2)}) collective-permute-start(bf16[4,272,384]{2,1,0:T(8,128)(2,1)S(1)} %shard_map.132.keys_ref), channel_id=1, source_target_pairs={{0,32},{32,64},{64,96},{96,128},{128,160},{160,192},{192,224},{224... | collective-permute-start | bytes 2506760 | tf_op jit(solution)/shard_map/ppermute | solution.py:331
  6.5 12.6 %copy-start.11 = (bf16[256,4,128]{2,1,0:T(4,128)(2,1)S(1)}, bf16[256,4,128]{2,1,0:T(4,128)(2,1)}, u32[]{:S(2)}) copy-start(bf16[256,4,128]{2,1,0:T(4,128)(2,1)} %param.19) | copy-start | bytes 786436
  13.9 0.8 copy-start.2
  14.7 16.6 %all-to-all-start = ((f32[4,128,384]{2,1,0:T(8,128)}), f32[4,128,384]{2,1,0:T(8,128)S(1)}, u32[]{:S(2)}, u32[]{:S(2)}) async-start(f32[4,128,384]{2,1,0:T(8,128)} %get-tuple-element.25), calls=%async_computation | async-start | bytes 1572864 | tf_op jit(solution)/shard_map/all_to_all | solution.py:349
  32.1 0.8 copy-start
  33.0 45.1 %all-to-all-start.1 = ((bf16[4,272,896]{2,1,0:T(8,128)(2,1)}), bf16[4,272,896]{2,1,0:T(8,128)(2,1)S(1)}, u32[]{:S(2)}, u32[]{:S(2)}) async-start(bf16[4,272,896]{2,1,0:T(8,128)(2,1)} %shard_map.133), calls=%async_computation.1 | async-start | bytes 3899392 | tf_op jit(solution)/shard_map/all_to_all | solution.py:361
  36.6 10.6 %collective-permute-start.1 = (f32[192,128]{1,0:T(8,128)S(1)}, f32[192,128]{1,0:T(8,128)S(1)}, u32[]{:S(2)}, u32[]{:S(2)}) collective-permute-start(f32[192,128]{1,0:T(8,128)S(1)} %get-tuple-element.29), channel_id=1, source_target_pairs={{0,32},{32,64},{64,96},{96,0},{1,33},{33,65},{65,97},{97,1},{2,34}... | collective-permute-start | bytes 294920 | tf_op jit(solution)/shard_map/ppermute | solution.py:305
  41.7 8.5 %collective-permute-start.2 = (f32[192,128]{1,0:T(8,128)S(1)}, f32[192,128]{1,0:T(8,128)S(1)}, u32[]{:S(2)}, u32[]{:S(2)}) collective-permute-start(f32[192,128]{1,0:T(8,128)S(1)} %get-tuple-element.30), channel_id=1, source_target_pairs={{0,64},{32,96},{64,0},{96,32},{1,65},{33,97},{65,1},{97,33},{2,66}... | collective-permute-start | bytes 294920 | tf_op jit(solution)/shard_map/ppermute | solution.py:305
  44.2 8.3 %collective-permute-start.3 = (f32[192,128]{1,0:T(8,128)S(1)}, f32[192,128]{1,0:T(8,128)S(1)}, u32[]{:S(2)}, u32[]{:S(2)}) collective-permute-start(f32[192,128]{1,0:T(8,128)S(1)} %get-tuple-element.31), channel_id=1, source_target_pairs={{0,96},{32,0},{64,32},{96,64},{1,97},{33,1},{65,33},{97,65},{2,98}... | collective-permute-start | bytes 294920 | tf_op jit(solution)/shard_map/ppermute | solution.py:305
  54.0 22.0 %collective-permute-start.7 = (f32[192,128]{1,0:T(8,128)}, f32[192,128]{1,0:T(8,128)S(1)}, u32[]{:S(2)}, u32[]{:S(2)}) collective-permute-start(f32[192,128]{1,0:T(8,128)} %get-tuple-element.33.map_ref), channel_id=1, source_target_pairs={{256,384},{257,385},{258,386},{259,387},{260,388},{261,389},{262,3... | collective-permute-start | bytes 294920 | tf_op jit(solution)/shard_map/ppermute | solution.py:370
  55.3 0.7 collective-permute-start.4
  57.7 2.0 %collective-permute-start.5 = (f32[64,128]{1,0:T(8,128)}, f32[64,128]{1,0:T(8,128)S(1)}, u32[]{:S(2)}, u32[]{:S(2)}) collective-permute-start(f32[64,128]{1,0:T(8,128)} %shard_map.136), channel_id=1, source_target_pairs={{128,256},{129,257},{130,258},{131,259},{132,260},{133,261},{134,2... | collective-permute-start | bytes 98312 | tf_op jit(solution)/shard_map/ppermute | solution.py:372
  58.4 17.6 %collective-permute-start.6 = (f32[64,128]{1,0:T(8,128)}, f32[64,128]{1,0:T(8,128)}, u32[]{:S(2)}, u32[]{:S(2)}) collective-permute-start(f32[64,128]{1,0:T(8,128)} %shard_map.136), channel_id=1, source_target_pairs={{128,384},{129,385},{130,386},{131,387},{132,388},{133,389},{134,3... | collective-permute-start | bytes 98312 | tf_op jit(solution)/shard_map/ppermute | solution.py:373
  78.1 8.9 %all-to-all-start.2 = ((f32[4,64,128]{2,1,0:T(8,128)}), f32[4,64,128]{2,1,0:T(8,128)S(1)}, u32[]{:S(2)}, u32[]{:S(2)}) async-start(f32[4,64,128]{2,1,0:T(8,128)} %shard_map.137), calls=%async_computation.2 | async-start | bytes 262144 | tf_op jit(solution)/shard_map/all_to_all | solution.py:380
  86.2 0.8 copy-start.4
  87.0 1.1 copy-start.1
  88.1 1.0 copy-start.5
  89.1 15.9 %copy-start.3 = (f32[4,256,128]{2,1,0:T(8,128)S(1)}, f32[4,256,128]{2,1,0:T(8,128)}, u32[]{:S(2)}) copy-start(f32[4,256,128]{2,1,0:T(8,128)} %copy-done.2) | copy-start | bytes 1572868
  105.0 11.4 %copy-start.6 = (f32[4,256]{1,0:T(4,128)S(1)}, f32[4,256]{1,0:T(4,128)}, u32[]{:S(2)}) copy-start(f32[4,256]{1,0:T(4,128)} %gain_ref.1) | copy-start | bytes 12292
  106.3 10.1 %all-to-all-start.4 = ((f32[8,8,256]{2,1,0:T(8,128)}), f32[8,8,256]{2,1,0:T(8,128)S(1)}, u32[]{:S(2)}, u32[]{:S(2)}) async-start(f32[8,8,256]{2,1,0:T(8,128)} %bitcast.11), calls=%async_computation.4 | async-start | bytes 131072 | tf_op jit(solution)/shard_map/all_to_all | solution.py:388

commit v7 on v6

--- a/solution.py
+++ b/solution.py
@@ -118,8 +118,9 @@
         last = log_col[ROWS - 1 : ROWS, :]
         high, low = halves((jnp.exp(last - log_col) * k_col) * new)
         update = dot(k, high, ((0,), (0,))) + dot(k, low, ((0,), (0,)))
-        map_ref[h, :, :KD] = jnp.where(row_k == col_k, jnp.exp(last), 0.0) - update[:, :KD]
-        map_ref[h, :, KD:] = update[:, KD:]
+        transition = jnp.where(row_k == col_k, jnp.exp(last), 0.0) - update[:, :KD]
+        map_ref[h, :, :KD], map_ref[h, :, KD : 2 * KD] = halves(transition)
+        map_ref[h, :, 2 * KD :] = update[:, KD:].astype(bf16)
         mixed = dot3(local_ref[h], new)
         carry_ref[h] = (jnp.exp(log_col) * q_col) * q_ref[h].astype(f32) - mixed[:, :KD]
         local_ref[h] = mixed[:, KD:]
@@ -139,37 +140,21 @@
     return jnp.concatenate([state[:, :KD], state[:, KD:] + offset], axis=1)
 
 
-def pick(index, choices):
-    picked = choices[0]
-    for i in range(1, len(choices)):
-        picked = jnp.where(index == i, choices[i], picked)
-    return picked
-
-
-def ahead(place, shift):
-    return lax.rem(place + shift, 4)
-
-
-def compose_plane(place_ref, maps_ref, before_ref, *send_refs):
-    state = maps_ref[0]
+def compose_plane(maps_ref, before_ref, send_ref):
+    def map_of(i):
+        wide = maps_ref[i].astype(f32)
+        return wide[:, :KD] + wide[:, KD : 2 * KD], wide[:, 2 * KD :]
+
+    state = jnp.concatenate(map_of(0), axis=1)
     for i in range(1, 4):
         before_ref[i - 1] = state
-        state = then(state, maps_ref[i, :, :KD], maps_ref[i, :, KD:])
-    quarters = [fold(state[:, KD + i * PART : KD + (i + 1) * PART]) for i in range(4)]
-    for d, send_ref in enumerate(send_refs):
-        send_ref[:KD, :] = state[:, :KD]
-        send_ref[KD:, :] = pick(ahead(place_ref[0], d), quarters)
-
-
-def in_order(place, refs, ordered_ref):
-    for d, ref in enumerate(refs):
-        ordered_ref[pl.ds(ahead(place, 4 - d), 1)] = ref[...][None]
-
-
-def compose_group(
-    place_ref, own_ref, one_ref, two_ref, three_ref, before_ref, total_ref, offset_ref, maps_ref
-):
-    in_order(place_ref[0], (own_ref, one_ref, two_ref, three_ref), maps_ref)
+        state = then(state, *map_of(i))
+    for i in range(4):
+        send_ref[i, :KD, :] = state[:, :KD]
+        send_ref[i, KD:, :] = fold(state[:, KD + i * PART : KD + (i + 1) * PART])
+
+
+def compose_group(maps_ref, before_ref, total_ref, offset_ref):
     state = jnp.concatenate([maps_ref[0, :KD, :], unfold(maps_ref[0, KD:, :])], axis=1)
     for i in range(1, 4):
         before_ref[i - 1] = state
@@ -205,16 +190,14 @@
         entering = state
         if i > 0:
             entering = dot3(before_ref[i - 1, :, :KD], state) + before_ref[i - 1, :, KD:]
-        out_ref[i, :KD, :], out_ref[i, KD : 2 * KD, :] = halves(entering)
-        out_ref[i, 2 * KD :, :] = attn_ref[i]
+        out_ref[i, :KD, :] = entering.astype(bf16)
+        out_ref[i, KD:, :] = attn_ref[i]
 
 
 def raw_rows(carry_ref, local_ref, state_ref, raw_ref, square_ref):
     total = jnp.zeros((ROWS, VD), f32)
     for h in range(HEADS):
-        carry_high, carry_low = halves(carry_ref[h])
-        high, low = state_ref[h, :KD, :], state_ref[h, KD : 2 * KD, :]
-        raw = local_ref[h] + dot(carry_high, high) + (dot(carry_high, low) + dot(carry_low, high))
+        raw = local_ref[h] + dot2(carry_ref[h], state_ref[h, :KD, :])
         raw_ref[h] = raw
         total = total + raw * raw
     column = jnp.sum(total, axis=1, keepdims=True)
@@ -300,13 +283,6 @@
     return jnp.swapaxes(block, 0, 1)
 
 
-def around(parts, axis):
-    return [
-        lax.ppermute(part, axis, [(i, (i + d) % 4) for i in range(4)]) if d else part
-        for d, part in enumerate(parts)
-    ]
-
-
 def shape_of(*dims, kind=f32):
     return jax.ShapeDtypeStruct(dims, kind)
 
@@ -331,7 +307,11 @@
     past = lax.ppermute(keys, ("zh", "zl"), [(i, i + 1) for i in range(15)])
     maps, carry, local = call(
         block_terms,
-        (shape_of(HEADS, KD, KD + VD), shape_of(HEADS, ROWS, KD), shape_of(HEADS, ROWS, VD)),
+        (
+            shape_of(HEADS, KD, 2 * KD + VD, kind=bf16),
+            shape_of(HEADS, ROWS, KD),
+            shape_of(HEADS, ROWS, VD),
+        ),
         scalars=1,
         inputs=5,
         scratch=[pltpu.VMEM((HEADS, ROWS, ROWS), f32)] * 2,
@@ -347,25 +327,20 @@
     )
     maps, attn_query = lax.optimization_barrier((maps, attn_query))
     exchanged = lax.all_to_all(maps, "x", 0, 0, tiled=True)
+    exchanged, past = lax.optimization_barrier((exchanged, past))
     packed = call(
         pack_heads, shape_of(HEADS, ROWS + MARK_ROWS, BEFORE + KD + VD, kind=bf16), inputs=3
     )(heads_first(attn_query), keys, past)
-    exchanged, packed = lax.optimization_barrier((exchanged, packed))
-    zl = lax.axis_index("zl").astype(jnp.int32).reshape(1)
-    plane_prefix, *plane_totals = call(
-        compose_plane,
-        (shape_of(3, KD, KD + VD),) + (shape_of(KD + PART, KD),) * 4,
-        scalars=1,
-    )(zl, exchanged)
-    _, packed = lax.optimization_barrier((plane_totals[0], packed))
-    blocks = lax.all_to_all(packed, "x", 0, 0, tiled=True)
+    plane_prefix, plane_total = call(
+        compose_plane, (shape_of(3, KD, KD + VD), shape_of(4, KD + PART, KD))
+    )(exchanged)
+    gathered = lax.all_to_all(plane_total, "zl", 0, 0, tiled=True)
     group_prefix, group_total, group_offset = call(
         compose_group,
         (shape_of(3, KD, KD + PART), shape_of(KD + PART, KD), shape_of(PART, KD)),
-        scalars=1,
-        inputs=4,
-        scratch=[pltpu.VMEM((4, KD + PART, KD), f32)],
-    )(zl, *around(plane_totals, "zl"))
+    )(gathered)
+    _, packed = lax.optimization_barrier((group_total, packed))
+    blocks = lax.all_to_all(packed, "x", 0, 0, tiled=True)
     first = lax.ppermute(group_offset, "zh", [(0, 1)])
     third = lax.ppermute(group_total, "zh", [(2, 3)])
     pair = call(step_state, shape_of(PART, KD), inputs=2)(group_total, first)
@@ -378,7 +353,7 @@
     planes, blocks = lax.optimization_barrier((planes, blocks))
     attn_heads = call(attend, shape_of(4, ROWS, VD, kind=bf16), flops=8e9, mib=16)(blocks)
     parts = lax.all_to_all(planes, "zl", 0, 0, tiled=True)
-    returned = call(plane_states, shape_of(4, 2 * KD + ROWS, VD, kind=bf16), inputs=3)(
+    returned = call(plane_states, shape_of(4, KD + ROWS, VD, kind=bf16), inputs=3)(
         parts, plane_prefix, attn_heads
     )
     states = lax.all_to_all(returned, "x", 0, 0, tiled=True)
@@ -389,7 +364,7 @@
     delta_heads = call(normed, shape_of(HEADS, ROWS, VD, kind=bf16), scalars=1, inputs=3)(
         delta_count, raw, squares, delta_gain
     )
-    return (heads_first(delta_heads), heads_first(states[:, 2 * KD :]))
+    return (heads_first(delta_heads), heads_first(states[:, KD:]))
 
 
 def solution(mesh):

time: 119 us -> 116 us (0.975); the launches traced: 118 us -> 114 us
  blocking collectives: 15.4 us -> 27.7 us
  waiting for transfers between devices: 35.7 us -> 26.3 us
  starting transfers between devices: 33.2 us -> 26 us
  Pallas kernels: 21.3 us -> 18.5 us
  local copies, waits for them, and re-layouts: 10 us -> 12.8 us
    all_to_all x0 -> x1, blocking collectives: none -> 13.7 us  [shards(): exchanged = lax.all_to_all(maps, 'x', 0, 0, tiled=True)]
    ppermute x3 -> x0, starting transfers between devices: 10.6 us -> none  [around(): lax.ppermute(part, axis, [(i, (i + d) % 4) for i in range(4)])]
    ppermute x1, waiting for transfers between devices: 7.57 us -> 0.01 us  [shards(): past = lax.ppermute(keys, ('zh', 'zl'), [(i, i + 1) for i in range(15)])]
    ppermute x3 -> x0, waiting for transfers between devices: 5.39 us -> none  [around(): lax.ppermute(part, axis, [(i, (i + d) % 4) for i in range(4)])]
    all_to_all x1, waiting for transfers between devices: 2.03 us -> 5.52 us  [shards(): gathered = lax.all_to_all(plane_total, 'zl', 0, 0, tiled=True)]
    unnamed x33 -> x41, local copies, waits for them, and re-layouts: 9.88 us -> 12.7 us
    all_to_all x1, starting transfers between devices: 4.3 us -> 6.68 us  [shards(): gathered = lax.all_to_all(plane_total, 'zl', 0, 0, tiled=True)]
    all_to_all x1, blocking collectives: 15.4 us -> 14 us  [shards(): states = lax.all_to_all(returned, 'x', 0, 0, tiled=True)]
  transfers between devices with their start and end apart: 12 -> 9, of which waited for: 6 -> 3; matrix products, arithmetic and copies ran while one was open for 1% -> 1% of each run, Pallas kernels for 16% -> 13%
where the time goes in v7:
time: 116 us; the launch traced here: 114 us
  blocking collectives  27.7 us (24%)
  waiting for transfers between devices  26.3 us (23%)
  starting transfers between devices  26 us (22%)
  Pallas kernels  18.5 us (16%)
  local copies, waits for them, and re-layouts  12.8 us (11%)
  between operations  2.26 us (2%)
    ppermute x1, waiting for transfers between devices, shards(): two = lax.ppermute(pair, 'zh', [(1, 3)])  16.4 us
    all_to_all x1, blocking collectives, shards(): states = lax.all_to_all(returned, 'x', 0, 0, tiled=True)  14 us
    all_to_all x1, blocking collectives, shards(): exchanged = lax.all_to_all(maps, 'x', 0, 0, tiled=True)  13.7 us
    unnamed x41, local copies, waits for them, and re-layouts  12.7 us
    pallas_call x1, Pallas kernels, shards(): call(block_terms, (shape_of(HEADS, KD, 2 * KD + VD, kind=bf16), shape_of(...  6.73 us
    all_to_all x1, starting transfers between devices, shards(): gathered = lax.all_to_all(plane_total, 'zl', 0, 0, tiled=True)  6.68 us
    all_to_all x1, waiting for transfers between devices, shards(): gathered = lax.all_to_all(plane_total, 'zl', 0, 0, tiled=True)  5.52 us
    all_to_all x1, starting transfers between devices, shards(): parts = lax.all_to_all(planes, 'zl', 0, 0, tiled=True)  5.42 us
  transfers between devices with their start and end apart: 9, of which 3 were waited for; matrix products, arithmetic and copies ran while one was open for 1% of the time, Pallas kernels for 13%

profile of v7, /device:TPU:480, one launch (start us, length us, event | category | flops | bytes accessed | tf_op | source)
XLA Modules:
  0.0 113.6 jit_solution(1124002223924252210)
XLA Ops:
  1.3 1.0 copy.31
  2.3 0.0 copy-start.16
  2.3 0.0 copy-start.17
  2.4 0.0 copy-start.13
  2.4 1.2 %copy.28 = bf16[256,4,256]{2,0,1:T(8,128)(2,1)S(1)} copy(bf16[256,4,256]{2,1,0:T(4,128)(2,1)} %param.21) | data formatting | bytes 1048576 | tf_op args[9]
  3.5 0.0 copy-start.12
  3.6 0.0 copy-start.11
  3.6 0.7 copy-done.11
  4.2 0.1 shard_map.132.keys_ref
  4.3 1.3 %collective-permute-start = (bf16[4,272,384]{2,1,0:T(8,128)(2,1)S(1)}, bf16[4,272,384]{2,1,0:T(8,128)(2,1)S(1)}, u32[]{:S(2)}, u32[]{:S(2)}) collective-permute-start(bf16[4,272,384]{2,1,0:T(8,128)(2,1)S(1)} %shard_map.132.keys_ref), channel_id=1, source_target_pairs={{0,32},{32,64},{64,96},{96,128},{128,160},{160,192},{192,224},{224... | collective-permute-start | bytes 2506760 | tf_op jit(solution)/shard_map/ppermute | solution.py:307
  6.3 0.1 copy.29
  6.4 0.1 copy_bitcast_fusion.4
  6.5 6.7 %shard_map.131 = (bf16[4,128,512]{2,1,0:T(8,128)(2,1)S(1)}, f32[4,256,128]{2,1,0:T(8,128)S(1)}, f32[4,256,256]{2,1,0:T(8,128)S(1)}) custom-call(s32[1]{0:T(128)S(6)} %copy.32.count_ref, bf16[4,256,128]{2,1,0:T(8,128)(2,1)S(1)} %get-tuple-element.39.q_ref, bf16[4,256,128]{2,1,0:T(8,128)(2,1)S(1)} %get-tuple-element.38.k_ref, ...), custom_call_target="tpu_custom_call" | custom-call | flops 8000000000 | bytes 1000000 | tf_op jit(solution)/shard_map/pallas_call | solution.py:308
  13.2 0.0 copy-start.4
  13.2 0.0 copy-start.15
  13.2 13.7 %all_to_all.36.maps_ref = bf16[4,128,512]{2,1,0:T(8,128)(2,1)S(1)} all-to-all(bf16[4,128,512]{2,1,0:T(8,128)(2,1)S(1)} %get-tuple-element.22), channel_id=1, replica_groups=mesh['zh'=4,'zl'=4,'x'=4,'head'=8] {'x'}, dimensions={0} | all-to-all | bytes 1048576 | tf_op jit(solution)/shard_map/all_to_all | solution.py:329
  26.9 0.9 copy-done
  27.8 1.6 %shard_map.133 = (f32[3,128,384]{2,1,0:T(8,128)S(1)}, f32[4,192,128]{2,1,0:T(8,128)}) custom-call(bf16[4,128,512]{2,1,0:T(8,128)(2,1)S(1)} %all_to_all.36.maps_ref), custom_call_target="tpu_custom_call" | custom-call | flops 10000000 | bytes 1000000 | tf_op jit(solution)/shard_map/pallas_call | solution.py:334
  29.4 0.8 copy-done.2
  30.3 6.7 %all-to-all-start.1 = ((f32[4,192,128]{2,1,0:T(8,128)}), f32[4,192,128]{2,1,0:T(8,128)S(1)}, u32[]{:S(2)}, u32[]{:S(2)}) async-start(f32[4,192,128]{2,1,0:T(8,128)} %get-tuple-element.24), calls=%async_computation.1 | async-start | bytes 786432 | tf_op jit(solution)/shard_map/all_to_all | solution.py:337
  37.0 1.1 %copy-done.1 = bf16[4,272,384]{2,1,0:T(8,128)(2,1)S(1)} copy-done((bf16[4,272,384]{2,1,0:T(8,128)(2,1)S(1)}, bf16[4,272,384]{2,1,0:T(8,128)(2,1)}, u32[]{:S(2)}) %copy-start.1) | copy-done | bytes 835608
  38.1 1.5 %shard_map.137 = bf16[4,272,896]{2,1,0:T(8,128)(2,1)} custom-call(bf16[4,256,128]{2,1,0:T(8,128)(2,1)S(1)} %bitcast.28, bf16[4,272,384]{2,1,0:T(8,128)(2,1)S(1)} %shard_map.132.keys_ref, bf16[4,272,384]{2,1,0:T(8,128)(2,1)S(1)} %copy-done.1), custom_call_target="tpu_custom_call" | custom-call | flops 10000000 | bytes 1000000 | tf_op jit(solution)/shard_map/pallas_call | solution.py:331
  39.6 5.5 %all-to-all-done.1.maps_ref = f32[4,192,128]{2,1,0:T(8,128)S(1)} async-done(((f32[4,192,128]{2,1,0:T(8,128)}), f32[4,192,128]{2,1,0:T(8,128)S(1)}, u32[]{:S(2)}, u32[]{:S(2)}) %all-to-all-start.1) | async-done | bytes 393248 | tf_op jit(solution)/shard_map/all_to_all | solution.py:337
  45.1 0.8 shard_map.134
  45.9 0.0 copy-start.8
  45.9 0.6 copy-done.8
  46.6 4.3 %all-to-all-start.2 = ((bf16[4,272,896]{2,1,0:T(8,128)(2,1)}), bf16[4,272,896]{2,1,0:T(8,128)(2,1)S(1)}, u32[]{:S(2)}, u32[]{:S(2)}) async-start(bf16[4,272,896]{2,1,0:T(8,128)(2,1)} %shard_map.137), calls=%async_computation.2 | async-start | bytes 3899392 | tf_op jit(solution)/shard_map/all_to_all | solution.py:343
  50.8 1.3 %collective-permute-start.4 = (f32[192,128]{1,0:T(8,128)}, f32[192,128]{1,0:T(8,128)S(1)}, u32[]{:S(2)}, u32[]{:S(2)}) collective-permute-start(f32[192,128]{1,0:T(8,128)} %copy-done.8), channel_id=1, source_target_pairs={{256,384},{257,385},{258,386},{259,387},{260,388},{261,389},{262,3... | collective-permute-start | bytes 294920 | tf_op jit(solution)/shard_map/ppermute | solution.py:345
  52.1 0.7 collective-permute-start.1
  52.8 0.9 copy-done.9
  53.7 0.9 shard_map.135
  54.6 0.7 collective-permute-start.2
  55.3 1.3 %collective-permute-start.3 = (f32[64,128]{1,0:T(8,128)}, f32[64,128]{1,0:T(8,128)}, u32[]{:S(2)}, u32[]{:S(2)}) collective-permute-start(f32[64,128]{1,0:T(8,128)} %shard_map.135), channel_id=1, source_target_pairs={{128,384},{129,385},{130,386},{131,387},{132,388},{133,389},{134,3... | collective-permute-start | bytes 98312 | tf_op jit(solution)/shard_map/ppermute | solution.py:348
  56.6 16.4 %collective-permute-done.3.two_ref = f32[64,128]{1,0:T(8,128)} collective-permute-done((f32[64,128]{1,0:T(8,128)}, f32[64,128]{1,0:T(8,128)}, u32[]{:S(2)}, u32[]{:S(2)}) %collective-permute-start.3) | collective-permute-done | bytes 32800 | tf_op jit(solution)/shard_map/ppermute | solution.py:348
  73.0 2.1 %shard_map.136 = f32[4,64,128]{2,1,0:T(8,128)} custom-call(s32[1]{0:T(128)} %bitcast.5.place_ref, f32[64,128]{1,0:T(8,128)S(1)} %collective-permute-done.1.earlier_ref.first_ref, f32[64,128]{1,0:T(8,128)S(1)} %collective-permute-done.2.one_ref, f32[64,128]{1,0:T(8,128)} %collective-permute-done.3.two_ref, f32[192,128]{1,0:T(8,128)S(1)} %collective-permute-done.4.third_ref, ...), custom_call_target="tpu_custom_call" | custom-call | flops 10000000 | bytes 1000000 | tf_op jit(solution)/shard_map/pallas_call | solution.py:350
  75.1 5.4 %all-to-all-start.3 = ((f32[4,64,128]{2,1,0:T(8,128)}), f32[4,64,128]{2,1,0:T(8,128)S(1)}, u32[]{:S(2)}, u32[]{:S(2)}) async-start(f32[4,64,128]{2,1,0:T(8,128)} %shard_map.136), calls=%async_computation.3 | async-start | bytes 262144 | tf_op jit(solution)/shard_map/all_to_all | solution.py:355
  80.6 3.0 %shard_map.138.attn_ref = bf16[4,256,256]{2,1,0:T(8,128)(2,1)S(1)} custom-call(bf16[4,272,896]{2,1,0:T(8,128)(2,1)S(1)} %all-to-all-done.2.blocks_ref), custom_call_target="tpu_custom_call" | custom-call | flops 8000000000 | bytes 1000000 | tf_op jit(solution)/shard_map/pallas_call | solution.py:354
  83.6 0.8 copy-done.6
  84.4 1.1 copy-done.3
  85.4 1.0 copy-done.7
  86.5 0.5 shard_map.139
  86.9 14.0 %all_to_all.37.state_ref = bf16[4,384,256]{2,1,0:T(8,128)(2,1)S(1)} all-to-all(bf16[4,384,256]{2,1,0:T(8,128)(2,1)S(1)} %shard_map.139), channel_id=1, replica_groups=mesh['zh'=4,'zl'=4,'x'=4,'head'=8] {'x'}, dimensions={0} | all-to-all | bytes 1572864 | tf_op jit(solution)/shard_map/all_to_all | solution.py:359
  101.0 1.1 %shard_map.140 = (f32[4,256,256]{2,1,0:T(8,128)S(1)}, f32[64,256]{1,0:T(8,128)}) custom-call(f32[4,256,128]{2,1,0:T(8,128)S(1)} %copy-done.5, f32[4,256,256]{2,1,0:T(8,128)S(1)} %get-tuple-element.20.local_ref, bf16[4,384,256]{2,1,0:T(8,128)(2,1)S(1)} %all_to_all.37.state_ref), custom_call_target="tpu_custom_call" | custom-call | flops 10000000 | bytes 1000000 | tf_op jit(solution)/shard_map/pallas_call | solution.py:360
  102.1 4.5 %all-to-all-start.5 = ((f32[8,8,256]{2,1,0:T(8,128)}), f32[8,8,256]{2,1,0:T(8,128)S(1)}, u32[]{:S(2)}, u32[]{:S(2)}) async-start(f32[8,8,256]{2,1,0:T(8,128)} %bitcast.10), calls=%async_computation.5 | async-start | bytes 131072 | tf_op jit(solution)/shard_map/all_to_all | solution.py:363
  106.6 1.2 %copy.21 = bf16[256,4,256]{2,1,0:T(4,128)(2,1)} copy(bf16[256,4,256]{2,0,1:T(8,128)(2,1)S(1)} %slice_bitcast_fusion) | data formatting | bytes 1048576
  107.8 4.4 %all-to-all-done.5 = f32[8,8,256]{2,1,0:T(8,128)S(1)} async-done(((f32[8,8,256]{2,1,0:T(8,128)}), f32[8,8,256]{2,1,0:T(8,128)S(1)}, u32[]{:S(2)}, u32[]{:S(2)}) %all-to-all-start.5) | async-done | bytes 65568 | tf_op jit(solution)/shard_map/all_to_all | solution.py:363
  112.2 0.2 shard_map.141
  112.4 1.2 %copy.20 = bf16[256,4,256]{2,1,0:T(4,128)(2,1)} copy(bf16[256,4,256]{2,0,1:T(8,128)(2,1)S(1)} %bitcast.25) | data formatting | bytes 1048576
  (27 shorter events, 0.1 us)
Async XLA Ops:
  0.6 5.6 %copy-start.14 = (bf16[256,4,256]{2,1,0:T(4,128)(2,1)S(1)}, bf16[256,4,256]{2,1,0:T(4,128)(2,1)}, u32[]{:S(2)}) copy-start(bf16[256,4,256]{2,1,0:T(4,128)(2,1)} %param.14) | copy-start | bytes 1572868
  2.3 4.0 %copy-start.16 = (bf16[256,4,128]{2,1,0:T(4,128)(2,1)S(1)}, bf16[256,4,128]{2,1,0:T(4,128)(2,1)}, u32[]{:S(2)}) copy-start(bf16[256,4,128]{2,1,0:T(4,128)(2,1)} %param.13) | copy-start | bytes 786436
  2.3 4.0 %copy-start.17 = (bf16[256,4,128]{2,1,0:T(4,128)(2,1)S(1)}, bf16[256,4,128]{2,1,0:T(4,128)(2,1)}, u32[]{:S(2)}) copy-start(bf16[256,4,128]{2,1,0:T(4,128)(2,1)} %param.12) | copy-start | bytes 786436
  2.4 4.1 %copy-start.13 = (f32[256,4]{0,1:T(4,128)S(1)}, f32[256,4]{0,1:T(4,128)}, u32[]{:S(2)}) copy-start(f32[256,4]{0,1:T(4,128)} %param.16) | copy-start | bytes 12292
  3.5 2.9 %copy-start.12 = (f32[256,4]{0,1:T(4,128)S(1)}, f32[256,4]{0,1:T(4,128)}, u32[]{:S(2)}) copy-start(f32[256,4]{0,1:T(4,128)} %param.15) | copy-start | bytes 12292
  3.6 0.7 copy-start.11
  4.3 22.6 %collective-permute-start = (bf16[4,272,384]{2,1,0:T(8,128)(2,1)S(1)}, bf16[4,272,384]{2,1,0:T(8,128)(2,1)S(1)}, u32[]{:S(2)}, u32[]{:S(2)}) collective-permute-start(bf16[4,272,384]{2,1,0:T(8,128)(2,1)S(1)} %shard_map.132.keys_ref), channel_id=1, source_target_pairs={{0,32},{32,64},{64,96},{96,128},{128,160},{160,192},{192,224},{224... | collective-permute-start | bytes 2506760 | tf_op jit(solution)/shard_map/ppermute | solution.py:307
  13.2 16.2 %copy-start.4 = (f32[4,256,128]{2,1,0:T(8,128)}, f32[4,256,128]{2,1,0:T(8,128)S(1)}, u32[]{:S(2)}) copy-start(f32[4,256,128]{2,1,0:T(8,128)S(1)} %get-tuple-element.19.carry_ref) | copy-start | bytes 1572868
  13.2 23.7 %copy-start.15 = (bf16[256,4,128]{2,1,0:T(4,128)(2,1)S(1)}, bf16[256,4,128]{2,1,0:T(4,128)(2,1)}, u32[]{:S(2)}) copy-start(bf16[256,4,128]{2,1,0:T(4,128)(2,1)} %param.19) | copy-start | bytes 786436
  26.9 0.9 copy-start
  29.4 0.8 copy-start.2
  30.3 14.9 %all-to-all-start.1 = ((f32[4,192,128]{2,1,0:T(8,128)}), f32[4,192,128]{2,1,0:T(8,128)S(1)}, u32[]{:S(2)}, u32[]{:S(2)}) async-start(f32[4,192,128]{2,1,0:T(8,128)} %get-tuple-element.24), calls=%async_computation.1 | async-start | bytes 786432 | tf_op jit(solution)/shard_map/all_to_all | solution.py:337
  37.0 1.2 %copy-start.1 = (bf16[4,272,384]{2,1,0:T(8,128)(2,1)S(1)}, bf16[4,272,384]{2,1,0:T(8,128)(2,1)}, u32[]{:S(2)}) copy-start(bf16[4,272,384]{2,1,0:T(8,128)(2,1)} %copy-done) | copy-start | bytes 2506756
  45.9 0.6 copy-start.8
  46.6 28.6 %all-to-all-start.2 = ((bf16[4,272,896]{2,1,0:T(8,128)(2,1)}), bf16[4,272,896]{2,1,0:T(8,128)(2,1)S(1)}, u32[]{:S(2)}, u32[]{:S(2)}) async-start(bf16[4,272,896]{2,1,0:T(8,128)(2,1)} %shard_map.137), calls=%async_computation.2 | async-start | bytes 3899392 | tf_op jit(solution)/shard_map/all_to_all | solution.py:343
  50.8 22.2 %collective-permute-start.4 = (f32[192,128]{1,0:T(8,128)}, f32[192,128]{1,0:T(8,128)S(1)}, u32[]{:S(2)}, u32[]{:S(2)}) collective-permute-start(f32[192,128]{1,0:T(8,128)} %copy-done.8), channel_id=1, source_target_pairs={{256,384},{257,385},{258,386},{259,387},{260,388},{261,389},{262,3... | collective-permute-start | bytes 294920 | tf_op jit(solution)/shard_map/ppermute | solution.py:345
  52.1 0.7 collective-permute-start.1
  52.8 0.9 copy-start.9
  54.6 2.0 %collective-permute-start.2 = (f32[64,128]{1,0:T(8,128)}, f32[64,128]{1,0:T(8,128)S(1)}, u32[]{:S(2)}, u32[]{:S(2)}) collective-permute-start(f32[64,128]{1,0:T(8,128)} %shard_map.135), channel_id=1, source_target_pairs={{128,256},{129,257},{130,258},{131,259},{132,260},{133,261},{134,2... | collective-permute-start | bytes 98312 | tf_op jit(solution)/shard_map/ppermute | solution.py:347
  55.3 17.7 %collective-permute-start.3 = (f32[64,128]{1,0:T(8,128)}, f32[64,128]{1,0:T(8,128)}, u32[]{:S(2)}, u32[]{:S(2)}) collective-permute-start(f32[64,128]{1,0:T(8,128)} %shard_map.135), channel_id=1, source_target_pairs={{128,384},{129,385},{130,386},{131,387},{132,388},{133,389},{134,3... | collective-permute-start | bytes 98312 | tf_op jit(solution)/shard_map/ppermute | solution.py:348
  75.1 9.2 %all-to-all-start.3 = ((f32[4,64,128]{2,1,0:T(8,128)}), f32[4,64,128]{2,1,0:T(8,128)S(1)}, u32[]{:S(2)}, u32[]{:S(2)}) async-start(f32[4,64,128]{2,1,0:T(8,128)} %shard_map.136), calls=%async_computation.3 | async-start | bytes 262144 | tf_op jit(solution)/shard_map/all_to_all | solution.py:355
  83.6 0.8 copy-start.6
  84.4 1.1 copy-start.3
  85.4 1.0 copy-start.7
  86.5 14.5 %copy-start.5 = (f32[4,256,128]{2,1,0:T(8,128)S(1)}, f32[4,256,128]{2,1,0:T(8,128)}, u32[]{:S(2)}) copy-start(f32[4,256,128]{2,1,0:T(8,128)} %copy-done.4) | copy-start | bytes 1572868
  101.0 11.2 %copy-start.10 = (f32[4,256]{1,0:T(4,128)S(1)}, f32[4,256]{1,0:T(4,128)}, u32[]{:S(2)}) copy-start(f32[4,256]{1,0:T(4,128)} %gain_ref.1) | copy-start | bytes 12292
  102.1 10.1 %all-to-all-start.5 = ((f32[8,8,256]{2,1,0:T(8,128)}), f32[8,8,256]{2,1,0:T(8,128)S(1)}, u32[]{:S(2)}, u32[]{:S(2)}) async-start(f32[8,8,256]{2,1,0:T(8,128)} %bitcast.10), calls=%async_computation.5 | async-start | bytes 131072 | tf_op jit(solution)/shard_map/all_to_all | solution.py:363

commit v8 on v7

--- a/solution.py
+++ b/solution.py
@@ -344,8 +344,9 @@
     first = lax.ppermute(group_offset, "zh", [(0, 1)])
     third = lax.ppermute(group_total, "zh", [(2, 3)])
     pair = call(step_state, shape_of(PART, KD), inputs=2)(group_total, first)
+    two = lax.ppermute(pair, "zh", [(1, 3)])
+    third, pair = lax.optimization_barrier((third, pair))
     one = lax.ppermute(pair, "zh", [(1, 2)])
-    two = lax.ppermute(pair, "zh", [(1, 3)])
     place = lax.axis_index("zh").astype(jnp.int32).reshape(1)
     planes = call(group_states, shape_of(4, PART, KD), scalars=1, inputs=5)(
         place, first, one, two, third, group_prefix

time: 116 us -> 116 us (level)
  the two profiles are of different devices: /device:TPU:480 before, /device:TPU:1 now
where the time goes in v8:
time: 116 us; the launch traced here: 115 us
  starting transfers between devices  43 us (37%)
  blocking collectives  21.7 us (19%)
  Pallas kernels  18.4 us (16%)
  waiting for transfers between devices  16.7 us (14%)
  local copies, waits for them, and re-layouts  12.8 us (11%)
  between operations  2.24 us (2%)
    unnamed x41, local copies, waits for them, and re-layouts  12.7 us
    all_to_all x1, blocking collectives, shards(): exchanged = lax.all_to_all(maps, 'x', 0, 0, tiled=True)  10.9 us
    all_to_all x1, blocking collectives, shards(): states = lax.all_to_all(returned, 'x', 0, 0, tiled=True)  10.7 us
    all_to_all x1, starting transfers between devices, shards(): squares = lax.all_to_all(squares, 'head', 0, 0, tiled=True)  9.78 us
    ppermute x1, starting transfers between devices, shards(): first = lax.ppermute(group_offset, 'zh', [(0, 1)])  8.82 us
    all_to_all x1, starting transfers between devices, shards(): gathered = lax.all_to_all(plane_total, 'zl', 0, 0, tiled=True)  7.79 us
    pallas_call x1, Pallas kernels, shards(): call(block_terms, (shape_of(HEADS, KD, 2 * KD + VD, kind=bf16), shape_of(...  6.72 us
    all_to_all x1, waiting for transfers between devices, shards(): gathered = lax.all_to_all(plane_total, 'zl', 0, 0, tiled=True)  6.34 us
  transfers between devices with their start and end apart: 9, of which 5 were waited for; matrix products, arithmetic and copies ran while one was open for 1% of the time, Pallas kernels for 12%

profile of v8, /device:TPU:1, one launch (start us, length us, event | category | flops | bytes accessed | tf_op | source)
XLA Modules:
  0.0 114.8 jit_solution(16063222414963937736)
XLA Ops:
  1.3 1.0 copy.31
  2.3 0.0 copy-start.16
  2.3 0.0 copy-start.17
  2.4 0.0 copy-start.13
  2.4 1.2 %copy.28 = bf16[256,4,256]{2,0,1:T(8,128)(2,1)S(1)} copy(bf16[256,4,256]{2,1,0:T(4,128)(2,1)} %param.21) | data formatting | bytes 1048576 | tf_op args[9]
  3.6 0.0 copy-start.11
  3.6 0.7 copy-done.11
  4.2 0.1 shard_map.132.keys_ref
  4.3 4.4 %collective-permute-start = (bf16[4,272,384]{2,1,0:T(8,128)(2,1)S(1)}, bf16[4,272,384]{2,1,0:T(8,128)(2,1)S(1)}, u32[]{:S(2)}, u32[]{:S(2)}) collective-permute-start(bf16[4,272,384]{2,1,0:T(8,128)(2,1)S(1)} %shard_map.132.keys_ref), channel_id=1, source_target_pairs={{0,32},{32,64},{64,96},{96,128},{128,160},{160,192},{192,224},{224... | collective-permute-start | bytes 2506760 | tf_op jit(solution)/shard_map/ppermute | solution.py:307
  9.4 0.1 copy.29
  9.5 0.1 copy_bitcast_fusion.4
  9.6 6.7 %shard_map.131 = (bf16[4,128,512]{2,1,0:T(8,128)(2,1)S(1)}, f32[4,256,128]{2,1,0:T(8,128)S(1)}, f32[4,256,256]{2,1,0:T(8,128)S(1)}) custom-call(s32[1]{0:T(128)S(6)} %copy.32.count_ref, bf16[4,256,128]{2,1,0:T(8,128)(2,1)S(1)} %get-tuple-element.43.q_ref, bf16[4,256,128]{2,1,0:T(8,128)(2,1)S(1)} %get-tuple-element.42.k_ref, ...), custom_call_target="tpu_custom_call" | custom-call | flops 8000000000 | bytes 1000000 | tf_op jit(solution)/shard_map/pallas_call | solution.py:308
  16.3 0.0 copy-start.4
  16.4 10.9 %all_to_all.36.maps_ref = bf16[4,128,512]{2,1,0:T(8,128)(2,1)S(1)} all-to-all(bf16[4,128,512]{2,1,0:T(8,128)(2,1)S(1)} %get-tuple-element.24), channel_id=1, replica_groups=mesh['zh'=4,'zl'=4,'x'=4,'head'=8] {'x'}, dimensions={0} | all-to-all | bytes 1048576 | tf_op jit(solution)/shard_map/all_to_all | solution.py:329
  27.3 0.9 copy-done
  28.2 1.6 %shard_map.133 = (f32[3,128,384]{2,1,0:T(8,128)S(1)}, f32[4,192,128]{2,1,0:T(8,128)}) custom-call(bf16[4,128,512]{2,1,0:T(8,128)(2,1)S(1)} %all_to_all.36.maps_ref), custom_call_target="tpu_custom_call" | custom-call | flops 10000000 | bytes 1000000 | tf_op jit(solution)/shard_map/pallas_call | solution.py:334
  29.8 0.8 copy-done.2
  30.6 7.8 %all-to-all-start.1 = ((f32[4,192,128]{2,1,0:T(8,128)}), f32[4,192,128]{2,1,0:T(8,128)S(1)}, u32[]{:S(2)}, u32[]{:S(2)}) async-start(f32[4,192,128]{2,1,0:T(8,128)} %get-tuple-element.26), calls=%async_computation.1 | async-start | bytes 786432 | tf_op jit(solution)/shard_map/all_to_all | solution.py:337
  38.4 1.1 copy-done.1
  39.6 1.5 %shard_map.137 = bf16[4,272,896]{2,1,0:T(8,128)(2,1)} custom-call(bf16[4,256,128]{2,1,0:T(8,128)(2,1)S(1)} %bitcast.28, bf16[4,272,384]{2,1,0:T(8,128)(2,1)S(1)} %shard_map.132.keys_ref, bf16[4,272,384]{2,1,0:T(8,128)(2,1)S(1)} %copy-done.1), custom_call_target="tpu_custom_call" | custom-call | flops 10000000 | bytes 1000000 | tf_op jit(solution)/shard_map/pallas_call | solution.py:331
  41.1 6.3 %all-to-all-done.1.maps_ref = f32[4,192,128]{2,1,0:T(8,128)S(1)} async-done(((f32[4,192,128]{2,1,0:T(8,128)}), f32[4,192,128]{2,1,0:T(8,128)S(1)}, u32[]{:S(2)}, u32[]{:S(2)}) %all-to-all-start.1) | async-done | bytes 393248 | tf_op jit(solution)/shard_map/all_to_all | solution.py:337
  47.4 0.8 shard_map.134
  48.2 0.0 copy-start.8
  48.2 0.6 copy-done.8
  48.8 3.6 %all-to-all-start.2 = ((bf16[4,272,896]{2,1,0:T(8,128)(2,1)}), bf16[4,272,896]{2,1,0:T(8,128)(2,1)S(1)}, u32[]{:S(2)}, u32[]{:S(2)}) async-start(bf16[4,272,896]{2,1,0:T(8,128)(2,1)} %shard_map.137), calls=%async_computation.2 | async-start | bytes 3899392 | tf_op jit(solution)/shard_map/all_to_all | solution.py:343
  52.4 0.7 collective-permute-start.2
  53.1 8.8 %collective-permute-start.1 = (f32[64,128]{1,0:T(8,128)S(1)}, f32[64,128]{1,0:T(8,128)S(1)}, u32[]{:S(2)}, u32[]{:S(2)}) collective-permute-start(f32[64,128]{1,0:T(8,128)S(1)} %get-tuple-element.27), channel_id=1, source_target_pairs={{0,128},{1,129},{2,130},{3,131},{4,132},{5,133},{6,134},{7,135},{8... | collective-permute-start | bytes 98312 | tf_op jit(solution)/shard_map/ppermute | solution.py:344
  61.9 1.0 collective-permute-done.1.earlier_ref.first_ref
  62.9 0.9 copy-done.9
  63.8 0.9 shard_map.135
  64.7 0.7 collective-permute-start.4
  65.4 1.3 %collective-permute-start.3 = (f32[64,128]{1,0:T(8,128)}, f32[64,128]{1,0:T(8,128)}, u32[]{:S(2)}, u32[]{:S(2)}) collective-permute-start(f32[64,128]{1,0:T(8,128)} %shard_map.135), channel_id=1, source_target_pairs={{128,256},{129,257},{130,258},{131,259},{132,260},{133,261},{134,2... | collective-permute-start | bytes 98312 | tf_op jit(solution)/shard_map/ppermute | solution.py:349
  66.7 2.1 %shard_map.136 = f32[4,64,128]{2,1,0:T(8,128)} custom-call(s32[1]{0:T(128)} %bitcast.5.place_ref, f32[64,128]{1,0:T(8,128)S(1)} %collective-permute-done.1.earlier_ref.first_ref, f32[64,128]{1,0:T(8,128)} %collective-permute-done.3.one_ref, f32[64,128]{1,0:T(8,128)S(1)} %collective-permute-done.4.two_ref, f32[192,128]{1,0:T(8,128)S(1)} %collective-permute-done.2.third_ref, ...), custom_call_target="tpu_custom_call" | custom-call | flops 10000000 | bytes 1000000 | tf_op jit(solution)/shard_map/pallas_call | solution.py:351
  68.8 4.8 %all-to-all-done.2.blocks_ref = bf16[4,272,896]{2,1,0:T(8,128)(2,1)S(1)} async-done(((bf16[4,272,896]{2,1,0:T(8,128)(2,1)}), bf16[4,272,896]{2,1,0:T(8,128)(2,1)S(1)}, u32[]{:S(2)}, u32[]{:S(2)}) %all-to-all-start.2) | async-done | bytes 1949728 | tf_op jit(solution)/shard_map/all_to_all | solution.py:343
  73.6 6.0 %all-to-all-start.3 = ((f32[4,64,128]{2,1,0:T(8,128)}), f32[4,64,128]{2,1,0:T(8,128)S(1)}, u32[]{:S(2)}, u32[]{:S(2)}) async-start(f32[4,64,128]{2,1,0:T(8,128)} %shard_map.136), calls=%async_computation.3 | async-start | bytes 262144 | tf_op jit(solution)/shard_map/all_to_all | solution.py:356
  79.6 3.0 %shard_map.138.attn_ref = bf16[4,256,256]{2,1,0:T(8,128)(2,1)S(1)} custom-call(bf16[4,272,896]{2,1,0:T(8,128)(2,1)S(1)} %all-to-all-done.2.blocks_ref), custom_call_target="tpu_custom_call" | custom-call | flops 8000000000 | bytes 1000000 | tf_op jit(solution)/shard_map/pallas_call | solution.py:355
  82.6 0.8 copy-done.6
  83.4 1.0 all-to-all-done.3.parts_ref
  84.3 1.1 copy-done.3
  85.4 1.0 copy-done.7
  86.4 0.4 shard_map.139
  86.9 10.7 %all_to_all.37.state_ref = bf16[4,384,256]{2,1,0:T(8,128)(2,1)S(1)} all-to-all(bf16[4,384,256]{2,1,0:T(8,128)(2,1)S(1)} %shard_map.139), channel_id=1, replica_groups=mesh['zh'=4,'zl'=4,'x'=4,'head'=8] {'x'}, dimensions={0} | all-to-all | bytes 1572864 | tf_op jit(solution)/shard_map/all_to_all | solution.py:360
  97.7 1.1 shard_map.140
  98.8 9.8 %all-to-all-start.5 = ((f32[8,8,256]{2,1,0:T(8,128)}), f32[8,8,256]{2,1,0:T(8,128)S(1)}, u32[]{:S(2)}, u32[]{:S(2)}) async-start(f32[8,8,256]{2,1,0:T(8,128)} %bitcast.10), calls=%async_computation.5 | async-start | bytes 131072 | tf_op jit(solution)/shard_map/all_to_all | solution.py:364
  108.6 1.2 %copy.21 = bf16[256,4,256]{2,1,0:T(4,128)(2,1)} copy(bf16[256,4,256]{2,0,1:T(8,128)(2,1)S(1)} %slice_bitcast_fusion) | data formatting | bytes 1048576
  109.8 3.6 %all-to-all-done.5 = f32[8,8,256]{2,1,0:T(8,128)S(1)} async-done(((f32[8,8,256]{2,1,0:T(8,128)}), f32[8,8,256]{2,1,0:T(8,128)S(1)}, u32[]{:S(2)}, u32[]{:S(2)}) %all-to-all-start.5) | async-done | bytes 65568 | tf_op jit(solution)/shard_map/all_to_all | solution.py:364
  113.4 0.2 shard_map.141
  113.6 1.2 %copy.20 = bf16[256,4,256]{2,1,0:T(4,128)(2,1)} copy(bf16[256,4,256]{2,0,1:T(8,128)(2,1)S(1)} %bitcast.25) | data formatting | bytes 1048576
  (27 shorter events, 0.1 us)
Async XLA Ops:
  0.6 8.8 %copy-start.14 = (bf16[256,4,256]{2,1,0:T(4,128)(2,1)S(1)}, bf16[256,4,256]{2,1,0:T(4,128)(2,1)}, u32[]{:S(2)}) copy-start(bf16[256,4,256]{2,1,0:T(4,128)(2,1)} %param.14) | copy-start | bytes 1572868
  2.3 7.2 %copy-start.16 = (bf16[256,4,128]{2,1,0:T(4,128)(2,1)S(1)}, bf16[256,4,128]{2,1,0:T(4,128)(2,1)}, u32[]{:S(2)}) copy-start(bf16[256,4,128]{2,1,0:T(4,128)(2,1)} %param.13) | copy-start | bytes 786436
  2.3 7.2 %copy-start.17 = (bf16[256,4,128]{2,1,0:T(4,128)(2,1)S(1)}, bf16[256,4,128]{2,1,0:T(4,128)(2,1)}, u32[]{:S(2)}) copy-start(bf16[256,4,128]{2,1,0:T(4,128)(2,1)} %param.12) | copy-start | bytes 786436
  2.4 7.2 %copy-start.13 = (f32[256,4]{0,1:T(4,128)S(1)}, f32[256,4]{0,1:T(4,128)}, u32[]{:S(2)}) copy-start(f32[256,4]{0,1:T(4,128)} %param.16) | copy-start | bytes 12292
  3.5 6.1 %copy-start.12 = (f32[256,4]{0,1:T(4,128)S(1)}, f32[256,4]{0,1:T(4,128)}, u32[]{:S(2)}) copy-start(f32[256,4]{0,1:T(4,128)} %param.15) | copy-start | bytes 12292
  3.6 0.7 copy-start.11
  4.3 23.0 %collective-permute-start = (bf16[4,272,384]{2,1,0:T(8,128)(2,1)S(1)}, bf16[4,272,384]{2,1,0:T(8,128)(2,1)S(1)}, u32[]{:S(2)}, u32[]{:S(2)}) collective-permute-start(bf16[4,272,384]{2,1,0:T(8,128)(2,1)S(1)} %shard_map.132.keys_ref), channel_id=1, source_target_pairs={{0,32},{32,64},{64,96},{96,128},{128,160},{160,192},{192,224},{224... | collective-permute-start | bytes 2506760 | tf_op jit(solution)/shard_map/ppermute | solution.py:307
  16.3 13.4 %copy-start.4 = (f32[4,256,128]{2,1,0:T(8,128)}, f32[4,256,128]{2,1,0:T(8,128)S(1)}, u32[]{:S(2)}) copy-start(f32[4,256,128]{2,1,0:T(8,128)S(1)} %get-tuple-element.21.carry_ref) | copy-start | bytes 1572868
  16.4 22.0 %copy-start.15 = (bf16[256,4,128]{2,1,0:T(4,128)(2,1)S(1)}, bf16[256,4,128]{2,1,0:T(4,128)(2,1)}, u32[]{:S(2)}) copy-start(bf16[256,4,128]{2,1,0:T(4,128)(2,1)} %param.19) | copy-start | bytes 786436
  27.3 0.9 copy-start
  29.8 0.8 copy-start.2
  30.6 16.8 %all-to-all-start.1 = ((f32[4,192,128]{2,1,0:T(8,128)}), f32[4,192,128]{2,1,0:T(8,128)S(1)}, u32[]{:S(2)}, u32[]{:S(2)}) async-start(f32[4,192,128]{2,1,0:T(8,128)} %get-tuple-element.26), calls=%async_computation.1 | async-start | bytes 786432 | tf_op jit(solution)/shard_map/all_to_all | solution.py:337
  38.4 1.2 %copy-start.1 = (bf16[4,272,384]{2,1,0:T(8,128)(2,1)S(1)}, bf16[4,272,384]{2,1,0:T(8,128)(2,1)}, u32[]{:S(2)}) copy-start(bf16[4,272,384]{2,1,0:T(8,128)(2,1)} %copy-done) | copy-start | bytes 2506756
  48.2 0.6 copy-start.8
  48.8 24.7 %all-to-all-start.2 = ((bf16[4,272,896]{2,1,0:T(8,128)(2,1)}), bf16[4,272,896]{2,1,0:T(8,128)(2,1)S(1)}, u32[]{:S(2)}, u32[]{:S(2)}) async-start(bf16[4,272,896]{2,1,0:T(8,128)(2,1)} %shard_map.137), calls=%async_computation.2 | async-start | bytes 3899392 | tf_op jit(solution)/shard_map/all_to_all | solution.py:343
  52.4 13.0 %collective-permute-start.2 = (f32[192,128]{1,0:T(8,128)}, f32[192,128]{1,0:T(8,128)S(1)}, u32[]{:S(2)}, u32[]{:S(2)}) collective-permute-start(f32[192,128]{1,0:T(8,128)} %copy-done.8), channel_id=1, source_target_pairs={{256,384},{257,385},{258,386},{259,387},{260,388},{261,389},{262,3... | collective-permute-start | bytes 294920 | tf_op jit(solution)/shard_map/ppermute | solution.py:345
  53.1 9.8 %collective-permute-start.1 = (f32[64,128]{1,0:T(8,128)S(1)}, f32[64,128]{1,0:T(8,128)S(1)}, u32[]{:S(2)}, u32[]{:S(2)}) collective-permute-start(f32[64,128]{1,0:T(8,128)S(1)} %get-tuple-element.27), channel_id=1, source_target_pairs={{0,128},{1,129},{2,130},{3,131},{4,132},{5,133},{6,134},{7,135},{8... | collective-permute-start | bytes 98312 | tf_op jit(solution)/shard_map/ppermute | solution.py:344
  62.9 0.9 copy-start.9
  64.7 1.9 %collective-permute-start.4 = (f32[64,128]{1,0:T(8,128)}, f32[64,128]{1,0:T(8,128)S(1)}, u32[]{:S(2)}, u32[]{:S(2)}) collective-permute-start(f32[64,128]{1,0:T(8,128)} %shard_map.135), channel_id=1, source_target_pairs={{128,384},{129,385},{130,386},{131,387},{132,388},{133,389},{134,3... | collective-permute-start | bytes 98312 | tf_op jit(solution)/shard_map/ppermute | solution.py:347
  65.4 1.3 %collective-permute-start.3 = (f32[64,128]{1,0:T(8,128)}, f32[64,128]{1,0:T(8,128)}, u32[]{:S(2)}, u32[]{:S(2)}) collective-permute-start(f32[64,128]{1,0:T(8,128)} %shard_map.135), channel_id=1, source_target_pairs={{128,256},{129,257},{130,258},{131,259},{132,260},{133,261},{134,2... | collective-permute-start | bytes 98312 | tf_op jit(solution)/shard_map/ppermute | solution.py:349
  73.6 10.8 %all-to-all-start.3 = ((f32[4,64,128]{2,1,0:T(8,128)}), f32[4,64,128]{2,1,0:T(8,128)S(1)}, u32[]{:S(2)}, u32[]{:S(2)}) async-start(f32[4,64,128]{2,1,0:T(8,128)} %shard_map.136), calls=%async_computation.3 | async-start | bytes 262144 | tf_op jit(solution)/shard_map/all_to_all | solution.py:356
  82.6 0.8 copy-start.6
  84.3 1.1 copy-start.3
  85.4 1.0 copy-start.7
  86.4 11.2 %copy-start.5 = (f32[4,256,128]{2,1,0:T(8,128)S(1)}, f32[4,256,128]{2,1,0:T(8,128)}, u32[]{:S(2)}) copy-start(f32[4,256,128]{2,1,0:T(8,128)} %copy-done.4) | copy-start | bytes 1572868
  97.6 15.8 %copy-start.10 = (f32[4,256]{1,0:T(4,128)S(1)}, f32[4,256]{1,0:T(4,128)}, u32[]{:S(2)}) copy-start(f32[4,256]{1,0:T(4,128)} %gain_ref.1) | copy-start | bytes 12292
  98.8 14.6 %all-to-all-start.5 = ((f32[8,8,256]{2,1,0:T(8,128)}), f32[8,8,256]{2,1,0:T(8,128)S(1)}, u32[]{:S(2)}, u32[]{:S(2)}) async-start(f32[8,8,256]{2,1,0:T(8,128)} %bitcast.10), calls=%async_computation.5 | async-start | bytes 131072 | tf_op jit(solution)/shard_map/all_to_all | solution.py:364
